TPU v7x, 32 devices: a whole 2x2x4 slice. The times are simulated.
32 devices in a mesh: tm: 8 (over y, x, core), freq: 4 (over z).
Axes of the slice: x: 2, y: 2, z: 4, core: 2. Of those that a mesh axis runs over, the one named last changes fastest.
Arguments:
- visibility: bfloat16 [2, 16, 512, 2048], P(None, None, 'freq', 'tm'), may hold values from -6 to 6
- spectrum_power_sum: float32 [512, 2048], P('freq', 'tm'), may hold values from 50 to 500, as said below
- square_sum: float32 [512, 2048], P('freq', 'tm'), as said below
- accum_count: int32 [512, 2048], P('freq', 'tm'), may hold values from 64 to 256
- rfi_mask: int32 [512, 2048], P('freq', 'tm'), may hold values 0 or 1
- baseline_delay_class: int32 [16, 1], P('freq'), may hold values from 0 to 3
- filter_bank: bfloat16 [4, 512, 512], replicated, may hold values from -0.25 to 0.25
Outputs:
- filtered: bfloat16 [2, 16, 512, 2048], P(None, 'freq', None, 'tm')
Inputs may be any that keep to these rules, and one draw needn't show every extreme that they name: `spectrum_power_sum`: positive in every sample. `square_sum`: positive in every sample.
All inputs are finite; a program needn't handle non-finite values. No bound on the sum of `rfi_mask` on one device may be relied on, other than what follows from the above.
Results may differ from a plain program's by a relative error of at most 0.0043.
The roundings to bfloat16 on the way count: a program that leaves them out, or rounds other values in their place, can miss the bound.
Values may be sent and summed in bfloat16 or wider, within the bound.
No kernel may reach another device: no remote copies, remote signals or barrier semaphores. Data moves between devices by JAX's collectives and lax.ppermute only.
A program may use at most 128 MiB of HBM per device.

v0:
```python
import math

import jax
import jax.numpy as jnp
from jax import lax
from jax.sharding import PartitionSpec as P

RIM = 16


def padded_2(value, sides, width):
    for axis, dim in sides:
        devices, length = (lax.axis_size(axis), value.shape[dim])
        up = [(i, (i + 1) % devices) for i in range(devices)]
        down = [(j, i) for i, j in up]
        last = lax.slice_in_dim(value, length - width, length, axis=dim)
        leading = lax.slice_in_dim(value, 0, width, axis=dim)
        before = lax.ppermute(last, axis, up)
        after = lax.ppermute(leading, axis, down)
        value = jnp.concatenate([before, value, after], axis=dim)
    return value


def rotation_table(rows_n, cols_n, period):
    row_index = jnp.arange(rows_n, dtype=jnp.int32)
    col_index = jnp.arange(cols_n, dtype=jnp.int32)
    phase = row_index[:, None] * col_index[None, :] % period
    angles = 2.0 * math.pi / period * phase.astype(jnp.float32)
    cosine = jnp.cos(angles)
    sine = jnp.sin(angles)
    real_row = jnp.stack([cosine, sine])
    imag_row = jnp.stack([-sine, cosine])
    return jnp.stack([real_row, imag_row])


def twist_table(rows_n, cols_n, period):
    row_index = jnp.arange(rows_n, dtype=jnp.int32)
    col_index = jnp.arange(cols_n, dtype=jnp.int32)
    phase = row_index[:, None] * col_index[None, :] % period
    angles = 2.0 * math.pi / period * phase.astype(jnp.float32)
    return (jnp.cos(angles), jnp.sin(angles))


def sidereal_transform(received):
    periods = lax.axis_size("tm")
    samples = received.shape[3]
    inner_len = samples // periods
    base_n = received.shape[1]
    chan_n = received.shape[2]
    widened = received.astype(jnp.float32).reshape(2, base_n, chan_n, periods, inner_len)
    better = lax.Precision.HIGH
    first_table = rotation_table(periods, periods, periods)
    stepped = jnp.einsum("cbfps,dcjp->dbfjs", widened, first_table, precision=better)
    cos_two, sin_two = twist_table(periods, inner_len, samples)
    twist_real = stepped[0] * cos_two + stepped[1] * sin_two
    twist_imag = stepped[1] * cos_two - stepped[0] * sin_two
    twisted = jnp.stack([twist_real, twist_imag])
    tertiary_lookup = rotation_table(inner_len, inner_len, inner_len)
    finished = jnp.einsum("cbfjs,dcks->dbfkj", twisted, tertiary_lookup, precision=better)
    norm_scale = 1.0 / math.sqrt(samples)
    finished = finished.reshape(2, base_n, chan_n, samples) * norm_scale
    return finished.astype(jnp.bfloat16)


def shards(
    visibility,
    spectrum_power_sum,
    square_sum,
    accum_count,
    rfi_mask,
    baseline_delay_class,
    filter_bank,
):
    counts = accum_count.astype(jnp.float32)
    kurtosis = (
        (counts + 1.0)
        / (counts - 1.0)
        * (counts * square_sum / (spectrum_power_sum * spectrum_power_sum) - 1.0)
    )
    flag_weight = rfi_mask.astype(jnp.float32) * jnp.exp(-2.0 * (kurtosis - 1.0) ** 2)
    local_len = flag_weight.shape[1]
    padded = padded_2(flag_weight, (("tm", 1),), RIM)
    smooth_weight = jnp.zeros(flag_weight.shape, jnp.float32)
    for offset in range(2 * RIM + 1):
        factor = (RIM + 1 - abs(offset - RIM)) / float((RIM + 1) ** 2)
        smooth_weight = smooth_weight + factor * padded[:, offset : offset + local_len]
    weighted = (visibility.astype(jnp.float32) * smooth_weight[None, None]).astype(jnp.bfloat16)
    spectrum = sidereal_transform(
        lax.all_to_all(weighted, "tm", split_axis=2, concat_axis=3, tiled=True)
    )
    chosen = jnp.take(filter_bank, baseline_delay_class[:, 0], axis=0)
    moved = lax.all_to_all(spectrum, "tm", split_axis=3, concat_axis=2, tiled=True)
    return jnp.einsum(
        "bgf,cbfm->cbgm",
        chosen,
        lax.all_to_all(moved, "freq", split_axis=1, concat_axis=2, tiled=True),
        preferred_element_type=jnp.float32,
    ).astype(jnp.bfloat16)


def solution(mesh):
    in_specs = (
        P(None, None, "freq", "tm"),
        P("freq", "tm"),
        P("freq", "tm"),
        P("freq", "tm"),
        P("freq", "tm"),
        P("freq", None),
        P(),
    )
    out_specs = P(None, "freq", None, "tm")
    return jax.shard_map(shards, mesh=mesh, in_specs=in_specs, out_specs=out_specs, check_vma=False)
```

profile of v0, /device:TPU:0, one launch (start us, length us, event | category | flops | bytes accessed | tf_op | source)
XLA Modules:
  0.0 230.2 jit_solution(7954124111669577495)
XLA Ops:
  0.0 1.3 exponential_multiply_fusion
  1.3 0.1 fusion.144
  1.4 0.5 collective-permute-start
  1.9 2.9 %collective-permute-start.1 = (f32[128,16]{1,0:T(8,128)S(1)}, f32[128,16]{1,0:T(8,128)S(1)}, u32[]{:S(2)}, u32[]{:S(2)}) collective-permute-start(f32[128,16]{1,0:T(8,128)S(1)} %get-tuple-element.10), channel_id=1, source_target_pairs={{4,0},{8,4},{12,8},{16,12},{20,16},{24,20},{28,24},{0,28},{5,1},{9... | collective-permute-start | bytes 24584 | tf_op jit(solution)/shard_map/ppermute | solution.py:19
  4.8 1.9 collective-permute-done
  6.7 0.0 collective-permute-done.1
  6.7 1.7 fusion.27
  8.4 4.4 %multiply_convert_fusion = bf16[2,16,128,256]{3,1,0,2:T(8,128)(2,1)} fusion(bf16[2,16,128,256]{3,2,1,0:T(8,128)(2,1)} %param.7, f32[128,256]{1,0:T(8,128)S(1)} %fusion.27), kind=kLoop, calls=%fused_computation.7 | loop fusion | flops 3145728 | bytes 4325376 | tf_op jit(solution)/shard_map/convert_element_type | solution.py:87
  12.8 4.7 %all-to-all-start = ((bf16[2,16,128,256]{3,1,0,2:T(8,128)(2,1)}), bf16[2,16,128,256]{3,1,0,2:T(8,128)(2,1)}, u32[]{:S(2)}, u32[]{:S(2)}) async-start(bf16[2,16,128,256]{3,1,0,2:T(8,128)(2,1)} %multiply_convert_fusion), calls=%async_computation | async-start | bytes 4194304 | tf_op jit(solution)/shard_map/all_to_all | solution.py:89
  17.5 0.1 fusion.139
  17.6 0.1 fusion.137
  17.6 0.1 fusion.132
  17.7 1.0 fusion.120
  18.7 1.0 fusion.118
  19.7 0.1 maximum_bitcast_fusion.2
  19.8 24.4 %all-to-all-done = bf16[2,16,128,256]{3,1,0,2:T(8,128)(2,1)} async-done(((bf16[2,16,128,256]{3,1,0,2:T(8,128)(2,1)}), bf16[2,16,128,256]{3,1,0,2:T(8,128)(2,1)}, u32[]{:S(2)}, u32[]{:S(2)}) %all-to-all-start) | async-done | bytes 2097184 | tf_op jit(solution)/shard_map/all_to_all | solution.py:89
  44.3 4.7 %convolution_bitcast_fusion = f32[2,16,16,8,256]{4,3,2,1,0:T(8,128)S(1)} fusion(bf16[2,16,8,16,256]{4,1,0,3,2:T(8,128)(2,1)} %bitcast.8, f32[1,2,8,8]{3,2,1,0:T(8,128)S(1)} %get-tuple-element.12, f32[1,2,8,8]{3,2,1,0:T(8,128)S(1)} %get-tuple-element.11), kind=kOutput, calls=%fused_computation.8 | convolution fusion | flops 100663552 | bytes 6292480 | tf_op jit(solution)/shard_map/cbfps,dcjp->dbfjs/dot_general | solution.py:53
  48.9 0.7 multiply_add_fusion
  49.6 0.4 pad_maximum_fusion
  50.1 4.8 %fusion.4 = bf16[2,16,16,256,8]{3,2,4,1,0:T(8,128)(2,1)} fusion(f32[2,16,16,8,256]{4,3,2,1,0:T(8,128)S(1)} %pad_maximum_fusion, f32[1,2,256,256]{3,2,1,0:T(8,128)S(1)} %get-tuple-element.8, f32[1,2,256,256]{3,2,1,0:T(8,128)S(1)} %get-tuple-element.7), kind=kOutput, calls=%fused_computation.9 | convolution fusion | flops 3223584768 | bytes 7340032 | tf_op jit(solution)/shard_map/cbfjs,dcks->dbfkj/dot_general | solution.py:59
  54.9 23.5 %copy.45 = bf16[2,16,16,256,8]{2,1,0,4,3:T(8,128)(2,1)} copy(bf16[2,16,16,256,8]{3,2,4,1,0:T(8,128)(2,1)} %fusion.4) | data formatting | bytes 4194304 | tf_op jit(solution)/shard_map/convert_element_type | solution.py:62
  78.3 19.6 %reshape.218 = bf16[8,2,65536]{2,1,0:T(2,128)(2,1)} reshape(bf16[2048,2,16,16]{3,2,1,0:T(8,128)(2,1)} %bitcast.72) | data formatting | bytes 4194304
  97.9 30.9 %all_to_all.51 = bf16[8,2,65536]{2,1,0:T(2,128)(2,1)} all-to-all(bf16[8,2,65536]{2,1,0:T(2,128)(2,1)} %reshape.218), channel_id=1, replica_groups=mesh['tm'=8,'freq'=4] {'tm'}, dimensions={0} | all-to-all | bytes 4194304 | tf_op jit(solution)/shard_map/all_to_all | solution.py:92
  128.8 13.9 %reshape.219 = bf16[2048,2,16,16]{3,2,1,0:T(8,128)(2,1)} reshape(bf16[8,2,65536]{2,1,0:T(2,128)(2,1)} %all_to_all.51) | data formatting | bytes 4194304
  142.7 17.0 %copy.48 = bf16[2,16,8,16,256]{4,3,2,0,1:T(8,128)(2,1)} copy(bf16[2,16,8,16,256]{3,1,0,4,2:T(8,128)(2,1)} %bitcast.73) | data formatting | bytes 4194304 | tf_op jit(solution)/shard_map/all_to_all | solution.py:92
  159.8 5.4 %all-to-all-start.2 = ((bf16[2,16,128,256]{3,2,0,1:T(8,128)(2,1)}), bf16[2,16,128,256]{3,2,0,1:T(8,128)(2,1)}, u32[]{:S(2)}, u32[]{:S(2)}) async-start(bf16[2,16,128,256]{3,2,0,1:T(8,128)(2,1)} %bitcast.74), calls=%async_computation.2 | async-start | bytes 4194304 | tf_op jit(solution)/shard_map/all_to_all | solution.py:96
  165.2 2.0 gather_fusion
  167.3 45.6 %all-to-all-done.2 = bf16[2,16,128,256]{3,2,0,1:T(8,128)(2,1)} async-done(((bf16[2,16,128,256]{3,2,0,1:T(8,128)(2,1)}), bf16[2,16,128,256]{3,2,0,1:T(8,128)(2,1)}, u32[]{:S(2)}, u32[]{:S(2)}) %all-to-all-start.2) | async-done | bytes 2097184 | tf_op jit(solution)/shard_map/all_to_all | solution.py:96
  212.9 4.2 %copy.36 = bf16[2,4,4,128,256]{3,2,4,0,1:T(4,128)(2,1)} copy(bf16[2,4,4,128,256]{4,3,0,1,2:T(8,128)(2,1)} %bitcast.28) | data formatting | bytes 4194304 | tf_op jit(solution)/shard_map/all_to_all | solution.py:96
  217.1 4.1 %all_to_all.47 = bf16[2,4,512,256]{2,3,0,1:T(8,128)(2,1)} reshape(bf16[2,4,4,128,256]{3,2,4,0,1:T(4,128)(2,1)} %copy.36) | data formatting | bytes 4194304 | tf_op jit(solution)/shard_map/all_to_all | solution.py:96
  221.2 4.9 %convert_bitcast_fusion = bf16[2,4,512,256]{2,3,0,1:T(8,128)(2,1)} fusion(bf16[2,4,512,256]{2,3,0,1:T(8,128)(2,1)} %all_to_all.47, bf16[4,512,512]{2,1,0:T(8,128)(2,1)} %gather_fusion, pred[4]{0:T(512)(128)(4,1)S(1)} %and_bitcast_fusion), kind=kOutput, calls=%fused_computation.14 | convolution fusion | flops 1075838976 | bytes 6291460 | tf_op jit(solution)/shard_map/bgf,cbfm->cbgm/dot_general | solution.py:93
  226.1 4.1 %copy.37 = bf16[2,4,512,256]{3,2,1,0:T(8,128)(2,1)} copy(bf16[2,4,512,256]{2,3,0,1:T(8,128)(2,1)} %convert_bitcast_fusion) | data formatting | bytes 4194304 | tf_op jit(solution)/shard_map/convert_element_type | solution.py:98
  (8 shorter events, 0.0 us)
Async XLA Ops:
  0.0 165.2 %copy-start = (bf16[4,512,512]{2,1,0:T(8,128)(2,1)S(1)}, bf16[4,512,512]{2,1,0:T(8,128)(2,1)}, u32[]{:S(2)}) copy-start(bf16[4,512,512]{2,1,0:T(8,128)(2,1)} %param.13) | copy-start | bytes 6291460
  1.4 5.3 %collective-permute-start = (f32[128,16]{1,0:T(8,128)S(1)}, f32[128,16]{1,0:T(8,128)S(1)}, u32[]{:S(2)}, u32[]{:S(2)}) collective-permute-start(f32[128,16]{1,0:T(8,128)S(1)} %get-tuple-element.9), channel_id=1, source_target_pairs={{0,4},{4,8},{8,12},{12,16},{16,20},{20,24},{24,28},{28,0},{1,5},{5... | collective-permute-start | bytes 24584 | tf_op jit(solution)/shard_map/ppermute | solution.py:18
  1.9 4.9 %collective-permute-start.1 = (f32[128,16]{1,0:T(8,128)S(1)}, f32[128,16]{1,0:T(8,128)S(1)}, u32[]{:S(2)}, u32[]{:S(2)}) collective-permute-start(f32[128,16]{1,0:T(8,128)S(1)} %get-tuple-element.10), channel_id=1, source_target_pairs={{4,0},{8,4},{12,8},{16,12},{20,16},{24,20},{28,24},{0,28},{5,1},{9... | collective-permute-start | bytes 24584 | tf_op jit(solution)/shard_map/ppermute | solution.py:19
  12.8 31.5 %all-to-all-start = ((bf16[2,16,128,256]{3,1,0,2:T(8,128)(2,1)}), bf16[2,16,128,256]{3,1,0,2:T(8,128)(2,1)}, u32[]{:S(2)}, u32[]{:S(2)}) async-start(bf16[2,16,128,256]{3,1,0,2:T(8,128)(2,1)} %multiply_convert_fusion), calls=%async_computation | async-start | bytes 4194304 | tf_op jit(solution)/shard_map/all_to_all | solution.py:89
  159.8 5.5 %copy-start.1 = (s32[4,1]{0,1:T(1,128)S(1)}, s32[4,1]{0,1:T(1,128)}, u32[]{:S(2)}) copy-start(s32[4,1]{0,1:T(1,128)} %param.12) | copy-start | bytes 52
  159.8 53.1 %all-to-all-start.2 = ((bf16[2,16,128,256]{3,2,0,1:T(8,128)(2,1)}), bf16[2,16,128,256]{3,2,0,1:T(8,128)(2,1)}, u32[]{:S(2)}, u32[]{:S(2)}) async-start(bf16[2,16,128,256]{3,2,0,1:T(8,128)(2,1)} %bitcast.74), calls=%async_computation.2 | async-start | bytes 4194304 | tf_op jit(solution)/shard_map/all_to_all | solution.py:96
where the time goes:
time: 231 us; the launch traced here: 230 us
  local copies, waits for them, and re-layouts  88.5 us (38%)
  waiting for transfers between devices  71.9 us (31%)
  blocking collectives  30.9 us (13%)
  matrix products  14.4 us (6%)
  starting transfers between devices  13.6 us (6%)
  other arithmetic  10.8 us (5%)
    all_to_all x1, waiting for transfers between devices, shards(): lax.all_to_all(moved, 'freq', split_axis=1, concat_axis=2, tiled=True)  45.6 us
    unnamed x6, local copies, waits for them, and re-layouts  33.5 us
    all_to_all x1, blocking collectives, shards(): lax.all_to_all(spectrum, 'tm', split_axis=3, concat_axis=2, tiled=True)  30.9 us
    all_to_all x1, waiting for transfers between devices, shards(): lax.all_to_all(weighted, 'tm', split_axis=2, concat_axis=3, tiled=True)  24.4 us
    convert_element_type x1, local copies, waits for them, and re-layouts, sidereal_transform(): return finished.astype(jnp.bfloat16)  23.5 us
    all_to_all x1, local copies, waits for them, and re-layouts, shards(): lax.all_to_all(spectrum, 'tm', split_axis=3, concat_axis=2, tiled=True)  17 us
    all_to_all x2, local copies, waits for them, and re-layouts, shards(): lax.all_to_all(moved, 'freq', split_axis=1, concat_axis=2, tiled=True)  8.31 us
    all_to_all x1, starting transfers between devices, shards(): lax.all_to_all(moved, 'freq', split_axis=1, concat_axis=2, tiled=True)  5.45 us
  transfers between devices with their start and end apart: 4, of which 3 were waited for; matrix products, arithmetic and copies ran while one was open for 2% of the time, Pallas kernels for 0%

commit v1 on v0

v1 whole, which is shorter than its diff:
```python
import functools
import math

import jax
import jax.numpy as jnp
import ml_dtypes
import numpy as np
from jax import lax
from jax.experimental import pallas as pl
from jax.experimental.pallas import tpu as pltpu
from jax.sharding import PartitionSpec as P

RIM = 16
LANES = 128
VMEM_BYTES = 48 * 1024 * 1024

WHOLE = pl.BlockSpec(memory_space=pltpu.VMEM)
SCALARS = pl.BlockSpec(memory_space=pltpu.SMEM)


def row_type(rows):
    return jnp.bfloat16 if rows % 16 == 0 else jnp.float32


def params():
    return pltpu.CompilerParams(vmem_limit_bytes=VMEM_BYTES)


def cost(flops, arrays):
    return pl.CostEstimate(flops=flops, bytes_accessed=sum(a.size * a.dtype.itemsize for a in arrays), transcendentals=0)


def swap(value, axis, k):
    size = lax.axis_size(axis)
    return lax.ppermute(value, axis, [(i, i ^ k) for i in range(size)])


def exchange(blocks, axis):
    order = sorted(range(1, len(blocks)), key=lambda k: (-bin(k >> 1).count("1"), k))
    moved = {0: blocks[0]}
    for k in order:
        moved[k] = swap(blocks[k], axis, k)
    return [moved[k] for k in range(len(blocks))]


def smoothing_weights(spectrum_power_sum, square_sum, accum_count, rfi_mask):
    counts = accum_count.astype(jnp.float32)
    kurtosis = (
        (counts + 1.0)
        / (counts - 1.0)
        * (counts * square_sum / (spectrum_power_sum * spectrum_power_sum) - 1.0)
    )
    flag_weight = rfi_mask.astype(jnp.float32) * jnp.exp(-2.0 * (kurtosis - 1.0) ** 2)
    devices, length = lax.axis_size("tm"), flag_weight.shape[1]
    up = [(i, (i + 1) % devices) for i in range(devices)]
    before = lax.ppermute(flag_weight[:, length - RIM :], "tm", up)
    after = lax.ppermute(flag_weight[:, :RIM], "tm", [(j, i) for i, j in up])
    padded = jnp.concatenate([before, flag_weight, after], axis=1)
    smooth_weight = jnp.zeros(flag_weight.shape, jnp.float32)
    for offset in range(2 * RIM + 1):
        factor = (RIM + 1 - abs(offset - RIM)) / float((RIM + 1) ** 2)
        smooth_weight = smooth_weight + factor * padded[:, offset : offset + length]
    return smooth_weight


def weigh_by_baseline(here, vis, smooth, *outs):
    me = here[1]
    for k, out in enumerate(outs):
        dest = me ^ k
        for c in range(2):
            for b in range(vis.shape[3]):
                out[c, b] = (vis[c, dest, 0, b].astype(jnp.float32) * smooth[...]).astype(jnp.bfloat16)


def weigh_by_channel(here, vis, smooth, *outs):
    me = here[0]
    fs = vis.shape[4] // len(outs)
    for k, out in enumerate(outs):
        rows = pl.ds(pl.multiple_of((me ^ k) * fs, fs), fs)
        part = smooth[rows, :]
        for c in range(2):
            for z in range(vis.shape[1]):
                for b in range(vis.shape[3]):
                    out[c, z * vis.shape[3] + b] = (vis[c, z, 0, b, rows, :].astype(jnp.float32) * part).astype(jnp.bfloat16)


def weigh(kernel, here, vis, smooth, half, shapes):
    parts, z, _, hb, fl, length = vis.shape
    block = pl.BlockSpec((parts, z, 1, hb, fl, length), lambda i: (0, 0, half, 0, 0, 0))
    fixed = pl.BlockSpec((fl, length), lambda i: (0, 0))
    outs = [jax.ShapeDtypeStruct(s, jnp.bfloat16) for s in shapes]
    return pl.pallas_call(
        kernel,
        grid=(1,),
        out_shape=outs,
        in_specs=[SCALARS, block, fixed],
        out_specs=[pl.BlockSpec(s, lambda i: (0, 0, 0, 0)) for s in shapes],
        compiler_params=params(),
        cost_estimate=cost(0, outs + outs),
    )(here, vis, smooth)


def channels_to_baselines(here, *refs, z_count):
    n = len(refs) - z_count
    ins, outs = refs[:n], refs[n:]
    fs, hb = ins[0].shape[2], outs[0].shape[1]
    for kz, out in enumerate(outs):
        dest = here[1] ^ kz
        for k, block in enumerate(ins):
            rows = pl.ds(pl.multiple_of((here[0] ^ k) * fs, fs), fs)
            for c in range(2):
                for b in range(hb):
                    out[c, b, rows, :] = block[c, dest * hb + b]


def baselines_to_channels(here, *refs, z_count):
    ins, outs = refs[:z_count], refs[z_count:]
    fs, hb = outs[0].shape[2], ins[0].shape[1]
    for k, out in enumerate(outs):
        rows = pl.ds(pl.multiple_of((here[0] ^ k) * fs, fs), fs)
        for kz, block in enumerate(ins):
            source = here[1] ^ kz
            for c in range(2):
                for b in range(hb):
                    out[c, source * hb + b] = block[c, b, rows, :]


def repack(kernel, here, blocks, shapes, z_count):
    outs = [jax.ShapeDtypeStruct(s, jnp.bfloat16) for s in shapes]
    return pl.pallas_call(
        functools.partial(kernel, z_count=z_count),
        out_shape=outs,
        in_specs=[SCALARS] + [WHOLE] * len(blocks),
        out_specs=[WHOLE] * len(outs),
        compiler_params=params(),
        cost_estimate=cost(0, list(blocks) + outs),
    )(here, *blocks)


def transform_tables(n, length):
    group = length // n
    lane = np.arange(length)
    order = np.zeros((length, length))
    order[lane, (lane % n) * group + lane // n] = 1.0
    angle = 2.0 * np.pi / length * (np.outer(lane, lane) % length)
    cosine, sine = np.cos(angle), np.sin(angle)
    table = np.block([[cosine, -sine], [sine, cosine]])
    high = table.astype(ml_dtypes.bfloat16)
    low = (table - high.astype(np.float64)).astype(ml_dtypes.bfloat16)
    turn = 2.0 * np.pi / (n * length) * np.outer(np.arange(n), lane)
    scale = 1.0 / math.sqrt(n * length)
    twiddle = np.stack([np.cos(turn), np.sin(turn)]) * scale
    return order.astype(ml_dtypes.bfloat16), high, low, twiddle.astype(np.float32)


def short_dft(values):
    n = len(values)
    if n == 1:
        return values
    even, odd = short_dft(values[0::2]), short_dft(values[1::2])
    out = [None] * n
    for k in range(n // 2):
        real, imag = odd[k]
        if 4 * k == n:
            real, imag = imag, -real
        elif k:
            c, s = math.cos(2.0 * math.pi * k / n), math.sin(2.0 * math.pi * k / n)
            if 8 * k == n:
                real, imag = c * (real + imag), c * (imag - real)
            elif 8 * k == 3 * n:
                real, imag = s * (imag - real), -s * (real + imag)
            else:
                real, imag = c * real + s * imag, c * imag - s * real
        out[k] = (even[k][0] + real, even[k][1] + imag)
        out[k + n // 2] = (even[k][0] - real, even[k][1] - imag)
    return out


def transpose_groups(values, group):
    values, n = [list(v) for v in values], len(values)
    lane = lax.broadcasted_iota(jnp.int32, values[0][0].shape, 1)
    bit = n // 2
    while bit:
        shift = bit * group
        for i in range(n):
            if i & bit:
                continue
            a, b = values[i], values[i + bit]
            if shift >= LANES:
                step = shift // LANES
                for col in range(len(a)):
                    if not col & step:
                        a[col + step], b[col] = b[col], a[col + step]
            else:
                upper = (lane & shift) != 0
                for col in range(len(a)):
                    x, y = a[col], b[col]
                    a[col] = jnp.where(upper, pltpu.roll(y, shift, 1), x)
                    b[col] = jnp.where(upper, y, pltpu.roll(x, LANES - shift, 1))
        bit //= 2
    return values


def transform(here, order, high, low, twiddle, *refs, n):
    ins, outs = refs[:n], refs[n : 2 * n]
    ordered, lined, stage, done = refs[2 * n :]
    me = here[0]
    parts, planes, fs, length = ins[0].shape
    group, cols = length // n, length // LANES
    per = lined.shape[1] // fs

    def step(i, carry):
        for c in range(parts):
            for k in range(n):
                block = ins[k][c, pl.ds(i * per, per)].reshape(per * fs, length)
                ordered[me ^ k] = jnp.dot(block, order[...], preferred_element_type=jnp.float32)
            for r in range(0, per * fs, 16):
                values = [[ordered[p, r : r + 16, q * LANES : (q + 1) * LANES] for q in range(cols)] for p in range(n)]
                for v, columns in enumerate(transpose_groups(values, group)):
                    for q, column in enumerate(columns):
                        lined[v, r : r + 16, c * length + q * LANES : c * length + (q + 1) * LANES] = column.astype(jnp.bfloat16)
        flat = lined[...].reshape(n * per * fs, 2 * length)
        total = jnp.dot(flat, high[...], preferred_element_type=jnp.float32)
        total = total + jnp.dot(flat, low[...], preferred_element_type=jnp.float32)
        stage[...] = total.reshape(n, per * fs, 2 * length)
        for r in range(0, per * fs, 16):
            for q in range(cols):
                first, second = slice(q * LANES, (q + 1) * LANES), slice(length + q * LANES, length + (q + 1) * LANES)
                turned = []
                for v in range(n):
                    real, imag = stage[v, r : r + 16, first], stage[v, r : r + 16, second]
                    c, s = twiddle[0, v : v + 1, first], twiddle[1, v : v + 1, first]
                    turned.append((real * c + imag * s, imag * c - real * s))
                for m, pair in enumerate(short_dft(turned)):
                    for c in range(2):
                        done[m, c, r : r + 16, first] = pair[c].astype(jnp.bfloat16)
        for k in range(n):
            for c in range(2):
                outs[k][c, pl.ds(i * per, per)] = done[me ^ k, c].reshape(per, fs, length)
        return carry

    lax.fori_loop(0, planes // per, step, 0)


def transform_call(here, blocks):
    n = len(blocks)
    parts, planes, fs, length = blocks[0].shape
    per = math.gcd(planes, 4)
    rows = per * fs
    tables = transform_tables(n, length)
    outs = [jax.ShapeDtypeStruct(b.shape, jnp.bfloat16) for b in blocks]
    return pl.pallas_call(
        functools.partial(transform, n=n),
        out_shape=outs,
        in_specs=[SCALARS] + [WHOLE] * (4 + n),
        out_specs=[WHOLE] * n,
        scratch_shapes=[
            pltpu.VMEM((n, rows, length), jnp.float32),
            pltpu.VMEM((n, rows, 2 * length), jnp.bfloat16),
            pltpu.VMEM((n, rows, 2 * length), jnp.float32),
            pltpu.VMEM((n, 2, rows, length), jnp.bfloat16),
        ],
        compiler_params=params(),
        cost_estimate=cost(4 * n * planes * fs * (2 * length) ** 2, list(blocks) + outs),
    )(here, *[jnp.asarray(t) for t in tables], *blocks)


def filter_kernel(classes, here, bank, *refs, count, from_baselines, aliased):
    ins, out, lined = refs[:count], refs[count + aliased], refs[-1]
    b = pl.program_id(0)
    length = out.shape[-1]
    if from_baselines:
        fl = ins[0].shape[2]
        for kz, block in enumerate(ins):
            rows = pl.ds(pl.multiple_of((here[1] ^ kz) * fl, fl), fl)
            for c in range(2):
                lined[rows, c * length : (c + 1) * length] = block[c, b].astype(lined.dtype)
    else:
        hb, fs = pl.num_programs(0), ins[0].shape[2]
        fl = fs * count
        for k, block in enumerate(ins):
            for z in range(lined.shape[0] // fl):
                rows = pl.ds(pl.multiple_of(z * fl + (here[0] ^ k) * fs, fs), fs)
                for c in range(2):
                    lined[rows, c * length : (c + 1) * length] = block[c, z * hb + b].astype(lined.dtype)
    total = jnp.dot(bank[0], lined[...].astype(jnp.bfloat16), preferred_element_type=jnp.float32)
    for c in range(2):
        out[c, 0] = total[:, c * length : (c + 1) * length].astype(jnp.bfloat16)


def delay_filter(classes, here, bank, blocks, half, hb, out_shape, before, from_baselines):
    _, channels, _ = bank.shape
    length = out_shape[-1]
    fixed = [pl.BlockSpec(b.shape, lambda i, classes, here: (0, 0, 0, 0)) for b in blocks]
    specs = [pl.BlockSpec((1, channels, channels), lambda i, classes, here: (classes[half * hb + i], 0, 0))] + fixed
    operands = [bank] + list(blocks)
    aliases = {}
    if before is not None:
        specs.append(pl.BlockSpec(memory_space=pl.ANY))
        operands.append(before)
        aliases = {2 + len(operands) - 1: 0}
    out = jax.ShapeDtypeStruct(out_shape, jnp.bfloat16)
    return pl.pallas_call(
        functools.partial(
            filter_kernel, count=len(blocks), from_baselines=from_baselines, aliased=int(before is not None)
        ),
        out_shape=out,
        grid_spec=pltpu.PrefetchScalarGridSpec(
            num_scalar_prefetch=2,
            grid=(hb,),
            in_specs=specs,
            out_specs=pl.BlockSpec((2, 1, channels, length), lambda i, classes, here: (0, half * hb + i, 0, 0)),
            scratch_shapes=[pltpu.VMEM((channels, 2 * length), row_type(blocks[0].shape[2]))],
        ),
        input_output_aliases=aliases,
        compiler_params=params(),
        cost_estimate=cost(4 * hb * length * channels**2, list(blocks) + [out]),
    )(classes, here, *operands)


def shards(
    visibility,
    spectrum_power_sum,
    square_sum,
    accum_count,
    rfi_mask,
    baseline_delay_class,
    filter_bank,
):
    n, z_count = lax.axis_size("tm"), lax.axis_size("freq")
    parts, baselines, fl, length = visibility.shape
    fs, hb = fl // n, baselines // z_count // 2
    here = jnp.stack([lax.axis_index("tm"), lax.axis_index("freq")]).astype(jnp.int32)
    classes = baseline_delay_class[:, 0]
    smooth = smoothing_weights(spectrum_power_sum, square_sum, accum_count, rfi_mask)
    vis = visibility.reshape(parts, z_count, 2, hb, fl, length)
    by_channel = [(parts, z_count * hb, fs, length)] * n
    by_baseline = [(parts, hb, fl, length)] * z_count
    out_shape = (parts, 2 * hb, fl * z_count, length)

    late = weigh(weigh_by_baseline, here, vis, smooth, 1, by_baseline)
    late = exchange(late, "freq")
    early = weigh(weigh_by_channel, here, vis, smooth, 0, by_channel)
    early = transform_call(here, exchange(early, "tm"))
    early = repack(channels_to_baselines, here, exchange(early, "tm"), by_baseline, z_count)
    early = exchange(early, "freq")

    late = repack(baselines_to_channels, here, late, by_channel, z_count)
    late = transform_call(here, exchange(late, "tm"))
    late = exchange(late, "tm")
    filtered = delay_filter(classes, here, filter_bank, early, 0, hb, out_shape, None, True)
    return delay_filter(classes, here, filter_bank, late, 1, hb, out_shape, filtered, False)


def solution(mesh):
    in_specs = (
        P(None, None, "freq", "tm"),
        P("freq", "tm"),
        P("freq", "tm"),
        P("freq", "tm"),
        P("freq", "tm"),
        P("freq", None),
        P(),
    )
    out_specs = P(None, "freq", None, "tm")
    return jax.shard_map(shards, mesh=mesh, in_specs=in_specs, out_specs=out_specs, check_vma=False)
```

time: 231 us -> 103 us (0.45)
  local copies, waits for them, and re-layouts: 88.5 us -> 1.69 us
  blocking collectives: 30.9 us -> 0 us
  waiting for transfers between devices: 71.9 us -> 43.3 us
  starting transfers between devices: 13.6 us -> 38.7 us
  Pallas kernels: 0 us -> 15.2 us
  matrix products: 14.4 us -> 0 us
  other arithmetic: 10.8 us -> 2.92 us
    all_to_all x2 -> x0, waiting for transfers between devices: 70 us -> none  [the longest x1 45.6 us: shards(): lax.all_to_all(moved, 'freq', split_axis=1, concat_axis=2, tiled=True)]
    ppermute x2 -> x36, waiting for transfers between devices: 1.91 us -> 43.3 us  [the longest x34 41.5 us: swap(): return lax.ppermute(value, axis, [(i, i ^ k) for i in range(size)])]
    ppermute x2 -> x36, starting transfers between devices: 3.42 us -> 38.7 us  [the longest x34 35.3 us: swap(): return lax.ppermute(value, axis, [(i, i ^ k) for i in range(size)])]
    unnamed x6 -> x14, local copies, waits for them, and re-layouts: 33.5 us -> 1.61 us
    all_to_all x1 -> x0, blocking collectives: 30.9 us -> none  [shards(): lax.all_to_all(spectrum, 'tm', split_axis=3, concat_axis=2, tiled=True)]
    convert_element_type x2 -> x0, local copies, waits for them, and re-layouts: 27.6 us -> none  [the longest x1 23.5 us: sidereal_transform(): return finished.astype(jnp.bfloat16)]
    all_to_all x3 -> x0, local copies, waits for them, and re-layouts: 25.3 us -> none  [the longest x1 17 us: shards(): lax.all_to_all(spectrum, 'tm', split_axis=3, concat_axis=2, tiled=True)]
    pallas_call x0 -> x8, Pallas kernels: none -> 15.2 us  [the longest x2 7.82 us: transform_call(): pl.pallas_call(functools.partial(transform, n=n), out_shape=outs, in_spec...]
  transfers between devices with their start and end apart: 4 -> 36, of which waited for: 3 -> 14; matrix products, arithmetic and copies ran while one was open for 2% -> 0% of each run, Pallas kernels for 0% -> 12%
where the time goes in v1:
time: 103 us; the launch traced here: 102 us
  waiting for transfers between devices  43.3 us (42%)
  starting transfers between devices  38.7 us (38%)
  Pallas kernels  15.2 us (15%)
  other arithmetic  2.92 us (3%)
  local copies, waits for them, and re-layouts  1.69 us (2%)
    ppermute x34, waiting for transfers between devices, swap(): return lax.ppermute(value, axis, [(i, i ^ k) for i in range(size)])  41.5 us
    ppermute x34, starting transfers between devices, swap(): return lax.ppermute(value, axis, [(i, i ^ k) for i in range(size)])  35.3 us
    pallas_call x2, Pallas kernels, transform_call(): pl.pallas_call(functools.partial(transform, n=n), out_shape=outs, in_spec...  7.82 us
    pallas_call x2, Pallas kernels, delay_filter(): pl.pallas_call(functools.partial(filter_kernel, count=len(blocks), from_b...  4.69 us
    ppermute x1, starting transfers between devices, smoothing_weights(): after = lax.ppermute(flag_weight[:, :RIM], 'tm', [(j, i) for i, j in up])  2.95 us
  transfers between devices with their start and end apart: 36, of which 14 were waited for; matrix products, arithmetic and copies ran while one was open for 0% of the time, Pallas kernels for 12%

profile of v1, /device:TPU:0, one launch (start us, length us, event | category | flops | bytes accessed | tf_op | source)
XLA Modules:
  0.0 102.1 jit_solution(2742109403467628717)
XLA Ops:
  0.0 1.2 %exponential_multiply_fusion = f32[128,256]{1,0:T(8,128)S(1)} fusion(f32[128,256]{1,0:T(8,128)} %param.16, f32[128,256]{1,0:T(8,128)} %param.17, s32[128,256]{1,0:T(8,128)} %param.18, s32[128,256]{1,0:T(8,128)} %param.19), kind=kLoop, calls=%fused_computation.156 | loop fusion | flops 458752 | bytes 655360 | tf_op jit(solution)/shard_map/mul | solution.py:53
  1.7 2.9 %collective-permute-start.1 = (f32[128,16]{1,0:T(8,128)S(1)}, f32[128,16]{1,0:T(8,128)S(1)}, u32[]{:S(2)}, u32[]{:S(2)}) collective-permute-start(f32[128,16]{1,0:T(8,128)S(1)} %get-tuple-element.86), channel_id=1, source_target_pairs={{4,0},{8,4},{12,8},{16,12},{20,16},{24,20},{28,24},{0,28},{5,1},{9... | collective-permute-start | bytes 24584 | tf_op jit(solution)/shard_map/ppermute | solution.py:57
  4.8 1.8 %collective-permute-done = f32[128,16]{1,0:T(8,128)S(1)} collective-permute-done((f32[128,16]{1,0:T(8,128)S(1)}, f32[128,16]{1,0:T(8,128)S(1)}, u32[]{:S(2)}, u32[]{:S(2)}) %collective-permute-start) | collective-permute-done | bytes 8224 | tf_op jit(solution)/shard_map/ppermute | solution.py:56
  6.6 1.7 %fusion.3.smooth = f32[128,256]{1,0:T(8,128)S(1)} fusion(f32[128,256]{1,0:T(8,128)S(1)} %exponential_multiply_fusion, f32[128,16]{1,0:T(8,128)S(1)} %collective-permute-done.1, f32[128,16]{1,0:T(8,128)S(1)} %collective-permute-done), kind=kLoop, calls=%fused_computation.63 | loop fusion | flops 3178496 | bytes 278528 | tf_op jit(solution)/shard_map/add | solution.py:62
  8.3 1.6 %copy-done = bf16[2,16,128,256]{3,2,1,0:T(8,128)(2,1)S(1)} copy-done((bf16[2,16,128,256]{3,2,1,0:T(8,128)(2,1)S(1)}, bf16[2,16,128,256]{3,2,1,0:T(8,128)(2,1)}, u32[]{:S(2)}) %copy-start) | copy-done | bytes 2097176
  10.6 1.5 %collective-permute-start.19 = (bf16[2,8,16,256]{3,2,1,0:T(8,128)(2,1)S(1)}, bf16[2,8,16,256]{3,2,1,0:T(8,128)(2,1)S(1)}, u32[]{:S(2)}, u32[]{:S(2)}) collective-permute-start(bf16[2,8,16,256]{3,2,1,0:T(8,128)(2,1)S(1)} %get-tuple-element.66), channel_id=1, source_target_pairs={{0,4},{4,0},{8,12},{12,8},{16,20},{20,16},{24,28},{28,24},{1,5},{5... | collective-permute-start | bytes 393224 | tf_op jit(solution)/shard_map/ppermute | solution.py:35
  12.1 2.4 %collective-permute-start.20 = (bf16[2,8,16,256]{3,2,1,0:T(8,128)(2,1)S(1)}, bf16[2,8,16,256]{3,2,1,0:T(8,128)(2,1)S(1)}, u32[]{:S(2)}, u32[]{:S(2)}) collective-permute-start(bf16[2,8,16,256]{3,2,1,0:T(8,128)(2,1)S(1)} %get-tuple-element.67), channel_id=1, source_target_pairs={{0,8},{4,12},{8,0},{12,4},{16,24},{20,28},{24,16},{28,20},{1,9},{5... | collective-permute-start | bytes 393224 | tf_op jit(solution)/shard_map/ppermute | solution.py:35
  16.0 1.7 %collective-permute-start.24 = (bf16[2,8,16,256]{3,2,1,0:T(8,128)(2,1)S(1)}, bf16[2,8,16,256]{3,2,1,0:T(8,128)(2,1)S(1)}, u32[]{:S(2)}, u32[]{:S(2)}) collective-permute-start(bf16[2,8,16,256]{3,2,1,0:T(8,128)(2,1)S(1)} %get-tuple-element.71), channel_id=1, source_target_pairs={{0,24},{4,28},{8,16},{12,20},{16,8},{20,12},{24,0},{28,4},{1,25},{... | collective-permute-start | bytes 393224 | tf_op jit(solution)/shard_map/ppermute | solution.py:35
  19.6 1.5 %collective-permute-done.21.refs_3_ = bf16[2,8,16,256]{3,2,1,0:T(8,128)(2,1)S(1)} collective-permute-done((bf16[2,8,16,256]{3,2,1,0:T(8,128)(2,1)S(1)}, bf16[2,8,16,256]{3,2,1,0:T(8,128)(2,1)S(1)}, u32[]{:S(2)}, u32[]{:S(2)}) %collective-permute-start.21) | collective-permute-done | bytes 131104 | tf_op jit(solution)/shard_map/ppermute | solution.py:35
  21.2 1.6 %collective-permute-start.2 = (bf16[2,2,128,256]{3,2,1,0:T(8,128)(2,1)S(1)}, bf16[2,2,128,256]{3,2,1,0:T(8,128)(2,1)S(1)}, u32[]{:S(2)}, u32[]{:S(2)}) collective-permute-start(bf16[2,2,128,256]{3,2,1,0:T(8,128)(2,1)S(1)} %get-tuple-element.46), channel_id=1, source_target_pairs={{0,1},{1,0},{2,3},{3,2},{4,5},{5,4},{6,7},{7,6},{8,9},{9,8},{10,11... | collective-permute-start | bytes 786440 | tf_op jit(solution)/shard_map/ppermute | solution.py:35
  22.8 2.6 %collective-permute-start.3 = (bf16[2,2,128,256]{3,2,1,0:T(8,128)(2,1)S(1)}, bf16[2,2,128,256]{3,2,1,0:T(8,128)(2,1)S(1)}, u32[]{:S(2)}, u32[]{:S(2)}) collective-permute-start(bf16[2,2,128,256]{3,2,1,0:T(8,128)(2,1)S(1)} %get-tuple-element.47), channel_id=1, source_target_pairs={{0,2},{1,3},{2,0},{3,1},{4,6},{5,7},{6,4},{7,5},{8,10},{9,11},{10,... | collective-permute-start | bytes 786440 | tf_op jit(solution)/shard_map/ppermute | solution.py:35
  25.3 2.3 %collective-permute-done.23.refs_5_ = bf16[2,8,16,256]{3,2,1,0:T(8,128)(2,1)S(1)} collective-permute-done((bf16[2,8,16,256]{3,2,1,0:T(8,128)(2,1)S(1)}, bf16[2,8,16,256]{3,2,1,0:T(8,128)(2,1)S(1)}, u32[]{:S(2)}, u32[]{:S(2)}) %collective-permute-start.23) | collective-permute-done | bytes 131104 | tf_op jit(solution)/shard_map/ppermute | solution.py:35
  27.7 3.6 %collective-permute-start.4 = (bf16[2,2,128,256]{3,2,1,0:T(8,128)(2,1)S(1)}, bf16[2,2,128,256]{3,2,1,0:T(8,128)(2,1)S(1)}, u32[]{:S(2)}, u32[]{:S(2)}) collective-permute-start(bf16[2,2,128,256]{3,2,1,0:T(8,128)(2,1)S(1)} %get-tuple-element.48), channel_id=1, source_target_pairs={{0,3},{1,2},{2,1},{3,0},{4,7},{5,6},{6,5},{7,4},{8,11},{9,10},{10,... | collective-permute-start | bytes 786440 | tf_op jit(solution)/shard_map/ppermute | solution.py:35
  31.3 3.9 %shard_map.149 = (bf16[2,8,16,256]{3,2,1,0:T(8,128)(2,1)S(1)}, bf16[2,8,16,256]{3,2,1,0:T(8,128)(2,1)S(1)}, bf16[2,8,16,256]{3,2,1,0:T(8,128)(2,1)S(1)}, bf16[2,...) custom-call(s32[2]{0:T(128)S(1)} %pad_add_fusion.here, ...), custom_call_target="tpu_custom_call" | custom-call | flops 1073741824 | bytes 2097152 | tf_op jit(solution)/shard_map/pallas_call | solution.py:252
  35.9 2.0 %collective-permute-start.27 = (bf16[2,8,16,256]{3,2,1,0:T(8,128)(2,1)S(1)}, bf16[2,8,16,256]{3,2,1,0:T(8,128)(2,1)S(1)}, u32[]{:S(2)}, u32[]{:S(2)}) collective-permute-start(bf16[2,8,16,256]{3,2,1,0:T(8,128)(2,1)S(1)} %get-tuple-element.75), channel_id=1, source_target_pairs={{0,8},{4,12},{8,0},{12,4},{16,24},{20,28},{24,16},{28,20},{1,9},{5... | collective-permute-start | bytes 393224 | tf_op jit(solution)/shard_map/ppermute | solution.py:35
  39.0 3.4 %collective-permute-done.27.refs_2_ = bf16[2,8,16,256]{3,2,1,0:T(8,128)(2,1)S(1)} collective-permute-done((bf16[2,8,16,256]{3,2,1,0:T(8,128)(2,1)S(1)}, bf16[2,8,16,256]{3,2,1,0:T(8,128)(2,1)S(1)}, u32[]{:S(2)}, u32[]{:S(2)}) %collective-permute-start.27) | collective-permute-done | bytes 131104 | tf_op jit(solution)/shard_map/ppermute | solution.py:35
  43.6 2.2 %collective-permute-start.31 = (bf16[2,8,16,256]{3,2,1,0:T(8,128)(2,1)S(1)}, bf16[2,8,16,256]{3,2,1,0:T(8,128)(2,1)S(1)}, u32[]{:S(2)}, u32[]{:S(2)}) collective-permute-start(bf16[2,8,16,256]{3,2,1,0:T(8,128)(2,1)S(1)} %get-tuple-element.79), channel_id=1, source_target_pairs={{0,24},{4,28},{8,16},{12,20},{16,8},{20,12},{24,0},{28,4},{1,25},{... | collective-permute-start | bytes 393224 | tf_op jit(solution)/shard_map/ppermute | solution.py:35
  47.4 6.4 %collective-permute-done.29.refs_4_ = bf16[2,8,16,256]{3,2,1,0:T(8,128)(2,1)S(1)} collective-permute-done((bf16[2,8,16,256]{3,2,1,0:T(8,128)(2,1)S(1)}, bf16[2,8,16,256]{3,2,1,0:T(8,128)(2,1)S(1)}, u32[]{:S(2)}, u32[]{:S(2)}) %collective-permute-start.29) | collective-permute-done | bytes 131104 | tf_op jit(solution)/shard_map/ppermute | solution.py:35
  54.7 1.5 %collective-permute-start.7 = (bf16[2,8,16,256]{3,2,1,0:T(8,128)(2,1)S(1)}, bf16[2,8,16,256]{3,2,1,0:T(8,128)(2,1)S(1)}, u32[]{:S(2)}, u32[]{:S(2)}) collective-permute-start(bf16[2,8,16,256]{3,2,1,0:T(8,128)(2,1)S(1)} %get-tuple-element.52), channel_id=1, source_target_pairs={{0,12},{4,8},{8,4},{12,0},{16,28},{20,24},{24,20},{28,16},{1,13},{... | collective-permute-start | bytes 393224 | tf_op jit(solution)/shard_map/ppermute | solution.py:35
  56.2 1.3 %collective-permute-start.8 = (bf16[2,8,16,256]{3,2,1,0:T(8,128)(2,1)S(1)}, bf16[2,8,16,256]{3,2,1,0:T(8,128)(2,1)S(1)}, u32[]{:S(2)}, u32[]{:S(2)}) collective-permute-start(bf16[2,8,16,256]{3,2,1,0:T(8,128)(2,1)S(1)} %get-tuple-element.53), channel_id=1, source_target_pairs={{0,16},{4,20},{8,24},{12,28},{16,0},{20,4},{24,8},{28,12},{1,17},{... | collective-permute-start | bytes 393224 | tf_op jit(solution)/shard_map/ppermute | solution.py:35
  57.6 1.2 %collective-permute-start.10 = (bf16[2,8,16,256]{3,2,1,0:T(8,128)(2,1)S(1)}, bf16[2,8,16,256]{3,2,1,0:T(8,128)(2,1)S(1)}, u32[]{:S(2)}, u32[]{:S(2)}) collective-permute-start(bf16[2,8,16,256]{3,2,1,0:T(8,128)(2,1)S(1)} %get-tuple-element.55), channel_id=1, source_target_pairs={{0,24},{4,28},{8,16},{12,20},{16,8},{20,12},{24,0},{28,4},{1,25},{... | collective-permute-start | bytes 393224 | tf_op jit(solution)/shard_map/ppermute | solution.py:35
  58.8 1.2 %collective-permute-done.6.refs_2_ = bf16[2,8,16,256]{3,2,1,0:T(8,128)(2,1)S(1)} collective-permute-done((bf16[2,8,16,256]{3,2,1,0:T(8,128)(2,1)S(1)}, bf16[2,8,16,256]{3,2,1,0:T(8,128)(2,1)S(1)}, u32[]{:S(2)}, u32[]{:S(2)}) %collective-permute-start.6) | collective-permute-done | bytes 131104 | tf_op jit(solution)/shard_map/ppermute | solution.py:35
  61.4 6.6 %collective-permute-done.8.refs_4_ = bf16[2,8,16,256]{3,2,1,0:T(8,128)(2,1)S(1)} collective-permute-done((bf16[2,8,16,256]{3,2,1,0:T(8,128)(2,1)S(1)}, bf16[2,8,16,256]{3,2,1,0:T(8,128)(2,1)S(1)}, u32[]{:S(2)}, u32[]{:S(2)}) %collective-permute-start.8) | collective-permute-done | bytes 131104 | tf_op jit(solution)/shard_map/ppermute | solution.py:35
  68.0 1.1 %collective-permute-done.9.refs_5_ = bf16[2,8,16,256]{3,2,1,0:T(8,128)(2,1)S(1)} collective-permute-done((bf16[2,8,16,256]{3,2,1,0:T(8,128)(2,1)S(1)}, bf16[2,8,16,256]{3,2,1,0:T(8,128)(2,1)S(1)}, u32[]{:S(2)}, u32[]{:S(2)}) %collective-permute-start.9) | collective-permute-done | bytes 131104 | tf_op jit(solution)/shard_map/ppermute | solution.py:35
  69.6 3.9 %shard_map.147 = (bf16[2,8,16,256]{3,2,1,0:T(8,128)(2,1)S(1)}, bf16[2,8,16,256]{3,2,1,0:T(8,128)(2,1)S(1)}, bf16[2,8,16,256]{3,2,1,0:T(8,128)(2,1)S(1)}, bf16[2,...) custom-call(s32[2]{0:T(128)S(1)} %pad_add_fusion.here, ...), custom_call_target="tpu_custom_call" | custom-call | flops 1073741824 | bytes 2097152 | tf_op jit(solution)/shard_map/pallas_call | solution.py:252
  73.5 1.3 %collective-permute-start.12 = (bf16[2,8,16,256]{3,2,1,0:T(8,128)(2,1)S(1)}, bf16[2,8,16,256]{3,2,1,0:T(8,128)(2,1)S(1)}, u32[]{:S(2)}, u32[]{:S(2)}) collective-permute-start(bf16[2,8,16,256]{3,2,1,0:T(8,128)(2,1)S(1)} %get-tuple-element.58), channel_id=1, source_target_pairs={{0,4},{4,0},{8,12},{12,8},{16,20},{20,16},{24,28},{28,24},{1,5},{5... | collective-permute-start | bytes 393224 | tf_op jit(solution)/shard_map/ppermute | solution.py:35
  76.2 11.0 %collective-permute-done.34.refs_2_ = bf16[2,2,128,256]{3,2,1,0:T(8,128)(2,1)S(1)} collective-permute-done((bf16[2,2,128,256]{3,2,1,0:T(8,128)(2,1)S(1)}, bf16[2,2,128,256]{3,2,1,0:T(8,128)(2,1)S(1)}, u32[]{:S(2)}, u32[]{:S(2)}) %collective-permute-start.34) | collective-permute-done | bytes 262176 | tf_op jit(solution)/shard_map/ppermute | solution.py:35
  87.3 1.1 %collective-permute-start.15 = (bf16[2,8,16,256]{3,2,1,0:T(8,128)(2,1)S(1)}, bf16[2,8,16,256]{3,2,1,0:T(8,128)(2,1)S(1)}, u32[]{:S(2)}, u32[]{:S(2)}) collective-permute-start(bf16[2,8,16,256]{3,2,1,0:T(8,128)(2,1)S(1)} %get-tuple-element.61), channel_id=1, source_target_pairs={{0,16},{4,20},{8,24},{12,28},{16,0},{20,4},{24,8},{28,12},{1,17},{... | collective-permute-start | bytes 393224 | tf_op jit(solution)/shard_map/ppermute | solution.py:35
  89.4 2.3 %collective-permute-start.18 = (bf16[2,8,16,256]{3,2,1,0:T(8,128)(2,1)S(1)}, bf16[2,8,16,256]{3,2,1,0:T(8,128)(2,1)S(1)}, u32[]{:S(2)}, u32[]{:S(2)}) collective-permute-start(bf16[2,8,16,256]{3,2,1,0:T(8,128)(2,1)S(1)} %get-tuple-element.64), channel_id=1, source_target_pairs={{0,28},{4,24},{8,20},{12,16},{16,12},{20,8},{24,4},{28,0},{1,29},{... | collective-permute-start | bytes 393224 | tf_op jit(solution)/shard_map/ppermute | solution.py:35
  91.7 2.3 %shard_map.151.refs_8_ = bf16[2,4,512,256]{3,2,1,0:T(8,128)(2,1)} custom-call(s32[4]{0:T(128)S(1)} %bitcast.6, s32[2]{0:T(128)S(1)} %pad_add_fusion.here, bf16[4,512,512]{2,1,0:T(8,128)(2,1)S(1)} %copy-done.1, bf16[2,2,128,256]{3,2,1,0:T(8,128)(2,1)S(1)} %get-tuple-element.81.refs_0_, bf16[2,2,128,256]{3,2,1,0:T(8,128)(2,1)S(1)} %collective-permute-done.33.refs_1_, ...), custom_call_target="tpu_custom_call" | custom-call | flops 536870912 | bytes 3145728 | tf_op jit(solution)/shard_map/pallas_call | solution.py:303
  94.0 4.8 %collective-permute-done.15.refs_4_ = bf16[2,8,16,256]{3,2,1,0:T(8,128)(2,1)S(1)} collective-permute-done((bf16[2,8,16,256]{3,2,1,0:T(8,128)(2,1)S(1)}, bf16[2,8,16,256]{3,2,1,0:T(8,128)(2,1)S(1)}, u32[]{:S(2)}, u32[]{:S(2)}) %collective-permute-start.15) | collective-permute-done | bytes 131104 | tf_op jit(solution)/shard_map/ppermute | solution.py:35
  99.7 2.4 %shard_map.152 = bf16[2,4,512,256]{3,2,1,0:T(8,128)(2,1)} custom-call(s32[4]{0:T(128)S(1)} %bitcast.7, s32[2]{0:T(128)S(1)} %pad_add_fusion.here, bf16[4,512,512]{2,1,0:T(8,128)(2,1)S(1)} %copy-done.1, bf16[2,8,16,256]{3,2,1,0:T(8,128)(2,1)S(1)} %get-tuple-element.57.refs_0_, ...), custom_call_target="tpu_custom_call", output_to_operand_aliasing={{}: (11, {})} | custom-call | flops 536870912 | bytes 3145728 | tf_op jit(solution)/shard_map/pallas_call | solution.py:303
  (66 shorter events, 15.5 us)
Async XLA Ops:
  12.1 6.7 %collective-permute-start.20 = (bf16[2,8,16,256]{3,2,1,0:T(8,128)(2,1)S(1)}, bf16[2,8,16,256]{3,2,1,0:T(8,128)(2,1)S(1)}, u32[]{:S(2)}, u32[]{:S(2)}) collective-permute-start(bf16[2,8,16,256]{3,2,1,0:T(8,128)(2,1)S(1)} %get-tuple-element.67), channel_id=1, source_target_pairs={{0,8},{4,12},{8,0},{12,4},{16,24},{20,28},{24,16},{28,20},{1,9},{5... | collective-permute-start | bytes 393224 | tf_op jit(solution)/shard_map/ppermute | solution.py:35
  14.5 6.7 %collective-permute-start.21 = (bf16[2,8,16,256]{3,2,1,0:T(8,128)(2,1)S(1)}, bf16[2,8,16,256]{3,2,1,0:T(8,128)(2,1)S(1)}, u32[]{:S(2)}, u32[]{:S(2)}) collective-permute-start(bf16[2,8,16,256]{3,2,1,0:T(8,128)(2,1)S(1)} %get-tuple-element.68), channel_id=1, source_target_pairs={{0,12},{4,8},{8,4},{12,0},{16,28},{20,24},{24,20},{28,16},{1,13},{... | collective-permute-start | bytes 393224 | tf_op jit(solution)/shard_map/ppermute | solution.py:35
  14.5 8.3 %collective-permute-start.22 = (bf16[2,8,16,256]{3,2,1,0:T(8,128)(2,1)S(1)}, bf16[2,8,16,256]{3,2,1,0:T(8,128)(2,1)S(1)}, u32[]{:S(2)}, u32[]{:S(2)}) collective-permute-start(bf16[2,8,16,256]{3,2,1,0:T(8,128)(2,1)S(1)} %get-tuple-element.69), channel_id=1, source_target_pairs={{0,16},{4,20},{8,24},{12,28},{16,0},{20,4},{24,8},{28,12},{1,17},{... | collective-permute-start | bytes 393224 | tf_op jit(solution)/shard_map/ppermute | solution.py:35
  15.1 12.6 %collective-permute-start.23 = (bf16[2,8,16,256]{3,2,1,0:T(8,128)(2,1)S(1)}, bf16[2,8,16,256]{3,2,1,0:T(8,128)(2,1)S(1)}, u32[]{:S(2)}, u32[]{:S(2)}) collective-permute-start(bf16[2,8,16,256]{3,2,1,0:T(8,128)(2,1)S(1)} %get-tuple-element.70), channel_id=1, source_target_pairs={{0,20},{4,16},{8,28},{12,24},{16,4},{20,0},{24,12},{28,8},{1,21},{... | collective-permute-start | bytes 393224 | tf_op jit(solution)/shard_map/ppermute | solution.py:35
  16.0 15.3 %collective-permute-start.24 = (bf16[2,8,16,256]{3,2,1,0:T(8,128)(2,1)S(1)}, bf16[2,8,16,256]{3,2,1,0:T(8,128)(2,1)S(1)}, u32[]{:S(2)}, u32[]{:S(2)}) collective-permute-start(bf16[2,8,16,256]{3,2,1,0:T(8,128)(2,1)S(1)} %get-tuple-element.71), channel_id=1, source_target_pairs={{0,24},{4,28},{8,16},{12,20},{16,8},{20,12},{24,0},{28,4},{1,25},{... | collective-permute-start | bytes 393224 | tf_op jit(solution)/shard_map/ppermute | solution.py:35
  18.8 12.5 %collective-permute-start.25 = (bf16[2,8,16,256]{3,2,1,0:T(8,128)(2,1)S(1)}, bf16[2,8,16,256]{3,2,1,0:T(8,128)(2,1)S(1)}, u32[]{:S(2)}, u32[]{:S(2)}) collective-permute-start(bf16[2,8,16,256]{3,2,1,0:T(8,128)(2,1)S(1)} %get-tuple-element.72), channel_id=1, source_target_pairs={{0,28},{4,24},{8,20},{12,16},{16,12},{20,8},{24,4},{28,0},{1,29},{... | collective-permute-start | bytes 393224 | tf_op jit(solution)/shard_map/ppermute | solution.py:35
  21.2 22.2 %collective-permute-start.2 = (bf16[2,2,128,256]{3,2,1,0:T(8,128)(2,1)S(1)}, bf16[2,2,128,256]{3,2,1,0:T(8,128)(2,1)S(1)}, u32[]{:S(2)}, u32[]{:S(2)}) collective-permute-start(bf16[2,2,128,256]{3,2,1,0:T(8,128)(2,1)S(1)} %get-tuple-element.46), channel_id=1, source_target_pairs={{0,1},{1,0},{2,3},{3,2},{4,5},{5,4},{6,7},{7,6},{8,9},{9,8},{10,11... | collective-permute-start | bytes 786440 | tf_op jit(solution)/shard_map/ppermute | solution.py:35
  22.8 20.9 %collective-permute-start.3 = (bf16[2,2,128,256]{3,2,1,0:T(8,128)(2,1)S(1)}, bf16[2,2,128,256]{3,2,1,0:T(8,128)(2,1)S(1)}, u32[]{:S(2)}, u32[]{:S(2)}) collective-permute-start(bf16[2,2,128,256]{3,2,1,0:T(8,128)(2,1)S(1)} %get-tuple-element.47), channel_id=1, source_target_pairs={{0,2},{1,3},{2,0},{3,1},{4,6},{5,7},{6,4},{7,5},{8,10},{9,11},{10,... | collective-permute-start | bytes 786440 | tf_op jit(solution)/shard_map/ppermute | solution.py:35
  27.7 18.1 %collective-permute-start.4 = (bf16[2,2,128,256]{3,2,1,0:T(8,128)(2,1)S(1)}, bf16[2,2,128,256]{3,2,1,0:T(8,128)(2,1)S(1)}, u32[]{:S(2)}, u32[]{:S(2)}) collective-permute-start(bf16[2,2,128,256]{3,2,1,0:T(8,128)(2,1)S(1)} %get-tuple-element.48), channel_id=1, source_target_pairs={{0,3},{1,2},{2,1},{3,0},{4,7},{5,6},{6,5},{7,4},{8,11},{9,10},{10,... | collective-permute-start | bytes 786440 | tf_op jit(solution)/shard_map/ppermute | solution.py:35
  35.9 6.4 %collective-permute-start.27 = (bf16[2,8,16,256]{3,2,1,0:T(8,128)(2,1)S(1)}, bf16[2,8,16,256]{3,2,1,0:T(8,128)(2,1)S(1)}, u32[]{:S(2)}, u32[]{:S(2)}) collective-permute-start(bf16[2,8,16,256]{3,2,1,0:T(8,128)(2,1)S(1)} %get-tuple-element.75), channel_id=1, source_target_pairs={{0,8},{4,12},{8,0},{12,4},{16,24},{20,28},{24,16},{28,20},{1,9},{5... | collective-permute-start | bytes 393224 | tf_op jit(solution)/shard_map/ppermute | solution.py:35
  37.9 9.4 %collective-permute-start.28 = (bf16[2,8,16,256]{3,2,1,0:T(8,128)(2,1)S(1)}, bf16[2,8,16,256]{3,2,1,0:T(8,128)(2,1)S(1)}, u32[]{:S(2)}, u32[]{:S(2)}) collective-permute-start(bf16[2,8,16,256]{3,2,1,0:T(8,128)(2,1)S(1)} %get-tuple-element.76), channel_id=1, source_target_pairs={{0,12},{4,8},{8,4},{12,0},{16,28},{20,24},{24,20},{28,16},{1,13},{... | collective-permute-start | bytes 393224 | tf_op jit(solution)/shard_map/ppermute | solution.py:35
  42.3 11.6 %collective-permute-start.29 = (bf16[2,8,16,256]{3,2,1,0:T(8,128)(2,1)S(1)}, bf16[2,8,16,256]{3,2,1,0:T(8,128)(2,1)S(1)}, u32[]{:S(2)}, u32[]{:S(2)}) collective-permute-start(bf16[2,8,16,256]{3,2,1,0:T(8,128)(2,1)S(1)} %get-tuple-element.77), channel_id=1, source_target_pairs={{0,16},{4,20},{8,24},{12,28},{16,0},{20,4},{24,8},{28,12},{1,17},{... | collective-permute-start | bytes 393224 | tf_op jit(solution)/shard_map/ppermute | solution.py:35
  43.4 11.3 %collective-permute-start.30 = (bf16[2,8,16,256]{3,2,1,0:T(8,128)(2,1)S(1)}, bf16[2,8,16,256]{3,2,1,0:T(8,128)(2,1)S(1)}, u32[]{:S(2)}, u32[]{:S(2)}) collective-permute-start(bf16[2,8,16,256]{3,2,1,0:T(8,128)(2,1)S(1)} %get-tuple-element.78), channel_id=1, source_target_pairs={{0,20},{4,16},{8,28},{12,24},{16,4},{20,0},{24,12},{28,8},{1,21},{... | collective-permute-start | bytes 393224 | tf_op jit(solution)/shard_map/ppermute | solution.py:35
  43.6 12.6 %collective-permute-start.31 = (bf16[2,8,16,256]{3,2,1,0:T(8,128)(2,1)S(1)}, bf16[2,8,16,256]{3,2,1,0:T(8,128)(2,1)S(1)}, u32[]{:S(2)}, u32[]{:S(2)}) collective-permute-start(bf16[2,8,16,256]{3,2,1,0:T(8,128)(2,1)S(1)} %get-tuple-element.79), channel_id=1, source_target_pairs={{0,24},{4,28},{8,16},{12,20},{16,8},{20,12},{24,0},{28,4},{1,25},{... | collective-permute-start | bytes 393224 | tf_op jit(solution)/shard_map/ppermute | solution.py:35
  45.8 11.8 %collective-permute-start.32 = (bf16[2,8,16,256]{3,2,1,0:T(8,128)(2,1)S(1)}, bf16[2,8,16,256]{3,2,1,0:T(8,128)(2,1)S(1)}, u32[]{:S(2)}, u32[]{:S(2)}) collective-permute-start(bf16[2,8,16,256]{3,2,1,0:T(8,128)(2,1)S(1)} %get-tuple-element.80), channel_id=1, source_target_pairs={{0,28},{4,24},{8,20},{12,16},{16,12},{20,8},{24,4},{28,0},{1,29},{... | collective-permute-start | bytes 393224 | tf_op jit(solution)/shard_map/ppermute | solution.py:35
  47.4 10.2 %collective-permute-start.5 = (bf16[2,8,16,256]{3,2,1,0:T(8,128)(2,1)S(1)}, bf16[2,8,16,256]{3,2,1,0:T(8,128)(2,1)S(1)}, u32[]{:S(2)}, u32[]{:S(2)}) collective-permute-start(bf16[2,8,16,256]{3,2,1,0:T(8,128)(2,1)S(1)} %get-tuple-element.50), channel_id=1, source_target_pairs={{0,4},{4,0},{8,12},{12,8},{16,20},{20,16},{24,28},{28,24},{1,5},{5... | collective-permute-start | bytes 393224 | tf_op jit(solution)/shard_map/ppermute | solution.py:35
  53.9 6.1 %collective-permute-start.6 = (bf16[2,8,16,256]{3,2,1,0:T(8,128)(2,1)S(1)}, bf16[2,8,16,256]{3,2,1,0:T(8,128)(2,1)S(1)}, u32[]{:S(2)}, u32[]{:S(2)}) collective-permute-start(bf16[2,8,16,256]{3,2,1,0:T(8,128)(2,1)S(1)} %get-tuple-element.51), channel_id=1, source_target_pairs={{0,8},{4,12},{8,0},{12,4},{16,24},{20,28},{24,16},{28,20},{1,9},{5... | collective-permute-start | bytes 393224 | tf_op jit(solution)/shard_map/ppermute | solution.py:35
  54.7 6.6 %collective-permute-start.7 = (bf16[2,8,16,256]{3,2,1,0:T(8,128)(2,1)S(1)}, bf16[2,8,16,256]{3,2,1,0:T(8,128)(2,1)S(1)}, u32[]{:S(2)}, u32[]{:S(2)}) collective-permute-start(bf16[2,8,16,256]{3,2,1,0:T(8,128)(2,1)S(1)} %get-tuple-element.52), channel_id=1, source_target_pairs={{0,12},{4,8},{8,4},{12,0},{16,28},{20,24},{24,20},{28,16},{1,13},{... | collective-permute-start | bytes 393224 | tf_op jit(solution)/shard_map/ppermute | solution.py:35
  56.2 11.8 %collective-permute-start.8 = (bf16[2,8,16,256]{3,2,1,0:T(8,128)(2,1)S(1)}, bf16[2,8,16,256]{3,2,1,0:T(8,128)(2,1)S(1)}, u32[]{:S(2)}, u32[]{:S(2)}) collective-permute-start(bf16[2,8,16,256]{3,2,1,0:T(8,128)(2,1)S(1)} %get-tuple-element.53), channel_id=1, source_target_pairs={{0,16},{4,20},{8,24},{12,28},{16,0},{20,4},{24,8},{28,12},{1,17},{... | collective-permute-start | bytes 393224 | tf_op jit(solution)/shard_map/ppermute | solution.py:35
  57.6 11.6 %collective-permute-start.9 = (bf16[2,8,16,256]{3,2,1,0:T(8,128)(2,1)S(1)}, bf16[2,8,16,256]{3,2,1,0:T(8,128)(2,1)S(1)}, u32[]{:S(2)}, u32[]{:S(2)}) collective-permute-start(bf16[2,8,16,256]{3,2,1,0:T(8,128)(2,1)S(1)} %get-tuple-element.54), channel_id=1, source_target_pairs={{0,20},{4,16},{8,28},{12,24},{16,4},{20,0},{24,12},{28,8},{1,21},{... | collective-permute-start | bytes 393224 | tf_op jit(solution)/shard_map/ppermute | solution.py:35
  57.6 12.0 %collective-permute-start.10 = (bf16[2,8,16,256]{3,2,1,0:T(8,128)(2,1)S(1)}, bf16[2,8,16,256]{3,2,1,0:T(8,128)(2,1)S(1)}, u32[]{:S(2)}, u32[]{:S(2)}) collective-permute-start(bf16[2,8,16,256]{3,2,1,0:T(8,128)(2,1)S(1)} %get-tuple-element.55), channel_id=1, source_target_pairs={{0,24},{4,28},{8,16},{12,20},{16,8},{20,12},{24,0},{28,4},{1,25},{... | collective-permute-start | bytes 393224 | tf_op jit(solution)/shard_map/ppermute | solution.py:35
  60.0 9.6 %collective-permute-start.11 = (bf16[2,8,16,256]{3,2,1,0:T(8,128)(2,1)S(1)}, bf16[2,8,16,256]{3,2,1,0:T(8,128)(2,1)S(1)}, u32[]{:S(2)}, u32[]{:S(2)}) collective-permute-start(bf16[2,8,16,256]{3,2,1,0:T(8,128)(2,1)S(1)} %get-tuple-element.56), channel_id=1, source_target_pairs={{0,28},{4,24},{8,20},{12,16},{16,12},{20,8},{24,4},{28,0},{1,29},{... | collective-permute-start | bytes 393224 | tf_op jit(solution)/shard_map/ppermute | solution.py:35
  61.3 14.3 %collective-permute-start.33 = (bf16[2,2,128,256]{3,2,1,0:T(8,128)(2,1)S(1)}, bf16[2,2,128,256]{3,2,1,0:T(8,128)(2,1)S(1)}, u32[]{:S(2)}, u32[]{:S(2)}) collective-permute-start(bf16[2,2,128,256]{3,2,1,0:T(8,128)(2,1)S(1)} %get-tuple-element.82), channel_id=1, source_target_pairs={{0,1},{1,0},{2,3},{3,2},{4,5},{5,4},{6,7},{7,6},{8,9},{9,8},{10,11... | collective-permute-start | bytes 786440 | tf_op jit(solution)/shard_map/ppermute | solution.py:35
  68.0 19.3 %collective-permute-start.34 = (bf16[2,2,128,256]{3,2,1,0:T(8,128)(2,1)S(1)}, bf16[2,2,128,256]{3,2,1,0:T(8,128)(2,1)S(1)}, u32[]{:S(2)}, u32[]{:S(2)}) collective-permute-start(bf16[2,2,128,256]{3,2,1,0:T(8,128)(2,1)S(1)} %get-tuple-element.83), channel_id=1, source_target_pairs={{0,2},{1,3},{2,0},{3,1},{4,6},{5,7},{6,4},{7,5},{8,10},{9,11},{10,... | collective-permute-start | bytes 786440 | tf_op jit(solution)/shard_map/ppermute | solution.py:35
  69.1 19.2 %collective-permute-start.35 = (bf16[2,2,128,256]{3,2,1,0:T(8,128)(2,1)S(1)}, bf16[2,2,128,256]{3,2,1,0:T(8,128)(2,1)S(1)}, u32[]{:S(2)}, u32[]{:S(2)}) collective-permute-start(bf16[2,2,128,256]{3,2,1,0:T(8,128)(2,1)S(1)} %get-tuple-element.84), channel_id=1, source_target_pairs={{0,3},{1,2},{2,1},{3,0},{4,7},{5,6},{6,5},{7,4},{8,11},{9,10},{10,... | collective-permute-start | bytes 786440 | tf_op jit(solution)/shard_map/ppermute | solution.py:35
  73.5 14.8 %collective-permute-start.12 = (bf16[2,8,16,256]{3,2,1,0:T(8,128)(2,1)S(1)}, bf16[2,8,16,256]{3,2,1,0:T(8,128)(2,1)S(1)}, u32[]{:S(2)}, u32[]{:S(2)}) collective-permute-start(bf16[2,8,16,256]{3,2,1,0:T(8,128)(2,1)S(1)} %get-tuple-element.58), channel_id=1, source_target_pairs={{0,4},{4,0},{8,12},{12,8},{16,20},{20,16},{24,28},{28,24},{1,5},{5... | collective-permute-start | bytes 393224 | tf_op jit(solution)/shard_map/ppermute | solution.py:35
  74.8 14.6 %collective-permute-start.13 = (bf16[2,8,16,256]{3,2,1,0:T(8,128)(2,1)S(1)}, bf16[2,8,16,256]{3,2,1,0:T(8,128)(2,1)S(1)}, u32[]{:S(2)}, u32[]{:S(2)}) collective-permute-start(bf16[2,8,16,256]{3,2,1,0:T(8,128)(2,1)S(1)} %get-tuple-element.59), channel_id=1, source_target_pairs={{0,8},{4,12},{8,0},{12,4},{16,24},{20,28},{24,16},{28,20},{1,9},{5... | collective-permute-start | bytes 393224 | tf_op jit(solution)/shard_map/ppermute | solution.py:35
  75.7 18.3 %collective-permute-start.14 = (bf16[2,8,16,256]{3,2,1,0:T(8,128)(2,1)S(1)}, bf16[2,8,16,256]{3,2,1,0:T(8,128)(2,1)S(1)}, u32[]{:S(2)}, u32[]{:S(2)}) collective-permute-start(bf16[2,8,16,256]{3,2,1,0:T(8,128)(2,1)S(1)} %get-tuple-element.60), channel_id=1, source_target_pairs={{0,12},{4,8},{8,4},{12,0},{16,28},{20,24},{24,20},{28,16},{1,13},{... | collective-permute-start | bytes 393224 | tf_op jit(solution)/shard_map/ppermute | solution.py:35
  87.3 11.6 %collective-permute-start.15 = (bf16[2,8,16,256]{3,2,1,0:T(8,128)(2,1)S(1)}, bf16[2,8,16,256]{3,2,1,0:T(8,128)(2,1)S(1)}, u32[]{:S(2)}, u32[]{:S(2)}) collective-permute-start(bf16[2,8,16,256]{3,2,1,0:T(8,128)(2,1)S(1)} %get-tuple-element.61), channel_id=1, source_target_pairs={{0,16},{4,20},{8,24},{12,28},{16,0},{20,4},{24,8},{28,12},{1,17},{... | collective-permute-start | bytes 393224 | tf_op jit(solution)/shard_map/ppermute | solution.py:35
  88.3 11.3 %collective-permute-start.16 = (bf16[2,8,16,256]{3,2,1,0:T(8,128)(2,1)S(1)}, bf16[2,8,16,256]{3,2,1,0:T(8,128)(2,1)S(1)}, u32[]{:S(2)}, u32[]{:S(2)}) collective-permute-start(bf16[2,8,16,256]{3,2,1,0:T(8,128)(2,1)S(1)} %get-tuple-element.62), channel_id=1, source_target_pairs={{0,20},{4,16},{8,28},{12,24},{16,4},{20,0},{24,12},{28,8},{1,21},{... | collective-permute-start | bytes 393224 | tf_op jit(solution)/shard_map/ppermute | solution.py:35
  88.4 11.3 %collective-permute-start.17 = (bf16[2,8,16,256]{3,2,1,0:T(8,128)(2,1)S(1)}, bf16[2,8,16,256]{3,2,1,0:T(8,128)(2,1)S(1)}, u32[]{:S(2)}, u32[]{:S(2)}) collective-permute-start(bf16[2,8,16,256]{3,2,1,0:T(8,128)(2,1)S(1)} %get-tuple-element.63), channel_id=1, source_target_pairs={{0,24},{4,28},{8,16},{12,20},{16,8},{20,12},{24,0},{28,4},{1,25},{... | collective-permute-start | bytes 393224 | tf_op jit(solution)/shard_map/ppermute | solution.py:35
  89.4 10.3 %collective-permute-start.18 = (bf16[2,8,16,256]{3,2,1,0:T(8,128)(2,1)S(1)}, bf16[2,8,16,256]{3,2,1,0:T(8,128)(2,1)S(1)}, u32[]{:S(2)}, u32[]{:S(2)}) collective-permute-start(bf16[2,8,16,256]{3,2,1,0:T(8,128)(2,1)S(1)} %get-tuple-element.64), channel_id=1, source_target_pairs={{0,28},{4,24},{8,20},{12,16},{16,12},{20,8},{24,4},{28,0},{1,29},{... | collective-permute-start | bytes 393224 | tf_op jit(solution)/shard_map/ppermute | solution.py:35
  (11 other events, 166.3 us)

commit v2 on v1

--- a/solution.py
+++ b/solution.py
@@ -12,10 +12,15 @@
 
 RIM = 16
 LANES = 128
-VMEM_BYTES = 48 * 1024 * 1024
+VMEM_BYTES = 20 * 1024 * 1024
 
 WHOLE = pl.BlockSpec(memory_space=pltpu.VMEM)
+ANYWHERE = pl.BlockSpec(memory_space=pl.ANY)
 SCALARS = pl.BlockSpec(memory_space=pltpu.SMEM)
+
+
+def row_type(rows):
+    return jnp.bfloat16 if rows % 16 == 0 else jnp.float32
 
 
 def row_type(rows):
@@ -41,6 +46,11 @@
     for k in order:
         moved[k] = swap(blocks[k], axis, k)
     return [moved[k] for k in range(len(blocks))]
+
+
+def exchange_both(packed):
+    flat = packed.reshape((-1,) + packed.shape[2:])
+    return lax.all_to_all(flat, ("tm", "freq"), 0, 0, tiled=True).reshape(packed.shape)
 
 
 def smoothing_weights(spectrum_power_sum, square_sum, accum_count, rfi_mask):
@@ -63,16 +73,17 @@
     return smooth_weight
 
 
-def weigh_by_baseline(here, vis, smooth, *outs):
-    me = here[1]
-    for k, out in enumerate(outs):
-        dest = me ^ k
+def weigh_by_both(here, vis, smooth, _, out):
+    n, z_count, _, hb, fs, _ = out.shape
+    for z in range(z_count):
         for c in range(2):
-            for b in range(vis.shape[3]):
-                out[c, b] = (vis[c, dest, 0, b].astype(jnp.float32) * smooth[...]).astype(jnp.bfloat16)
-
-
-def weigh_by_channel(here, vis, smooth, *outs):
+            for b in range(hb):
+                value = (vis[c, z, 0, b].astype(jnp.float32) * smooth[...]).astype(jnp.bfloat16)
+                for t in range(n):
+                    out[t, z, c, b] = value[t * fs : (t + 1) * fs]
+
+
+def weigh_by_channel(here, vis, smooth, _, *outs):
     me = here[0]
     fs = vis.shape[4] // len(outs)
     for k, out in enumerate(outs):
@@ -84,7 +95,7 @@
                     out[c, z * vis.shape[3] + b] = (vis[c, z, 0, b, rows, :].astype(jnp.float32) * part).astype(jnp.bfloat16)
 
 
-def weigh(kernel, here, vis, smooth, half, shapes):
+def weigh(kernel, here, after, vis, smooth, half, shapes):
     parts, z, _, hb, fl, length = vis.shape
     block = pl.BlockSpec((parts, z, 1, hb, fl, length), lambda i: (0, 0, half, 0, 0, 0))
     fixed = pl.BlockSpec((fl, length), lambda i: (0, 0))
@@ -93,48 +104,11 @@
         kernel,
         grid=(1,),
         out_shape=outs,
-        in_specs=[SCALARS, block, fixed],
-        out_specs=[pl.BlockSpec(s, lambda i: (0, 0, 0, 0)) for s in shapes],
+        in_specs=[SCALARS, block, fixed, ANYWHERE],
+        out_specs=[pl.BlockSpec(s, lambda i, dims=len(s): (0,) * dims) for s in shapes],
         compiler_params=params(),
         cost_estimate=cost(0, outs + outs),
-    )(here, vis, smooth)
-
-
-def channels_to_baselines(here, *refs, z_count):
-    n = len(refs) - z_count
-    ins, outs = refs[:n], refs[n:]
-    fs, hb = ins[0].shape[2], outs[0].shape[1]
-    for kz, out in enumerate(outs):
-        dest = here[1] ^ kz
-        for k, block in enumerate(ins):
-            rows = pl.ds(pl.multiple_of((here[0] ^ k) * fs, fs), fs)
-            for c in range(2):
-                for b in range(hb):
-                    out[c, b, rows, :] = block[c, dest * hb + b]
-
-
-def baselines_to_channels(here, *refs, z_count):
-    ins, outs = refs[:z_count], refs[z_count:]
-    fs, hb = outs[0].shape[2], ins[0].shape[1]
-    for k, out in enumerate(outs):
-        rows = pl.ds(pl.multiple_of((here[0] ^ k) * fs, fs), fs)
-        for kz, block in enumerate(ins):
-            source = here[1] ^ kz
-            for c in range(2):
-                for b in range(hb):
-                    out[c, source * hb + b] = block[c, b, rows, :]
-
-
-def repack(kernel, here, blocks, shapes, z_count):
-    outs = [jax.ShapeDtypeStruct(s, jnp.bfloat16) for s in shapes]
-    return pl.pallas_call(
-        functools.partial(kernel, z_count=z_count),
-        out_shape=outs,
-        in_specs=[SCALARS] + [WHOLE] * len(blocks),
-        out_specs=[WHOLE] * len(outs),
-        compiler_params=params(),
-        cost_estimate=cost(0, list(blocks) + outs),
-    )(here, *blocks)
+    )(here, vis, smooth, after)
 
 
 def transform_tables(n, length):
@@ -201,19 +175,26 @@
     return values
 
 
-def transform(here, order, high, low, twiddle, *refs, n):
-    ins, outs = refs[:n], refs[n : 2 * n]
-    ordered, lined, stage, done = refs[2 * n :]
+def transform(here, _, order, high, low, twiddle, *refs, n, first):
+    blocks, packed = (refs[:n], refs[n]) if first else (refs[1 : n + 1], refs[0])
+    ordered, lined, stage, done = refs[n + 1 :]
     me = here[0]
-    parts, planes, fs, length = ins[0].shape
+    _, z_count, parts, hb, fs, length = packed.shape
+    planes = z_count * hb
     group, cols = length // n, length // LANES
     per = lined.shape[1] // fs
+    zs = per // hb
 
     def step(i, carry):
         for c in range(parts):
             for k in range(n):
-                block = ins[k][c, pl.ds(i * per, per)].reshape(per * fs, length)
-                ordered[me ^ k] = jnp.dot(block, order[...], preferred_element_type=jnp.float32)
+                if first:
+                    block = blocks[k][c, pl.ds(i * per, per)].reshape(per * fs, length)
+                    target = me ^ k
+                else:
+                    block = packed[k, pl.ds(i * zs, zs), c].reshape(per * fs, length)
+                    target = k
+                ordered[target] = jnp.dot(block, order[...], preferred_element_type=jnp.float32)
             for r in range(0, per * fs, 16):
                 values = [[ordered[p, r : r + 16, q * LANES : (q + 1) * LANES] for q in range(cols)] for p in range(n)]
                 for v, columns in enumerate(transpose_groups(values, group)):
@@ -225,35 +206,38 @@
         stage[...] = total.reshape(n, per * fs, 2 * length)
         for r in range(0, per * fs, 16):
             for q in range(cols):
-                first, second = slice(q * LANES, (q + 1) * LANES), slice(length + q * LANES, length + (q + 1) * LANES)
+                left, right = slice(q * LANES, (q + 1) * LANES), slice(length + q * LANES, length + (q + 1) * LANES)
                 turned = []
                 for v in range(n):
-                    real, imag = stage[v, r : r + 16, first], stage[v, r : r + 16, second]
-                    c, s = twiddle[0, v : v + 1, first], twiddle[1, v : v + 1, first]
+                    real, imag = stage[v, r : r + 16, left], stage[v, r : r + 16, right]
+                    c, s = twiddle[0, v : v + 1, left], twiddle[1, v : v + 1, left]
                     turned.append((real * c + imag * s, imag * c - real * s))
                 for m, pair in enumerate(short_dft(turned)):
                     for c in range(2):
-                        done[m, c, r : r + 16, first] = pair[c].astype(jnp.bfloat16)
+                        done[m, c, r : r + 16, left] = pair[c].astype(jnp.bfloat16)
         for k in range(n):
             for c in range(2):
-                outs[k][c, pl.ds(i * per, per)] = done[me ^ k, c].reshape(per, fs, length)
+                if first:
+                    packed[k, pl.ds(i * zs, zs), c] = done[k, c].reshape(zs, hb, fs, length)
+                else:
+                    blocks[k][c, pl.ds(i * per, per)] = done[me ^ k, c].reshape(per, fs, length)
         return carry
 
     lax.fori_loop(0, planes // per, step, 0)
 
 
-def transform_call(here, blocks):
-    n = len(blocks)
-    parts, planes, fs, length = blocks[0].shape
+def transform_call(here, after, blocks, out_shapes, first):
+    n, z_count, parts, hb, fs, length = out_shapes[0] if first else blocks[0].shape
+    planes = z_count * hb
     per = math.gcd(planes, 4)
     rows = per * fs
     tables = transform_tables(n, length)
-    outs = [jax.ShapeDtypeStruct(b.shape, jnp.bfloat16) for b in blocks]
+    outs = [jax.ShapeDtypeStruct(s, jnp.bfloat16) for s in out_shapes]
     return pl.pallas_call(
-        functools.partial(transform, n=n),
+        functools.partial(transform, n=n, first=first),
         out_shape=outs,
-        in_specs=[SCALARS] + [WHOLE] * (4 + n),
-        out_specs=[WHOLE] * n,
+        in_specs=[SCALARS, ANYWHERE] + [WHOLE] * (4 + len(blocks)),
+        out_specs=[WHOLE] * len(outs),
         scratch_shapes=[
             pltpu.VMEM((n, rows, length), jnp.float32),
             pltpu.VMEM((n, rows, 2 * length), jnp.bfloat16),
@@ -262,19 +246,20 @@
         ],
         compiler_params=params(),
         cost_estimate=cost(4 * n * planes * fs * (2 * length) ** 2, list(blocks) + outs),
-    )(here, *[jnp.asarray(t) for t in tables], *blocks)
-
-
-def filter_kernel(classes, here, bank, *refs, count, from_baselines, aliased):
+    )(here, after, *[jnp.asarray(t) for t in tables], *blocks)
+
+
+def filter_kernel(classes, here, bank, *refs, count, packed, aliased):
     ins, out, lined = refs[:count], refs[count + aliased], refs[-1]
     b = pl.program_id(0)
     length = out.shape[-1]
-    if from_baselines:
-        fl = ins[0].shape[2]
-        for kz, block in enumerate(ins):
-            rows = pl.ds(pl.multiple_of((here[1] ^ kz) * fl, fl), fl)
-            for c in range(2):
-                lined[rows, c * length : (c + 1) * length] = block[c, b].astype(lined.dtype)
+    if packed:
+        n, z_count, _, _, fs, _ = ins[0].shape
+        for t in range(n):
+            for z in range(z_count):
+                rows = slice((z * n + t) * fs, (z * n + t + 1) * fs)
+                for c in range(2):
+                    lined[rows, c * length : (c + 1) * length] = ins[0][t, z, c, b].astype(lined.dtype)
     else:
         hb, fs = pl.num_programs(0), ins[0].shape[2]
         fl = fs * count
@@ -288,10 +273,10 @@
         out[c, 0] = total[:, c * length : (c + 1) * length].astype(jnp.bfloat16)
 
 
-def delay_filter(classes, here, bank, blocks, half, hb, out_shape, before, from_baselines):
+def delay_filter(classes, here, bank, blocks, half, hb, out_shape, before, packed):
     _, channels, _ = bank.shape
     length = out_shape[-1]
-    fixed = [pl.BlockSpec(b.shape, lambda i, classes, here: (0, 0, 0, 0)) for b in blocks]
+    fixed = [pl.BlockSpec(b.shape, lambda i, classes, here, dims=len(b.shape): (0,) * dims) for b in blocks]
     specs = [pl.BlockSpec((1, channels, channels), lambda i, classes, here: (classes[half * hb + i], 0, 0))] + fixed
     operands = [bank] + list(blocks)
     aliases = {}
@@ -302,7 +287,7 @@
     out = jax.ShapeDtypeStruct(out_shape, jnp.bfloat16)
     return pl.pallas_call(
         functools.partial(
-            filter_kernel, count=len(blocks), from_baselines=from_baselines, aliased=int(before is not None)
+            filter_kernel, count=len(blocks), packed=packed, aliased=int(before is not None)
         ),
         out_shape=out,
         grid_spec=pltpu.PrefetchScalarGridSpec(
@@ -335,21 +320,18 @@
     smooth = smoothing_weights(spectrum_power_sum, square_sum, accum_count, rfi_mask)
     vis = visibility.reshape(parts, z_count, 2, hb, fl, length)
     by_channel = [(parts, z_count * hb, fs, length)] * n
-    by_baseline = [(parts, hb, fl, length)] * z_count
+    by_both = [(n, z_count, parts, hb, fs, length)]
     out_shape = (parts, 2 * hb, fl * z_count, length)
 
-    late = weigh(weigh_by_baseline, here, vis, smooth, 1, by_baseline)
-    late = exchange(late, "freq")
-    early = weigh(weigh_by_channel, here, vis, smooth, 0, by_channel)
-    early = transform_call(here, exchange(early, "tm"))
-    early = repack(channels_to_baselines, here, exchange(early, "tm"), by_baseline, z_count)
-    early = exchange(early, "freq")
-
-    late = repack(baselines_to_channels, here, late, by_channel, z_count)
-    late = transform_call(here, exchange(late, "tm"))
-    late = exchange(late, "tm")
-    filtered = delay_filter(classes, here, filter_bank, early, 0, hb, out_shape, None, True)
-    return delay_filter(classes, here, filter_bank, late, 1, hb, out_shape, filtered, False)
+    (late_out,) = weigh(weigh_by_both, here, smooth, vis, smooth, 1, by_both)
+    late = exchange_both(late_out)
+    early_out = weigh(weigh_by_channel, here, late_out, vis, smooth, 0, by_channel)
+    early_out = transform_call(here, early_out[0], exchange(early_out, "tm"), by_both, True)
+    early = exchange_both(early_out[0])
+    late_out = transform_call(here, early_out[0], [late], by_channel, False)
+    late = exchange(late_out, "tm")
+    filtered = delay_filter(classes, here, filter_bank, late, 1, hb, out_shape, None, False)
+    return delay_filter(classes, here, filter_bank, [early], 0, hb, out_shape, filtered, True)
 
 
 def solution(mesh):

time: 103 us -> 87.5 us (0.85)
  waiting for transfers between devices: 43.3 us -> 33.2 us
  starting transfers between devices: 38.7 us -> 28.9 us
  local copies, waits for them, and re-layouts: 1.69 us -> 6.13 us
    ppermute x34 -> x14, starting transfers between devices: 35.3 us -> 14.1 us  [swap(): return lax.ppermute(value, axis, [(i, i ^ k) for i in range(size)])]
    all_to_all x0 -> x2, starting transfers between devices: none -> 11.4 us  [exchange_both(): lax.all_to_all(flat, ('tm', 'freq'), 0, 0, tiled=True).reshape(packed.shape)]
    ppermute x34 -> x14, waiting for transfers between devices: 41.5 us -> 31.4 us  [swap(): return lax.ppermute(value, axis, [(i, i ^ k) for i in range(size)])]
    unnamed x14 -> x24, local copies, waits for them, and re-layouts: 1.61 us -> 6.05 us
    pallas_call x6 -> x4, Pallas kernels: 13.8 us -> 13.4 us  [the longest x2 8.76 us: transform_call(): pl.pallas_call(functools.partial(transform, n=n, first=first), out_shape=...]
  transfers between devices with their start and end apart: 36 -> 18, of which waited for: 14 -> 11; matrix products, arithmetic and copies ran while one was open for 0% -> 0% of each run, Pallas kernels for 12% -> 14%
where the time goes in v2:
time: 87.5 us; the launch traced here: 87.1 us
  waiting for transfers between devices  33.2 us (38%)
  starting transfers between devices  28.9 us (33%)
  Pallas kernels  15.8 us (18%)
  local copies, waits for them, and re-layouts  6.13 us (7%)
  other arithmetic  2.92 us (3%)
    ppermute x14, waiting for transfers between devices, swap(): return lax.ppermute(value, axis, [(i, i ^ k) for i in range(size)])  31.4 us
    ppermute x14, starting transfers between devices, swap(): return lax.ppermute(value, axis, [(i, i ^ k) for i in range(size)])  14.1 us
    all_to_all x2, starting transfers between devices, exchange_both(): lax.all_to_all(flat, ('tm', 'freq'), 0, 0, tiled=True).reshape(packed.shape)  11.4 us
    pallas_call x2, Pallas kernels, transform_call(): pl.pallas_call(functools.partial(transform, n=n, first=first), out_shape=...  8.76 us
    unnamed x24, local copies, waits for them, and re-layouts  6.05 us
    pallas_call x2, Pallas kernels, delay_filter(): pl.pallas_call(functools.partial(filter_kernel, count=len(blocks), packed...  4.61 us
    ppermute x1, starting transfers between devices, smoothing_weights(): after = lax.ppermute(flag_weight[:, :RIM], 'tm', [(j, i) for i, j in up])  2.95 us
    pallas_call x2, Pallas kernels, weigh(): pl.pallas_call(kernel, grid=(1,), out_shape=outs, in_specs=[SCALARS, bloc...  2.4 us
  transfers between devices with their start and end apart: 18, of which 11 were waited for; matrix products, arithmetic and copies ran while one was open for 0% of the time, Pallas kernels for 14%

profile of v2, /device:TPU:0, one launch (start us, length us, event | category | flops | bytes accessed | tf_op | source)
XLA Modules:
  0.0 87.1 jit_solution(12937080886360204229)
XLA Ops:
  0.0 1.2 %exponential_multiply_fusion = f32[128,256]{1,0:T(8,128)S(1)} fusion(f32[128,256]{1,0:T(8,128)} %param.16, f32[128,256]{1,0:T(8,128)} %param.17, s32[128,256]{1,0:T(8,128)} %param.18, s32[128,256]{1,0:T(8,128)} %param.19), kind=kLoop, calls=%fused_computation.156 | loop fusion | flops 458752 | bytes 655360 | tf_op jit(solution)/shard_map/mul | solution.py:63
  1.7 2.9 %collective-permute-start.1 = (f32[128,16]{1,0:T(8,128)S(1)}, f32[128,16]{1,0:T(8,128)S(1)}, u32[]{:S(2)}, u32[]{:S(2)}) collective-permute-start(f32[128,16]{1,0:T(8,128)S(1)} %get-tuple-element.38), channel_id=1, source_target_pairs={{4,0},{8,4},{12,8},{16,12},{20,16},{24,20},{28,24},{0,28},{5,1},{9... | collective-permute-start | bytes 24584 | tf_op jit(solution)/shard_map/ppermute | solution.py:67
  4.8 1.8 %collective-permute-done = f32[128,16]{1,0:T(8,128)S(1)} collective-permute-done((f32[128,16]{1,0:T(8,128)S(1)}, f32[128,16]{1,0:T(8,128)S(1)}, u32[]{:S(2)}, u32[]{:S(2)}) %collective-permute-start) | collective-permute-done | bytes 8224 | tf_op jit(solution)/shard_map/ppermute | solution.py:66
  6.6 1.7 %fusion.3.smooth._ = f32[128,256]{1,0:T(8,128)S(1)} fusion(f32[128,256]{1,0:T(8,128)S(1)} %exponential_multiply_fusion, f32[128,16]{1,0:T(8,128)S(1)} %collective-permute-done.1, f32[128,16]{1,0:T(8,128)S(1)} %collective-permute-done), kind=kLoop, calls=%fused_computation.63 | loop fusion | flops 3178496 | bytes 278528 | tf_op jit(solution)/shard_map/add | solution.py:72
  8.3 1.6 %copy-done = bf16[2,16,128,256]{3,2,1,0:T(8,128)(2,1)S(1)} copy-done((bf16[2,16,128,256]{3,2,1,0:T(8,128)(2,1)S(1)}, bf16[2,16,128,256]{3,2,1,0:T(8,128)(2,1)}, u32[]{:S(2)}) %copy-start) | copy-done | bytes 2097176
  9.9 1.7 %shard_map.145._ = bf16[8,4,2,2,16,256]{5,4,3,2,1,0:T(8,128)(2,1)} custom-call(s32[2]{0:T(128)S(1)} %pad_add_fusion.here, bf16[2,4,2,2,128,256]{5,4,3,2,1,0:T(8,128)(2,1)S(1)} %bitcast.8, f32[128,256]{1,0:T(8,128)S(1)} %fusion.3.smooth._, f32[128,256]{1,0:T(8,128)S(1)} %fusion.3.smooth._), custom_call_target="tpu_custom_call" | custom-call | bytes 2097152 | tf_op jit(solution)/shard_map/pallas_call | solution.py:103
  11.5 6.8 %all-to-all-start.1 = ((bf16[32,2,2,16,256]{4,3,2,1,0:T(8,128)(2,1)}), bf16[32,2,2,16,256]{4,3,2,1,0:T(8,128)(2,1)S(1)}, u32[]{:S(2)}, u32[]{:S(2)}) async-start(bf16[32,2,2,16,256]{4,3,2,1,0:T(8,128)(2,1)} %bitcast.6), calls=%async_computation.1 | async-start | bytes 2097152 | tf_op jit(solution)/shard_map/all_to_all | solution.py:53
  19.5 1.7 %collective-permute-start.3 = (bf16[2,8,16,256]{3,2,1,0:T(8,128)(2,1)S(1)}, bf16[2,8,16,256]{3,2,1,0:T(8,128)(2,1)S(1)}, u32[]{:S(2)}, u32[]{:S(2)}) collective-permute-start(bf16[2,8,16,256]{3,2,1,0:T(8,128)(2,1)S(1)} %get-tuple-element.23), channel_id=1, source_target_pairs={{0,8},{4,12},{8,0},{12,4},{16,24},{20,28},{24,16},{28,20},{1,9},{5... | collective-permute-start | bytes 393224 | tf_op jit(solution)/shard_map/ppermute | solution.py:40
  21.2 1.7 %collective-permute-start.5 = (bf16[2,8,16,256]{3,2,1,0:T(8,128)(2,1)S(1)}, bf16[2,8,16,256]{3,2,1,0:T(8,128)(2,1)S(1)}, u32[]{:S(2)}, u32[]{:S(2)}) collective-permute-start(bf16[2,8,16,256]{3,2,1,0:T(8,128)(2,1)S(1)} %get-tuple-element.25), channel_id=1, source_target_pairs={{0,16},{4,20},{8,24},{12,28},{16,0},{20,4},{24,8},{28,12},{1,17},{... | collective-permute-start | bytes 393224 | tf_op jit(solution)/shard_map/ppermute | solution.py:40
  23.0 2.6 %collective-permute-start.7 = (bf16[2,8,16,256]{3,2,1,0:T(8,128)(2,1)S(1)}, bf16[2,8,16,256]{3,2,1,0:T(8,128)(2,1)S(1)}, u32[]{:S(2)}, u32[]{:S(2)}) collective-permute-start(bf16[2,8,16,256]{3,2,1,0:T(8,128)(2,1)S(1)} %get-tuple-element.27), channel_id=1, source_target_pairs={{0,24},{4,28},{8,16},{12,20},{16,8},{20,12},{24,0},{28,4},{1,25},{... | collective-permute-start | bytes 393224 | tf_op jit(solution)/shard_map/ppermute | solution.py:40
  25.6 6.3 %collective-permute-done.3.refs_2_ = bf16[2,8,16,256]{3,2,1,0:T(8,128)(2,1)S(1)} collective-permute-done((bf16[2,8,16,256]{3,2,1,0:T(8,128)(2,1)S(1)}, bf16[2,8,16,256]{3,2,1,0:T(8,128)(2,1)S(1)}, u32[]{:S(2)}, u32[]{:S(2)}) %collective-permute-start.3) | collective-permute-done | bytes 131104 | tf_op jit(solution)/shard_map/ppermute | solution.py:40
  32.0 2.6 %collective-permute-done.4.refs_3_ = bf16[2,8,16,256]{3,2,1,0:T(8,128)(2,1)S(1)} collective-permute-done((bf16[2,8,16,256]{3,2,1,0:T(8,128)(2,1)S(1)}, bf16[2,8,16,256]{3,2,1,0:T(8,128)(2,1)S(1)}, u32[]{:S(2)}, u32[]{:S(2)}) %collective-permute-start.4) | collective-permute-done | bytes 131104 | tf_op jit(solution)/shard_map/ppermute | solution.py:40
  35.4 6.2 %collective-permute-done.7.refs_6_ = bf16[2,8,16,256]{3,2,1,0:T(8,128)(2,1)S(1)} collective-permute-done((bf16[2,8,16,256]{3,2,1,0:T(8,128)(2,1)S(1)}, bf16[2,8,16,256]{3,2,1,0:T(8,128)(2,1)S(1)}, u32[]{:S(2)}, u32[]{:S(2)}) %collective-permute-start.7) | collective-permute-done | bytes 131104 | tf_op jit(solution)/shard_map/ppermute | solution.py:40
  41.6 2.6 %collective-permute-done.8.refs_7_ = bf16[2,8,16,256]{3,2,1,0:T(8,128)(2,1)S(1)} collective-permute-done((bf16[2,8,16,256]{3,2,1,0:T(8,128)(2,1)S(1)}, bf16[2,8,16,256]{3,2,1,0:T(8,128)(2,1)S(1)}, u32[]{:S(2)}, u32[]{:S(2)}) %collective-permute-start.8) | collective-permute-done | bytes 131104 | tf_op jit(solution)/shard_map/ppermute | solution.py:40
  44.2 5.0 %shard_map.147._ = bf16[8,4,2,2,16,256]{5,4,3,2,1,0:T(8,128)(2,1)} custom-call(s32[2]{0:T(128)S(1)} %pad_add_fusion.here, bf16[2,8,16,256]{3,2,1,0:T(8,128)(2,1)S(1)} %get-tuple-element.21._.refs_0_, bf16[256,256]{1,0:T(8,128)(2,1)S(1)} %copy-done.10, bf16[512,512]{1,0:T(8,128)(2,1)S(1)} %copy-done.8, bf16[512,512]{1,0:T(8,128)(2,1)S(1)} %copy-done.6, ...), custom_call_target="tpu_custom_call" | custom-call | flops 1073741824 | bytes 2097152 | tf_op jit(solution)/shard_map/pallas_call | solution.py:236
  49.1 1.0 %copy-done.3 = bf16[32,2,2,16,256]{4,3,2,1,0:T(8,128)(2,1)} copy-done((bf16[32,2,2,16,256]{4,3,2,1,0:T(8,128)(2,1)}, bf16[32,2,2,16,256]{4,3,2,1,0:T(8,128)(2,1)S(1)}, u32[]{:S(2)}) %copy-start.3) | copy-done | bytes 1048600
  50.1 4.5 %all-to-all-start = ((bf16[32,2,2,16,256]{4,3,2,1,0:T(8,128)(2,1)}), bf16[32,2,2,16,256]{4,3,2,1,0:T(8,128)(2,1)S(1)}, u32[]{:S(2)}, u32[]{:S(2)}) async-start(bf16[32,2,2,16,256]{4,3,2,1,0:T(8,128)(2,1)} %bitcast.4), calls=%async_computation | async-start | bytes 2097152 | tf_op jit(solution)/shard_map/all_to_all | solution.py:53
  54.7 1.4 %copy-done.4 = bf16[32,2,2,16,256]{4,3,2,1,0:T(8,128)(2,1)S(1)} copy-done((bf16[32,2,2,16,256]{4,3,2,1,0:T(8,128)(2,1)S(1)}, bf16[32,2,2,16,256]{4,3,2,1,0:T(8,128)(2,1)}, u32[]{:S(2)}) %copy-start.4) | copy-done | bytes 1048600
  56.0 1.0 %copy-done.7 = bf16[512,512]{1,0:T(8,128)(2,1)S(1)} copy-done((bf16[512,512]{1,0:T(8,128)(2,1)S(1)}, bf16[512,512]{1,0:T(8,128)(2,1)}, u32[]{:S(2)}) %copy-start.7) | copy-done | bytes 524312
  57.1 1.0 %copy-done.9 = bf16[512,512]{1,0:T(8,128)(2,1)S(1)} copy-done((bf16[512,512]{1,0:T(8,128)(2,1)S(1)}, bf16[512,512]{1,0:T(8,128)(2,1)}, u32[]{:S(2)}) %copy-start.9) | copy-done | bytes 524312
  58.1 3.8 %shard_map.148 = (bf16[2,8,16,256]{3,2,1,0:T(8,128)(2,1)S(1)}, bf16[2,8,16,256]{3,2,1,0:T(8,128)(2,1)S(1)}, bf16[2,8,16,256]{3,2,1,0:T(8,128)(2,1)S(1)}, bf16[2,...) custom-call(s32[2]{0:T(128)S(1)} %pad_add_fusion.here, ...), custom_call_target="tpu_custom_call" | custom-call | flops 1073741824 | bytes 2097152 | tf_op jit(solution)/shard_map/pallas_call | solution.py:236
  62.3 1.7 %collective-permute-start.10 = (bf16[2,8,16,256]{3,2,1,0:T(8,128)(2,1)S(1)}, bf16[2,8,16,256]{3,2,1,0:T(8,128)(2,1)S(1)}, u32[]{:S(2)}, u32[]{:S(2)}) collective-permute-start(bf16[2,8,16,256]{3,2,1,0:T(8,128)(2,1)S(1)} %get-tuple-element.31), channel_id=1, source_target_pairs={{0,8},{4,12},{8,0},{12,4},{16,24},{20,28},{24,16},{28,20},{1,9},{5... | collective-permute-start | bytes 393224 | tf_op jit(solution)/shard_map/ppermute | solution.py:40
  63.9 1.7 %collective-permute-start.12 = (bf16[2,8,16,256]{3,2,1,0:T(8,128)(2,1)S(1)}, bf16[2,8,16,256]{3,2,1,0:T(8,128)(2,1)S(1)}, u32[]{:S(2)}, u32[]{:S(2)}) collective-permute-start(bf16[2,8,16,256]{3,2,1,0:T(8,128)(2,1)S(1)} %get-tuple-element.33), channel_id=1, source_target_pairs={{0,16},{4,20},{8,24},{12,28},{16,0},{20,4},{24,8},{28,12},{1,17},{... | collective-permute-start | bytes 393224 | tf_op jit(solution)/shard_map/ppermute | solution.py:40
  65.8 2.6 %collective-permute-start.14 = (bf16[2,8,16,256]{3,2,1,0:T(8,128)(2,1)S(1)}, bf16[2,8,16,256]{3,2,1,0:T(8,128)(2,1)S(1)}, u32[]{:S(2)}, u32[]{:S(2)}) collective-permute-start(bf16[2,8,16,256]{3,2,1,0:T(8,128)(2,1)S(1)} %get-tuple-element.35), channel_id=1, source_target_pairs={{0,24},{4,28},{8,16},{12,20},{16,8},{20,12},{24,0},{28,4},{1,25},{... | collective-permute-start | bytes 393224 | tf_op jit(solution)/shard_map/ppermute | solution.py:40
  68.3 2.2 %collective-permute-done.10.refs_2_ = bf16[2,8,16,256]{3,2,1,0:T(8,128)(2,1)S(1)} collective-permute-done((bf16[2,8,16,256]{3,2,1,0:T(8,128)(2,1)S(1)}, bf16[2,8,16,256]{3,2,1,0:T(8,128)(2,1)S(1)}, u32[]{:S(2)}, u32[]{:S(2)}) %collective-permute-start.10) | collective-permute-done | bytes 131104 | tf_op jit(solution)/shard_map/ppermute | solution.py:40
  70.6 1.2 %collective-permute-start.15 = (bf16[2,8,16,256]{3,2,1,0:T(8,128)(2,1)S(1)}, bf16[2,8,16,256]{3,2,1,0:T(8,128)(2,1)S(1)}, u32[]{:S(2)}, u32[]{:S(2)}) collective-permute-start(bf16[2,8,16,256]{3,2,1,0:T(8,128)(2,1)S(1)} %get-tuple-element.36), channel_id=1, source_target_pairs={{0,28},{4,24},{8,20},{12,16},{16,12},{20,8},{24,4},{28,0},{1,29},{... | collective-permute-start | bytes 393224 | tf_op jit(solution)/shard_map/ppermute | solution.py:40
  71.8 1.8 %collective-permute-done.11.refs_3_ = bf16[2,8,16,256]{3,2,1,0:T(8,128)(2,1)S(1)} collective-permute-done((bf16[2,8,16,256]{3,2,1,0:T(8,128)(2,1)S(1)}, bf16[2,8,16,256]{3,2,1,0:T(8,128)(2,1)S(1)}, u32[]{:S(2)}, u32[]{:S(2)}) %collective-permute-start.11) | collective-permute-done | bytes 131104 | tf_op jit(solution)/shard_map/ppermute | solution.py:40
  73.6 1.6 %collective-permute-done.13.refs_5_ = bf16[2,8,16,256]{3,2,1,0:T(8,128)(2,1)S(1)} collective-permute-done((bf16[2,8,16,256]{3,2,1,0:T(8,128)(2,1)S(1)}, bf16[2,8,16,256]{3,2,1,0:T(8,128)(2,1)S(1)}, u32[]{:S(2)}, u32[]{:S(2)}) %collective-permute-start.13) | collective-permute-done | bytes 131104 | tf_op jit(solution)/shard_map/ppermute | solution.py:40
  75.2 4.2 %collective-permute-done.14.refs_6_ = bf16[2,8,16,256]{3,2,1,0:T(8,128)(2,1)S(1)} collective-permute-done((bf16[2,8,16,256]{3,2,1,0:T(8,128)(2,1)S(1)}, bf16[2,8,16,256]{3,2,1,0:T(8,128)(2,1)S(1)}, u32[]{:S(2)}, u32[]{:S(2)}) %collective-permute-start.14) | collective-permute-done | bytes 131104 | tf_op jit(solution)/shard_map/ppermute | solution.py:40
  79.4 3.1 %collective-permute-done.15.refs_7_ = bf16[2,8,16,256]{3,2,1,0:T(8,128)(2,1)S(1)} collective-permute-done((bf16[2,8,16,256]{3,2,1,0:T(8,128)(2,1)S(1)}, bf16[2,8,16,256]{3,2,1,0:T(8,128)(2,1)S(1)}, u32[]{:S(2)}, u32[]{:S(2)}) %collective-permute-start.15) | collective-permute-done | bytes 131104 | tf_op jit(solution)/shard_map/ppermute | solution.py:40
  82.5 2.4 %shard_map.149.refs_1_ = bf16[2,4,512,256]{3,2,1,0:T(8,128)(2,1)} custom-call(s32[4]{0:T(128)S(1)} %bitcast.12, s32[2]{0:T(128)S(1)} %pad_add_fusion.here, bf16[4,512,512]{2,1,0:T(8,128)(2,1)S(1)} %copy-done.2, bf16[2,8,16,256]{3,2,1,0:T(8,128)(2,1)S(1)} %get-tuple-element.29.refs_0_, bf16[2,8,16,256]{3,2,1,0:T(8,128)(2,1)S(1)} %collective-permute-done.9.refs_1_, ...), custom_call_target="tpu_custom_call" | custom-call | flops 536870912 | bytes 3145728 | tf_op jit(solution)/shard_map/pallas_call | solution.py:288
  84.9 2.3 %shard_map.150 = bf16[2,4,512,256]{3,2,1,0:T(8,128)(2,1)} custom-call(s32[4]{0:T(128)S(1)} %bitcast.13, s32[2]{0:T(128)S(1)} %pad_add_fusion.here, bf16[4,512,512]{2,1,0:T(8,128)(2,1)S(1)} %copy-done.2, bf16[8,4,2,2,16,256]{5,4,3,2,1,0:T(8,128)(2,1)S(1)} %bitcast.10, bf16[2,4,512,256]{3,2,1,0:T(8,128)(2,1)} %shard_map.149.refs_1_), custom_call_target="tpu_custom_call", output_to_operand_aliasing={{}: (4, {})} | custom-call | flops 536870912 | bytes 3145728 | tf_op jit(solution)/shard_map/pallas_call | solution.py:288
  (38 shorter events, 3.2 us)
Async XLA Ops:
  1.3 5.3 %collective-permute-start = (f32[128,16]{1,0:T(8,128)S(1)}, f32[128,16]{1,0:T(8,128)S(1)}, u32[]{:S(2)}, u32[]{:S(2)}) collective-permute-start(f32[128,16]{1,0:T(8,128)S(1)} %get-tuple-element.37), channel_id=1, source_target_pairs={{0,4},{4,8},{8,12},{12,16},{16,20},{20,24},{24,28},{28,0},{1,5},{5... | collective-permute-start | bytes 24584 | tf_op jit(solution)/shard_map/ppermute | solution.py:66
  1.7 4.9 %collective-permute-start.1 = (f32[128,16]{1,0:T(8,128)S(1)}, f32[128,16]{1,0:T(8,128)S(1)}, u32[]{:S(2)}, u32[]{:S(2)}) collective-permute-start(f32[128,16]{1,0:T(8,128)S(1)} %get-tuple-element.38), channel_id=1, source_target_pairs={{4,0},{8,4},{12,8},{16,12},{20,16},{24,20},{28,24},{0,28},{5,1},{9... | collective-permute-start | bytes 24584 | tf_op jit(solution)/shard_map/ppermute | solution.py:67
  8.3 1.6 %copy-start = (bf16[2,16,128,256]{3,2,1,0:T(8,128)(2,1)S(1)}, bf16[2,16,128,256]{3,2,1,0:T(8,128)(2,1)}, u32[]{:S(2)}) copy-start(bf16[2,16,128,256]{3,2,1,0:T(8,128)(2,1)} %param.15) | copy-start | bytes 6291460
  9.9 8.5 %copy-start.1 = (bf16[2,16,128,256]{3,2,1,0:T(8,128)(2,1)S(1)}, bf16[2,16,128,256]{3,2,1,0:T(8,128)(2,1)}, u32[]{:S(2)}) copy-start(bf16[2,16,128,256]{3,2,1,0:T(8,128)(2,1)} %param.15) | copy-start | bytes 6291460
  11.5 37.6 %all-to-all-start.1 = ((bf16[32,2,2,16,256]{4,3,2,1,0:T(8,128)(2,1)}), bf16[32,2,2,16,256]{4,3,2,1,0:T(8,128)(2,1)S(1)}, u32[]{:S(2)}, u32[]{:S(2)}) async-start(bf16[32,2,2,16,256]{4,3,2,1,0:T(8,128)(2,1)} %bitcast.6), calls=%async_computation.1 | async-start | bytes 2097152 | tf_op jit(solution)/shard_map/all_to_all | solution.py:53
  18.4 25.8 %copy-start.6 = (bf16[512,512]{1,0:T(8,128)(2,1)S(1)}, bf16[512,512]{1,0:T(8,128)(2,1)}, u32[]{:S(2)}) copy-start(bf16[512,512]{1,0:T(8,128)(2,1)} %constant.61.clone.low) | copy-start | bytes 1572868
  18.4 25.7 %copy-start.8 = (bf16[512,512]{1,0:T(8,128)(2,1)S(1)}, bf16[512,512]{1,0:T(8,128)(2,1)}, u32[]{:S(2)}) copy-start(bf16[512,512]{1,0:T(8,128)(2,1)} %constant.60.clone.high) | copy-start | bytes 1572868
  18.4 25.7 %copy-start.10 = (bf16[256,256]{1,0:T(8,128)(2,1)S(1)}, bf16[256,256]{1,0:T(8,128)(2,1)}, u32[]{:S(2)}) copy-start(bf16[256,256]{1,0:T(8,128)(2,1)} %constant.59.clone.order) | copy-start | bytes 393220
  18.4 25.7 %copy-start.11 = (f32[2,8,256]{2,1,0:T(8,128)S(1)}, f32[2,8,256]{2,1,0:T(8,128)}, u32[]{:S(2)}) copy-start(f32[2,8,256]{2,1,0:T(8,128)} %constant.62.clone.twiddle) | copy-start | bytes 49156
  19.2 3.8 %collective-permute-start.2 = (bf16[2,8,16,256]{3,2,1,0:T(8,128)(2,1)S(1)}, bf16[2,8,16,256]{3,2,1,0:T(8,128)(2,1)S(1)}, u32[]{:S(2)}, u32[]{:S(2)}) collective-permute-start(bf16[2,8,16,256]{3,2,1,0:T(8,128)(2,1)S(1)} %get-tuple-element.22), channel_id=1, source_target_pairs={{0,4},{4,0},{8,12},{12,8},{16,20},{20,16},{24,28},{28,24},{1,5},{5... | collective-permute-start | bytes 393224 | tf_op jit(solution)/shard_map/ppermute | solution.py:40
  19.5 12.4 %collective-permute-start.3 = (bf16[2,8,16,256]{3,2,1,0:T(8,128)(2,1)S(1)}, bf16[2,8,16,256]{3,2,1,0:T(8,128)(2,1)S(1)}, u32[]{:S(2)}, u32[]{:S(2)}) collective-permute-start(bf16[2,8,16,256]{3,2,1,0:T(8,128)(2,1)S(1)} %get-tuple-element.23), channel_id=1, source_target_pairs={{0,8},{4,12},{8,0},{12,4},{16,24},{20,28},{24,16},{28,20},{1,9},{5... | collective-permute-start | bytes 393224 | tf_op jit(solution)/shard_map/ppermute | solution.py:40
  21.2 13.4 %collective-permute-start.4 = (bf16[2,8,16,256]{3,2,1,0:T(8,128)(2,1)S(1)}, bf16[2,8,16,256]{3,2,1,0:T(8,128)(2,1)S(1)}, u32[]{:S(2)}, u32[]{:S(2)}) collective-permute-start(bf16[2,8,16,256]{3,2,1,0:T(8,128)(2,1)S(1)} %get-tuple-element.24), channel_id=1, source_target_pairs={{0,12},{4,8},{8,4},{12,0},{16,28},{20,24},{24,20},{28,16},{1,13},{... | collective-permute-start | bytes 393224 | tf_op jit(solution)/shard_map/ppermute | solution.py:40
  21.2 13.4 %collective-permute-start.5 = (bf16[2,8,16,256]{3,2,1,0:T(8,128)(2,1)S(1)}, bf16[2,8,16,256]{3,2,1,0:T(8,128)(2,1)S(1)}, u32[]{:S(2)}, u32[]{:S(2)}) collective-permute-start(bf16[2,8,16,256]{3,2,1,0:T(8,128)(2,1)S(1)} %get-tuple-element.25), channel_id=1, source_target_pairs={{0,16},{4,20},{8,24},{12,28},{16,0},{20,4},{24,8},{28,12},{1,17},{... | collective-permute-start | bytes 393224 | tf_op jit(solution)/shard_map/ppermute | solution.py:40
  22.9 12.5 %collective-permute-start.6 = (bf16[2,8,16,256]{3,2,1,0:T(8,128)(2,1)S(1)}, bf16[2,8,16,256]{3,2,1,0:T(8,128)(2,1)S(1)}, u32[]{:S(2)}, u32[]{:S(2)}) collective-permute-start(bf16[2,8,16,256]{3,2,1,0:T(8,128)(2,1)S(1)} %get-tuple-element.26), channel_id=1, source_target_pairs={{0,20},{4,16},{8,28},{12,24},{16,4},{20,0},{24,12},{28,8},{1,21},{... | collective-permute-start | bytes 393224 | tf_op jit(solution)/shard_map/ppermute | solution.py:40
  23.0 18.6 %collective-permute-start.7 = (bf16[2,8,16,256]{3,2,1,0:T(8,128)(2,1)S(1)}, bf16[2,8,16,256]{3,2,1,0:T(8,128)(2,1)S(1)}, u32[]{:S(2)}, u32[]{:S(2)}) collective-permute-start(bf16[2,8,16,256]{3,2,1,0:T(8,128)(2,1)S(1)} %get-tuple-element.27), channel_id=1, source_target_pairs={{0,24},{4,28},{8,16},{12,20},{16,8},{20,12},{24,0},{28,4},{1,25},{... | collective-permute-start | bytes 393224 | tf_op jit(solution)/shard_map/ppermute | solution.py:40
  31.9 12.2 %collective-permute-start.8 = (bf16[2,8,16,256]{3,2,1,0:T(8,128)(2,1)S(1)}, bf16[2,8,16,256]{3,2,1,0:T(8,128)(2,1)S(1)}, u32[]{:S(2)}, u32[]{:S(2)}) collective-permute-start(bf16[2,8,16,256]{3,2,1,0:T(8,128)(2,1)S(1)} %get-tuple-element.28), channel_id=1, source_target_pairs={{0,28},{4,24},{8,20},{12,16},{16,12},{20,8},{24,4},{28,0},{1,29},{... | collective-permute-start | bytes 393224 | tf_op jit(solution)/shard_map/ppermute | solution.py:40
  49.1 1.0 %copy-start.3 = (bf16[32,2,2,16,256]{4,3,2,1,0:T(8,128)(2,1)}, bf16[32,2,2,16,256]{4,3,2,1,0:T(8,128)(2,1)S(1)}, u32[]{:S(2)}) copy-start(bf16[32,2,2,16,256]{4,3,2,1,0:T(8,128)(2,1)S(1)} %all-to-all-done.1) | copy-start | bytes 3145732
  50.1 34.8 %all-to-all-start = ((bf16[32,2,2,16,256]{4,3,2,1,0:T(8,128)(2,1)}), bf16[32,2,2,16,256]{4,3,2,1,0:T(8,128)(2,1)S(1)}, u32[]{:S(2)}, u32[]{:S(2)}) async-start(bf16[32,2,2,16,256]{4,3,2,1,0:T(8,128)(2,1)} %bitcast.4), calls=%async_computation | async-start | bytes 2097152 | tf_op jit(solution)/shard_map/all_to_all | solution.py:53
  54.7 27.9 %copy-start.2 = (bf16[4,512,512]{2,1,0:T(8,128)(2,1)S(1)}, bf16[4,512,512]{2,1,0:T(8,128)(2,1)}, u32[]{:S(2)}) copy-start(bf16[4,512,512]{2,1,0:T(8,128)(2,1)} %bank.3) | copy-start | bytes 6291460
  54.7 1.4 %copy-start.4 = (bf16[32,2,2,16,256]{4,3,2,1,0:T(8,128)(2,1)S(1)}, bf16[32,2,2,16,256]{4,3,2,1,0:T(8,128)(2,1)}, u32[]{:S(2)}) copy-start(bf16[32,2,2,16,256]{4,3,2,1,0:T(8,128)(2,1)} %copy-done.3) | copy-start | bytes 3145732
  56.0 1.0 %copy-start.7 = (bf16[512,512]{1,0:T(8,128)(2,1)S(1)}, bf16[512,512]{1,0:T(8,128)(2,1)}, u32[]{:S(2)}) copy-start(bf16[512,512]{1,0:T(8,128)(2,1)} %constant.61.clone.low) | copy-start | bytes 1572868
  57.1 1.0 %copy-start.9 = (bf16[512,512]{1,0:T(8,128)(2,1)S(1)}, bf16[512,512]{1,0:T(8,128)(2,1)}, u32[]{:S(2)}) copy-start(bf16[512,512]{1,0:T(8,128)(2,1)} %constant.60.clone.high) | copy-start | bytes 1572868
  58.1 24.4 %copy-start.5 = (s32[4,1]{0,1:T(1,128)S(1)}, s32[4,1]{0,1:T(1,128)}, u32[]{:S(2)}) copy-start(s32[4,1]{0,1:T(1,128)} %param.20) | copy-start | bytes 52
  61.9 3.8 %collective-permute-start.9 = (bf16[2,8,16,256]{3,2,1,0:T(8,128)(2,1)S(1)}, bf16[2,8,16,256]{3,2,1,0:T(8,128)(2,1)S(1)}, u32[]{:S(2)}, u32[]{:S(2)}) collective-permute-start(bf16[2,8,16,256]{3,2,1,0:T(8,128)(2,1)S(1)} %get-tuple-element.30), channel_id=1, source_target_pairs={{0,4},{4,0},{8,12},{12,8},{16,20},{20,16},{24,28},{28,24},{1,5},{5... | collective-permute-start | bytes 393224 | tf_op jit(solution)/shard_map/ppermute | solution.py:40
  62.3 8.3 %collective-permute-start.10 = (bf16[2,8,16,256]{3,2,1,0:T(8,128)(2,1)S(1)}, bf16[2,8,16,256]{3,2,1,0:T(8,128)(2,1)S(1)}, u32[]{:S(2)}, u32[]{:S(2)}) collective-permute-start(bf16[2,8,16,256]{3,2,1,0:T(8,128)(2,1)S(1)} %get-tuple-element.31), channel_id=1, source_target_pairs={{0,8},{4,12},{8,0},{12,4},{16,24},{20,28},{24,16},{28,20},{1,9},{5... | collective-permute-start | bytes 393224 | tf_op jit(solution)/shard_map/ppermute | solution.py:40
  63.9 9.6 %collective-permute-start.11 = (bf16[2,8,16,256]{3,2,1,0:T(8,128)(2,1)S(1)}, bf16[2,8,16,256]{3,2,1,0:T(8,128)(2,1)S(1)}, u32[]{:S(2)}, u32[]{:S(2)}) collective-permute-start(bf16[2,8,16,256]{3,2,1,0:T(8,128)(2,1)S(1)} %get-tuple-element.32), channel_id=1, source_target_pairs={{0,12},{4,8},{8,4},{12,0},{16,28},{20,24},{24,20},{28,16},{1,13},{... | collective-permute-start | bytes 393224 | tf_op jit(solution)/shard_map/ppermute | solution.py:40
  63.9 9.6 %collective-permute-start.12 = (bf16[2,8,16,256]{3,2,1,0:T(8,128)(2,1)S(1)}, bf16[2,8,16,256]{3,2,1,0:T(8,128)(2,1)S(1)}, u32[]{:S(2)}, u32[]{:S(2)}) collective-permute-start(bf16[2,8,16,256]{3,2,1,0:T(8,128)(2,1)S(1)} %get-tuple-element.33), channel_id=1, source_target_pairs={{0,16},{4,20},{8,24},{12,28},{16,0},{20,4},{24,8},{28,12},{1,17},{... | collective-permute-start | bytes 393224 | tf_op jit(solution)/shard_map/ppermute | solution.py:40
  65.6 9.6 %collective-permute-start.13 = (bf16[2,8,16,256]{3,2,1,0:T(8,128)(2,1)S(1)}, bf16[2,8,16,256]{3,2,1,0:T(8,128)(2,1)S(1)}, u32[]{:S(2)}, u32[]{:S(2)}) collective-permute-start(bf16[2,8,16,256]{3,2,1,0:T(8,128)(2,1)S(1)} %get-tuple-element.34), channel_id=1, source_target_pairs={{0,20},{4,16},{8,28},{12,24},{16,4},{20,0},{24,12},{28,8},{1,21},{... | collective-permute-start | bytes 393224 | tf_op jit(solution)/shard_map/ppermute | solution.py:40
  65.8 13.7 %collective-permute-start.14 = (bf16[2,8,16,256]{3,2,1,0:T(8,128)(2,1)S(1)}, bf16[2,8,16,256]{3,2,1,0:T(8,128)(2,1)S(1)}, u32[]{:S(2)}, u32[]{:S(2)}) collective-permute-start(bf16[2,8,16,256]{3,2,1,0:T(8,128)(2,1)S(1)} %get-tuple-element.35), channel_id=1, source_target_pairs={{0,24},{4,28},{8,16},{12,20},{16,8},{20,12},{24,0},{28,4},{1,25},{... | collective-permute-start | bytes 393224 | tf_op jit(solution)/shard_map/ppermute | solution.py:40
  70.6 11.9 %collective-permute-start.15 = (bf16[2,8,16,256]{3,2,1,0:T(8,128)(2,1)S(1)}, bf16[2,8,16,256]{3,2,1,0:T(8,128)(2,1)S(1)}, u32[]{:S(2)}, u32[]{:S(2)}) collective-permute-start(bf16[2,8,16,256]{3,2,1,0:T(8,128)(2,1)S(1)} %get-tuple-element.36), channel_id=1, source_target_pairs={{0,28},{4,24},{8,20},{12,16},{16,12},{20,8},{24,4},{28,0},{1,29},{... | collective-permute-start | bytes 393224 | tf_op jit(solution)/shard_map/ppermute | solution.py:40

commit v3 on v2

v3 whole, which is shorter than its diff:
```python
import functools
import math

import jax
import jax.numpy as jnp
import ml_dtypes
import numpy as np
from jax import lax
from jax.experimental import pallas as pl
from jax.experimental.pallas import tpu as pltpu
from jax.sharding import PartitionSpec as P

RIM = 16
LANES = 128
VMEM_BYTES = 20 * 1024 * 1024
MOST_VMEM_BYTES = 60 * 1024 * 1024

WHOLE = pl.BlockSpec(memory_space=pltpu.VMEM)
ANYWHERE = pl.BlockSpec(memory_space=pl.ANY)
SCALARS = pl.BlockSpec(memory_space=pltpu.SMEM)


def row_type(rows):
    return jnp.bfloat16 if rows % 16 == 0 else jnp.float32


def row_type(rows):
    return jnp.bfloat16 if rows % 16 == 0 else jnp.float32


def fixed(array):
    return pl.BlockSpec(array.shape, lambda i, dims=len(array.shape): (0,) * dims)


def params(limit=VMEM_BYTES):
    return pltpu.CompilerParams(vmem_limit_bytes=limit)


def cost(flops, arrays):
    return pl.CostEstimate(flops=flops, bytes_accessed=sum(a.size * a.dtype.itemsize for a in arrays), transcendentals=0)


def swap(value, axis, k):
    size = lax.axis_size(axis)
    return lax.ppermute(value, axis, [(i, i ^ k) for i in range(size)])


def exchange(blocks, axis):
    order = sorted(range(1, len(blocks)), key=lambda k: (-bin(k >> 1).count("1"), k))
    moved = {0: blocks[0]}
    for k in order:
        moved[k] = swap(blocks[k], axis, k)
    return [moved[k] for k in range(len(blocks))]


def exchange_both(packed):
    flat = packed.reshape((-1,) + packed.shape[2:])
    return lax.all_to_all(flat, ("tm", "freq"), 0, 0, tiled=True).reshape(packed.shape)


def flag_weights(spectrum_power_sum, square_sum, accum_count, rfi_mask):
    counts = accum_count.astype(jnp.float32)
    kurtosis = (
        (counts + 1.0)
        / (counts - 1.0)
        * (counts * square_sum / (spectrum_power_sum * spectrum_power_sum) - 1.0)
    )
    return rfi_mask.astype(jnp.float32) * jnp.exp(-2.0 * (kurtosis - 1.0) ** 2)


def taps(source, target):
    return np.maximum(RIM + 1 - np.abs(np.asarray(source)[:, None] - np.asarray(target)[None, :]), 0)


def smoothing_table(length, margin):
    return taps(np.arange(-margin, length + margin), np.arange(length)).astype(ml_dtypes.bfloat16)


def ends_tables(length):
    lane = np.arange(length)
    ends = np.concatenate([lane[: 2 * RIM], lane[length - 2 * RIM :]])
    outer = (lane < RIM) | (lane >= length - RIM)
    picked = (lane[:, None] == ends[None, :]).astype(np.float32)
    none = np.zeros_like(picked)
    pick = np.stack([np.concatenate([picked, none], 1), np.concatenate([none, picked], 1)])
    near = [np.tile(taps(ends + shift * length, lane) * outer, (2, 1)) for shift in (-1, 0, 1)]
    return pick.astype(ml_dtypes.bfloat16), np.concatenate(near).astype(ml_dtypes.bfloat16)


def smoothed(parts, table):
    total = sum(jnp.dot(part, table, preferred_element_type=jnp.float32) for part in parts)
    return total * (1.0 / (RIM + 1) ** 2)


def in_parts(value, count):
    parts = []
    for _ in range(count):
        parts.append(value.astype(jnp.bfloat16))
        value = value - parts[-1].astype(jnp.float32)
    return parts


def weigh_by_both(vis, flag_weight, table, pick, _, out, smooth, ends):
    n, _, planes, fs, _ = out.shape
    _, _, _, hb, fl, length = vis.shape
    cols = length // LANES

    @pl.when(pl.program_id(0) == 0)
    def _():
        lane = lax.broadcasted_iota(jnp.int32, (fl, length), 1)
        inside = (lane >= RIM) & (lane < length - RIM)
        smooth[...] = jnp.where(inside, smoothed(in_parts(flag_weight[...], 3), table[...]), 1.0)
        high, low = in_parts(flag_weight[...], 2)
        picked = jnp.dot(high, pick[0], preferred_element_type=jnp.float32)
        picked = picked + jnp.dot(low, pick[1], preferred_element_type=jnp.float32)
        ends[...] = picked.astype(jnp.bfloat16)

    for t in range(n):
        out[t, 0, planes - 1] = ends[t * fs : (t + 1) * fs]
    for c in range(2):
        for b in range(hb):
            value = (vis[c, 0, 0, b].astype(jnp.float32) * smooth[...]).astype(jnp.bfloat16)
            for t in range(n):
                for q in range(cols):
                    out[t, 0, (c * hb + b) * cols + q] = value[t * fs : (t + 1) * fs, q * LANES : (q + 1) * LANES]


def weigh(after, vis, flag_weight, half, n):
    parts, z_count, _, hb, fl, length = vis.shape
    fs, planes = fl // n, parts * hb * (length // LANES) + 1
    small = (flag_weight, jnp.asarray(smoothing_table(length, 0)), jnp.asarray(ends_tables(length)[0]))
    out = jax.ShapeDtypeStruct((n, z_count, planes, fs, LANES), jnp.bfloat16)
    return pl.pallas_call(
        weigh_by_both,
        grid=(z_count,),
        out_shape=out,
        in_specs=[pl.BlockSpec((parts, 1, 1, hb, fl, length), lambda i: (0, i, half, 0, 0, 0))]
        + [fixed(a) for a in small]
        + [ANYWHERE],
        out_specs=pl.BlockSpec((n, 1, planes, fs, LANES), lambda i: (0, i, 0, 0, 0)),
        scratch_shapes=[pltpu.VMEM((fl, length), jnp.float32), pltpu.VMEM((fl, LANES), jnp.bfloat16)],
        compiler_params=params(),
        cost_estimate=cost(0, [out, out]),
    )(vis, *small, after)


def pack_by_channel(here, vis, flag_weight, _, *outs):
    fs, hb = outs[0].shape[1], vis.shape[3]
    for k, out in enumerate(outs):
        rows = pl.ds(pl.multiple_of((here[0] ^ k) * fs, fs), fs)
        value = flag_weight[rows, :]
        high = value.astype(jnp.bfloat16)
        out[out.shape[0] - 2] = high
        out[out.shape[0] - 1] = (value - high.astype(jnp.float32)).astype(jnp.bfloat16)
        for c in range(2):
            for z in range(vis.shape[1]):
                for b in range(hb):
                    out[(c * vis.shape[1] + z) * hb + b] = vis[c, z, 0, b, rows, :]


def pack(kernel, here, after, vis, smooth, half, shapes):
    parts, z, _, hb, fl, length = vis.shape
    block = pl.BlockSpec((parts, z, 1, hb, fl, length), lambda i: (0, 0, half, 0, 0, 0))
    fixed = pl.BlockSpec((fl, length), lambda i: (0, 0))
    outs = [jax.ShapeDtypeStruct(s, jnp.bfloat16) for s in shapes]
    return pl.pallas_call(
        kernel,
        grid=(1,),
        out_shape=outs,
        in_specs=[SCALARS, block, fixed, ANYWHERE],
        out_specs=[pl.BlockSpec(s, lambda i, dims=len(s): (0,) * dims) for s in shapes],
        compiler_params=params(),
        cost_estimate=cost(0, outs + outs),
    )(here, vis, smooth, after)


def transform_tables(n, length):
    group = length // n
    lane = np.arange(length)
    order = np.zeros((n, length, length))
    for p in range(n):
        order[p, lane, (lane % n + p) % n * group + lane // n] = 1.0
    angle = 2.0 * np.pi / length * (np.outer(lane, lane) % length)
    cosine, sine = np.cos(angle), np.sin(angle)
    table = np.block([[cosine, -sine], [sine, cosine]])
    high = table.astype(ml_dtypes.bfloat16)
    low = (table - high.astype(np.float64)).astype(ml_dtypes.bfloat16)
    turn = 2.0 * np.pi / (n * length) * (np.outer(np.arange(n), lane) * (1 - length) % (n * length))
    scale = 1.0 / math.sqrt(n * length)
    twiddle = np.stack([np.cos(turn), np.sin(turn)]) * scale
    return order.astype(ml_dtypes.bfloat16), high, low, twiddle.astype(np.float32)


def short_dft(values):
    n = len(values)
    if n == 1:
        return values
    even, odd = short_dft(values[0::2]), short_dft(values[1::2])
    out = [None] * n
    for k in range(n // 2):
        real, imag = odd[k]
        if 4 * k == n:
            real, imag = imag, -real
        elif k:
            c, s = math.cos(2.0 * math.pi * k / n), math.sin(2.0 * math.pi * k / n)
            if 8 * k == n:
                real, imag = c * (real + imag), c * (imag - real)
            elif 8 * k == 3 * n:
                real, imag = s * (imag - real), -s * (real + imag)
            else:
                real, imag = c * real + s * imag, c * imag - s * real
        out[k] = (even[k][0] + real, even[k][1] + imag)
        out[k + n // 2] = (even[k][0] - real, even[k][1] - imag)
    return out


def gather_groups(values, group):
    n = len(values)
    lane = lax.broadcasted_iota(jnp.int32, values[0][0].shape, 1)
    bit = 1
    while bit < n:
        span = bit * group
        if span >= LANES:
            pick = lambda q, x, y: y if q * LANES & span else x
        else:
            upper = (lane & span) != 0
            pick = lambda q, x, y: jnp.where(upper, y, x)
        values = [[pick(q, x, y) for q, (x, y) in enumerate(zip(values[i], values[(i + bit) % n]))] for i in range(n)]
        bit *= 2
    return [values[-v % n] for v in range(n)]


def transform(here, _, order, high, low, twiddle, near, *refs, n, first, hb):
    blocks, packed = (refs[:n], refs[n]) if first else (refs[1 : n + 1], refs[0])
    ready, ordered, lined, stage, done, wide, smooth = refs[n + 1 :]
    i, me = pl.program_id(0), here[0]
    zs, fs = packed.shape[1], smooth.shape[2]
    rows, length = ready.shape[2:]
    per = zs * hb
    planes = per * pl.num_programs(0)
    group, cols = length // n, length // LANES

    if first:

        @pl.when(i == 0)
        def _():
            for k, block in enumerate(blocks):
                last, p = block.shape[0], me ^ k
                for part in range(2):
                    value = block[last - 2 + part]
                    wide[part, p, :, LANES : LANES + length] = value
                    wide[part, (p + 1) % n, :, :LANES] = value[:, length - LANES :]
                    wide[part, (p + n - 1) % n, :, LANES + length :] = value[:, :LANES]
            parts = [wide[part].reshape(n * fs, length + 2 * LANES) for part in range(2)]
            smooth[0] = smoothed(parts, near[...]).reshape(n, fs, length)

        for k, block in enumerate(blocks):
            weight = smooth[0, me ^ k]
            for c in range(2):
                for j in range(per):
                    value = block[c * planes + i * per + j].astype(jnp.float32) * weight
                    ready[me ^ k, c, j * fs : (j + 1) * fs] = value.astype(jnp.bfloat16)
    else:
        last = packed.shape[2] - 1
        for p in range(n):
            for shift in range(3):
                wide[p, :, :, shift * LANES : (shift + 1) * LANES] = packed[(p + shift - 1) % n, :, last]
        lane = lax.broadcasted_iota(jnp.int32, (n * zs * fs, length), 1)
        inside = (lane >= RIM) & (lane < length - RIM)
        ends = smoothed([wide[...].reshape(n * zs * fs, 3 * LANES)], near[...])
        smooth[...] = jnp.where(inside, 1.0, ends).reshape(n, zs, fs, length)
        for p in range(n):
            for z in range(zs):
                for c in range(2):
                    for b in range(hb):
                        first_row = (z * hb + b) * fs
                        for q in range(cols):
                            lanes = slice(q * LANES, (q + 1) * LANES)
                            value = packed[p, z, (c * hb + b) * cols + q].astype(jnp.float32) * smooth[p, z, :, lanes]
                            ready[p, c, first_row : first_row + fs, lanes] = value.astype(jnp.bfloat16)
    for p in range(n):
        moved = jnp.dot(ready[p].reshape(2 * rows, length), order[p], preferred_element_type=jnp.float32)
        ordered[p] = moved.astype(ordered.dtype).reshape(2, rows, length)
    for c in range(2):
        for r in range(0, rows, 16):
            values = [[ordered[p, c, r : r + 16, q * LANES : (q + 1) * LANES] for q in range(cols)] for p in range(n)]
            for v, columns in enumerate(gather_groups(values, group)):
                for q, column in enumerate(columns):
                    lined[v, r : r + 16, c * length + q * LANES : c * length + (q + 1) * LANES] = column.astype(jnp.bfloat16)
    flat = lined[...].reshape(n * rows, 2 * length)
    total = jnp.dot(flat, high[...], preferred_element_type=jnp.float32)
    total = total + jnp.dot(flat, low[...], preferred_element_type=jnp.float32)
    stage[...] = total.reshape(n, rows, 2 * length)
    for r in range(0, rows, 16):
        for q in range(cols):
            left, right = slice(q * LANES, (q + 1) * LANES), slice(length + q * LANES, length + (q + 1) * LANES)
            turned = []
            for v in range(n):
                real, imag = stage[v, r : r + 16, left], stage[v, r : r + 16, right]
                c, s = twiddle[0, v : v + 1, left], twiddle[1, v : v + 1, left]
                turned.append((real * c + imag * s, imag * c - real * s))
            for m, pair in enumerate(short_dft(turned)):
                for c in range(2):
                    done[m, c, r : r + 16, left] = pair[c].astype(jnp.bfloat16)
    for k in range(n):
        for c in range(2):
            if first:
                packed[k, :, c] = done[k, c].reshape(zs, hb, fs, length)
            else:
                blocks[k][c] = done[me ^ k, c].reshape(per, fs, length)


def transform_call(here, after, blocks, by_both, first):
    n, z_count, parts, hb, fs, length = by_both
    planes = z_count * hb
    steps = max(1, planes // 4)
    per = planes // steps
    rows = per * fs
    zs = per // hb
    near = smoothing_table(length, LANES) if first else ends_tables(length)[1]
    tables = [jnp.asarray(t) for t in transform_tables(n, length) + (near,)]
    if first:
        split = pl.BlockSpec((n, zs, parts, hb, fs, length), lambda i: (0, i, 0, 0, 0, 0))
    else:
        split = pl.BlockSpec((n, zs) + blocks[0].shape[2:], lambda i: (0, i, 0, 0, 0))
    if first:
        outs, out_specs, in_specs = [by_both], [split], [WHOLE] * n
    else:
        outs, in_specs = [(parts, planes, fs, length)] * n, [split]
        out_specs = [pl.BlockSpec((parts, per, fs, length), lambda i: (0, i, 0, 0))] * n
    outs = [jax.ShapeDtypeStruct(s, jnp.bfloat16) for s in outs]
    return pl.pallas_call(
        functools.partial(transform, n=n, first=first, hb=hb),
        grid=(steps,),
        out_shape=outs,
        in_specs=[SCALARS, ANYWHERE] + [WHOLE if first else fixed(t) for t in tables] + in_specs,
        out_specs=out_specs,
        scratch_shapes=[
            pltpu.VMEM((n, 2, rows, length), jnp.bfloat16),
            pltpu.VMEM((n, 2, rows, length), jnp.bfloat16),
            pltpu.VMEM((n, rows, 2 * length), jnp.bfloat16),
            pltpu.VMEM((n, rows, 2 * length), jnp.float32),
            pltpu.VMEM((n, 2, rows, length), jnp.bfloat16),
            pltpu.VMEM((2, n, fs, length + 2 * LANES) if first else (n, zs, fs, 3 * LANES), jnp.bfloat16),
            pltpu.VMEM((1, n, fs, length) if first else (n, zs, fs, length), jnp.float32),
        ],
        compiler_params=params(VMEM_BYTES if first else MOST_VMEM_BYTES),
        cost_estimate=cost(4 * n * planes * fs * (2 * length) ** 2, list(blocks) + outs),
    )(here, after, *tables, *blocks)


def filter_kernel(classes, here, bank, *refs, count, packed, aliased):
    ins, out, lined = refs[:count], refs[count + aliased], refs[-1]
    b = pl.program_id(0)
    length = out.shape[-1]
    if packed:
        n, z_count, _, _, fs, _ = ins[0].shape
        for t in range(n):
            for z in range(z_count):
                rows = slice((z * n + t) * fs, (z * n + t + 1) * fs)
                for c in range(2):
                    lined[rows, c * length : (c + 1) * length] = ins[0][t, z, c, b].astype(lined.dtype)
    else:
        hb, fs = pl.num_programs(0), ins[0].shape[2]
        fl = fs * count
        for k, block in enumerate(ins):
            for z in range(lined.shape[0] // fl):
                rows = pl.ds(pl.multiple_of(z * fl + (here[0] ^ k) * fs, fs), fs)
                for c in range(2):
                    lined[rows, c * length : (c + 1) * length] = block[c, z * hb + b].astype(lined.dtype)
    total = jnp.dot(bank[0], lined[...].astype(jnp.bfloat16), preferred_element_type=jnp.float32)
    for c in range(2):
        out[c, 0] = total[:, c * length : (c + 1) * length].astype(jnp.bfloat16)


def delay_filter(classes, here, bank, blocks, half, hb, out_shape, before, packed):
    _, channels, _ = bank.shape
    length = out_shape[-1]
    fixed = [WHOLE] * len(blocks)
    specs = [pl.BlockSpec((1, channels, channels), lambda i, classes, here: (classes[half * hb + i], 0, 0))] + fixed
    operands = [bank] + list(blocks)
    aliases = {}
    if before is not None:
        specs.append(pl.BlockSpec(memory_space=pl.ANY))
        operands.append(before)
        aliases = {2 + len(operands) - 1: 0}
    out = jax.ShapeDtypeStruct(out_shape, jnp.bfloat16)
    return pl.pallas_call(
        functools.partial(
            filter_kernel, count=len(blocks), packed=packed, aliased=int(before is not None)
        ),
        out_shape=out,
        grid_spec=pltpu.PrefetchScalarGridSpec(
            num_scalar_prefetch=2,
            grid=(hb,),
            in_specs=specs,
            out_specs=pl.BlockSpec((2, 1, channels, length), lambda i, classes, here: (0, half * hb + i, 0, 0)),
            scratch_shapes=[pltpu.VMEM((channels, 2 * length), row_type(blocks[0].shape[2]))],
        ),
        input_output_aliases=aliases,
        compiler_params=params(),
        cost_estimate=cost(4 * hb * length * channels**2, list(blocks) + [out]),
    )(classes, here, *operands)


def shards(
    visibility,
    spectrum_power_sum,
    square_sum,
    accum_count,
    rfi_mask,
    baseline_delay_class,
    filter_bank,
):
    n, z_count = lax.axis_size("tm"), lax.axis_size("freq")
    parts, baselines, fl, length = visibility.shape
    fs, hb = fl // n, baselines // z_count // 2
    here = jnp.stack([lax.axis_index("tm"), lax.axis_index("freq")]).astype(jnp.int32)
    classes = baseline_delay_class[:, 0]
    vis = visibility.reshape(parts, z_count, 2, hb, fl, length)
    planes = z_count * hb
    raw_by_channel = [(parts * planes + 2, fs, length)] * n
    out_shape = (parts, 2 * hb, fl * z_count, length)
    by_both = (n, z_count, parts, hb, fs, length)

    flag_weight = flag_weights(spectrum_power_sum, square_sum, accum_count, rfi_mask)
    early_out = pack(pack_by_channel, here, flag_weight, vis, flag_weight, 0, raw_by_channel)
    early = exchange(early_out, "tm")
    late_out = weigh(early_out[0], vis, flag_weight, 1, n)
    first = (3, 5)
    late_out, *tied = lax.optimization_barrier((late_out, *[early[k] for k in first]))
    for k, value in zip(first, tied):
        early[k] = value
    late = exchange_both(late_out)
    early_out = transform_call(here, late_out, early, by_both, True)
    early = exchange_both(early_out[0])
    late_out = transform_call(here, early_out[0], [late], by_both, False)
    late = exchange(late_out, "tm")
    filtered = delay_filter(classes, here, filter_bank, [early], 0, hb, out_shape, None, True)
    return delay_filter(classes, here, filter_bank, late, 1, hb, out_shape, filtered, False)


def solution(mesh):
    in_specs = (
        P(None, None, "freq", "tm"),
        P("freq", "tm"),
        P("freq", "tm"),
        P("freq", "tm"),
        P("freq", "tm"),
        P("freq", None),
        P(),
    )
    out_specs = P(None, "freq", None, "tm")
    return jax.shard_map(shards, mesh=mesh, in_specs=in_specs, out_specs=out_specs, check_vma=False)
```

time: 87.5 us -> 82.9 us (0.947); the launches traced: 87.1 us -> 81.5 us
  local copies, waits for them, and re-layouts: 6.13 us -> 1.65 us
  Pallas kernels: 15.8 us -> 18.7 us
  other arithmetic: 2.92 us -> 1.3 us
  waiting for transfers between devices: 33.2 us -> 31.6 us
    all_to_all x2, waiting for transfers between devices: 0.01 us -> 8.83 us  [exchange_both(): lax.all_to_all(flat, ('tm', 'freq'), 0, 0, tiled=True).reshape(packed.shape)]
    ppermute x14, waiting for transfers between devices: 31.4 us -> 22.7 us  [swap(): return lax.ppermute(value, axis, [(i, i ^ k) for i in range(size)])]
    unnamed x24 -> x30, local copies, waits for them, and re-layouts: 6.05 us -> 1.65 us
    ppermute x2 -> x0, starting transfers between devices: 3.42 us -> none  [the longest x1 2.95 us: smoothing_weights(): after = lax.ppermute(flag_weight[:, :RIM], 'tm', [(j, i) for i, j in up])]
    ppermute x14, starting transfers between devices: 14.1 us -> 17.5 us  [swap(): return lax.ppermute(value, axis, [(i, i ^ k) for i in range(size)])]
    ppermute x2 -> x0, waiting for transfers between devices: 1.83 us -> none  [the longest x1 1.81 us: smoothing_weights(): before = lax.ppermute(flag_weight[:, length - RIM:], 'tm', up)]
    pallas_call x4, Pallas kernels: 11.2 us -> 13 us  [the longest x2 10.4 us: transform_call(): pl.pallas_call(functools.partial(transform, n=n, first=first, hb=hb), gri...]
    add x1 -> x0, other arithmetic: 1.67 us -> none  [smoothing_weights(): smooth_weight = smooth_weight + factor * padded[:, offset:offset + length]]
  transfers between devices with their start and end apart: 18 -> 16, of which waited for: 11 -> 8; matrix products, arithmetic and copies ran while one was open for 0% -> 0% of each run, Pallas kernels for 14% -> 18%
where the time goes in v3:
time: 82.9 us; the launch traced here: 81.5 us
  waiting for transfers between devices  31.6 us (38%)
  starting transfers between devices  28.1 us (34%)
  Pallas kernels  18.7 us (23%)
  local copies, waits for them, and re-layouts  1.65 us (2%)
  other arithmetic  1.3 us (2%)
    ppermute x14, waiting for transfers between devices, swap(): return lax.ppermute(value, axis, [(i, i ^ k) for i in range(size)])  22.7 us
    ppermute x14, starting transfers between devices, swap(): return lax.ppermute(value, axis, [(i, i ^ k) for i in range(size)])  17.5 us
    all_to_all x2, starting transfers between devices, exchange_both(): lax.all_to_all(flat, ('tm', 'freq'), 0, 0, tiled=True).reshape(packed.shape)  10.6 us
    pallas_call x2, Pallas kernels, transform_call(): pl.pallas_call(functools.partial(transform, n=n, first=first, hb=hb), gri...  10.4 us
    all_to_all x2, waiting for transfers between devices, exchange_both(): lax.all_to_all(flat, ('tm', 'freq'), 0, 0, tiled=True).reshape(packed.shape)  8.83 us
    pallas_call x2, Pallas kernels, delay_filter(): pl.pallas_call(functools.partial(filter_kernel, count=len(blocks), packed...  5.71 us
    pallas_call x1, Pallas kernels, weigh(): pl.pallas_call(weigh_by_both, grid=(z_count,), out_shape=out, in_specs=[p...  1.97 us
  transfers between devices with their start and end apart: 16, of which 8 were waited for; matrix products, arithmetic and copies ran while one was open for 0% of the time, Pallas kernels for 18%

profile of v3, /device:TPU:0, one launch (start us, length us, event | category | flops | bytes accessed | tf_op | source)
XLA Modules:
  0.0 81.5 jit_solution(12527931076772289260)
XLA Ops:
  0.0 0.1 pad_add_fusion.here
  0.1 1.2 %exponential_multiply_fusion.flag_weight._ = f32[128,256]{1,0:T(8,128)S(1)} fusion(f32[128,256]{1,0:T(8,128)} %param.20, f32[128,256]{1,0:T(8,128)} %param.21, s32[128,256]{1,0:T(8,128)} %param.22, s32[128,256]{1,0:T(8,128)} %param.23), kind=kLoop, calls=%fused_computation | loop fusion | flops 458752 | bytes 655360 | tf_op jit(solution)/shard_map/mul | solution.py:68
  1.3 1.6 %copy-done = bf16[2,16,128,256]{3,2,1,0:T(8,128)(2,1)S(1)} copy-done((bf16[2,16,128,256]{3,2,1,0:T(8,128)(2,1)S(1)}, bf16[2,16,128,256]{3,2,1,0:T(8,128)(2,1)}, u32[]{:S(2)}) %copy-start) | copy-done | bytes 2097176
  2.9 0.6 shard_map.181
  3.5 2.4 %collective-permute-start = (bf16[18,16,256]{2,1,0:T(8,128)(2,1)S(1)}, bf16[18,16,256]{2,1,0:T(8,128)(2,1)S(1)}, u32[]{:S(2)}, u32[]{:S(2)}) collective-permute-start(bf16[18,16,256]{2,1,0:T(8,128)(2,1)S(1)} %get-tuple-element.25), channel_id=1, source_target_pairs={{0,12},{4,8},{8,4},{12,0},{16,28},{20,24},{24,20},{28,16},{1,13},{... | collective-permute-start | bytes 442376 | tf_op jit(solution)/shard_map/ppermute | solution.py:45
  6.0 1.8 %collective-permute-start.1 = (bf16[18,16,256]{2,1,0:T(8,128)(2,1)S(1)}, bf16[18,16,256]{2,1,0:T(8,128)(2,1)S(1)}, u32[]{:S(2)}, u32[]{:S(2)}) collective-permute-start(bf16[18,16,256]{2,1,0:T(8,128)(2,1)S(1)} %get-tuple-element.26), channel_id=1, source_target_pairs={{0,20},{4,16},{8,28},{12,24},{16,4},{20,0},{24,12},{28,8},{1,21},{... | collective-permute-start | bytes 442376 | tf_op jit(solution)/shard_map/ppermute | solution.py:45
  7.8 2.0 %shard_map.182._ = bf16[8,4,9,16,128]{4,3,2,1,0:T(8,128)(2,1)} custom-call(bf16[2,4,2,2,128,256]{5,4,3,2,1,0:T(8,128)(2,1)S(1)} %bitcast.9, f32[128,256]{1,0:T(8,128)S(1)} %exponential_multiply_fusion.flag_weight._, bf16[256,256]{1,0:T(8,128)(2,1)S(1)} %copy-done.9, bf16[2,256,128]{2,1,0:T(8,128)(2,1)S(1)} %copy-done.8, ...), custom_call_target="tpu_custom_call" | custom-call | bytes 2359296 | tf_op jit(solution)/shard_map/pallas_call | solution.py:133
  9.8 0.4 collective-permute-done.refs_3_
  10.2 1.2 %collective-permute-done.1.refs_5_ = bf16[18,16,256]{2,1,0:T(8,128)(2,1)S(1)} collective-permute-done((bf16[18,16,256]{2,1,0:T(8,128)(2,1)S(1)}, bf16[18,16,256]{2,1,0:T(8,128)(2,1)S(1)}, u32[]{:S(2)}, u32[]{:S(2)}) %collective-permute-start.1) | collective-permute-done | bytes 147488 | tf_op jit(solution)/shard_map/ppermute | solution.py:45
  11.4 5.7 %all-to-all-start = ((bf16[32,9,16,128]{3,2,1,0:T(8,128)(2,1)}), bf16[32,9,16,128]{3,2,1,0:T(8,128)(2,1)}, u32[]{:S(2)}, u32[]{:S(2)}) async-start(bf16[32,9,16,128]{3,2,1,0:T(8,128)(2,1)} %bitcast.4), calls=%async_computation | async-start | bytes 2359296 | tf_op jit(solution)/shard_map/all_to_all | solution.py:58
  17.2 0.3 collective-permute-start.2
  17.4 1.7 %collective-permute-start.3 = (bf16[18,16,256]{2,1,0:T(8,128)(2,1)S(1)}, bf16[18,16,256]{2,1,0:T(8,128)(2,1)S(1)}, u32[]{:S(2)}, u32[]{:S(2)}) collective-permute-start(bf16[18,16,256]{2,1,0:T(8,128)(2,1)S(1)} %get-tuple-element.29), channel_id=1, source_target_pairs={{0,8},{4,12},{8,0},{12,4},{16,24},{20,28},{24,16},{28,20},{1,9},{5... | collective-permute-start | bytes 442376 | tf_op jit(solution)/shard_map/ppermute | solution.py:45
  19.1 1.5 %collective-permute-start.4 = (bf16[18,16,256]{2,1,0:T(8,128)(2,1)S(1)}, bf16[18,16,256]{2,1,0:T(8,128)(2,1)S(1)}, u32[]{:S(2)}, u32[]{:S(2)}) collective-permute-start(bf16[18,16,256]{2,1,0:T(8,128)(2,1)S(1)} %get-tuple-element.31), channel_id=1, source_target_pairs={{0,16},{4,20},{8,24},{12,28},{16,0},{20,4},{24,8},{28,12},{1,17},{... | collective-permute-start | bytes 442376 | tf_op jit(solution)/shard_map/ppermute | solution.py:45
  20.6 0.3 collective-permute-start.5
  20.9 1.7 %collective-permute-start.6 = (bf16[18,16,256]{2,1,0:T(8,128)(2,1)S(1)}, bf16[18,16,256]{2,1,0:T(8,128)(2,1)S(1)}, u32[]{:S(2)}, u32[]{:S(2)}) collective-permute-start(bf16[18,16,256]{2,1,0:T(8,128)(2,1)S(1)} %get-tuple-element.34), channel_id=1, source_target_pairs={{0,28},{4,24},{8,20},{12,16},{16,12},{20,8},{24,4},{28,0},{1,29},{... | collective-permute-start | bytes 442376 | tf_op jit(solution)/shard_map/ppermute | solution.py:45
  22.6 9.2 %collective-permute-done.3.refs_2_ = bf16[18,16,256]{2,1,0:T(8,128)(2,1)S(1)} collective-permute-done((bf16[18,16,256]{2,1,0:T(8,128)(2,1)S(1)}, bf16[18,16,256]{2,1,0:T(8,128)(2,1)S(1)}, u32[]{:S(2)}, u32[]{:S(2)}) %collective-permute-start.3) | collective-permute-done | bytes 147488 | tf_op jit(solution)/shard_map/ppermute | solution.py:45
  31.8 1.4 %collective-permute-done.4.refs_4_ = bf16[18,16,256]{2,1,0:T(8,128)(2,1)S(1)} collective-permute-done((bf16[18,16,256]{2,1,0:T(8,128)(2,1)S(1)}, bf16[18,16,256]{2,1,0:T(8,128)(2,1)S(1)}, u32[]{:S(2)}, u32[]{:S(2)}) %collective-permute-start.4) | collective-permute-done | bytes 147488 | tf_op jit(solution)/shard_map/ppermute | solution.py:45
  33.2 4.2 %collective-permute-done.5.refs_6_ = bf16[18,16,256]{2,1,0:T(8,128)(2,1)S(1)} collective-permute-done((bf16[18,16,256]{2,1,0:T(8,128)(2,1)S(1)}, bf16[18,16,256]{2,1,0:T(8,128)(2,1)S(1)}, u32[]{:S(2)}, u32[]{:S(2)}) %collective-permute-start.5) | collective-permute-done | bytes 147488 | tf_op jit(solution)/shard_map/ppermute | solution.py:45
  37.5 3.7 %collective-permute-done.6.refs_7_ = bf16[18,16,256]{2,1,0:T(8,128)(2,1)S(1)} collective-permute-done((bf16[18,16,256]{2,1,0:T(8,128)(2,1)S(1)}, bf16[18,16,256]{2,1,0:T(8,128)(2,1)S(1)}, u32[]{:S(2)}, u32[]{:S(2)}) %collective-permute-start.6) | collective-permute-done | bytes 147488 | tf_op jit(solution)/shard_map/ppermute | solution.py:45
  41.2 4.5 %shard_map.183._ = bf16[8,4,2,2,16,256]{5,4,3,2,1,0:T(8,128)(2,1)} custom-call(s32[2]{0:T(128)S(1)} %pad_add_fusion.here, bf16[8,4,9,16,128]{4,3,2,1,0:T(8,128)(2,1)} %shard_map.182._, bf16[8,256,256]{2,1,0:T(8,128)(2,1)S(1)} %copy-done.3, bf16[512,512]{1,0:T(8,128)(2,1)S(1)} %copy-done.5, bf16[512,512]{1,0:T(8,128)(2,1)S(1)} %copy-done.4, ...), custom_call_target="tpu_custom_call" | custom-call | flops 1073741824 | bytes 2228224 | tf_op jit(solution)/shard_map/pallas_call | solution.py:332
  45.7 4.9 %all-to-all-start.1 = ((bf16[32,2,2,16,256]{4,3,2,1,0:T(8,128)(2,1)}), bf16[32,2,2,16,256]{4,3,2,1,0:T(8,128)(2,1)S(1)}, u32[]{:S(2)}, u32[]{:S(2)}) async-start(bf16[32,2,2,16,256]{4,3,2,1,0:T(8,128)(2,1)} %bitcast.6), calls=%async_computation.1 | async-start | bytes 2097152 | tf_op jit(solution)/shard_map/all_to_all | solution.py:58
  50.7 5.9 %shard_map.184 = (bf16[2,8,16,256]{3,2,1,0:T(8,128)(2,1)}, bf16[2,8,16,256]{3,2,1,0:T(8,128)(2,1)}, bf16[2,8,16,256]{3,2,1,0:T(8,128)(2,1)}, bf16[2,8,16,256]{3,...) custom-call(s32[2]{0:T(128)} %copy-done.11, ...), custom_call_target="tpu_custom_call" | custom-call | flops 1073741824 | bytes 2228224 | tf_op jit(solution)/shard_map/pallas_call | solution.py:332
  56.6 0.3 collective-permute-start.7
  56.9 1.7 %collective-permute-start.8 = (bf16[2,8,16,256]{3,2,1,0:T(8,128)(2,1)}, bf16[2,8,16,256]{3,2,1,0:T(8,128)(2,1)S(1)}, u32[]{:S(2)}, u32[]{:S(2)}) collective-permute-start(bf16[2,8,16,256]{3,2,1,0:T(8,128)(2,1)} %get-tuple-element.37), channel_id=1, source_target_pairs={{0,8},{4,12},{8,0},{12,4},{16,24},{20,28},{24,16},{28,20},{1,9},{5... | collective-permute-start | bytes 393224 | tf_op jit(solution)/shard_map/ppermute | solution.py:45
  58.6 1.7 %collective-permute-start.10 = (bf16[2,8,16,256]{3,2,1,0:T(8,128)(2,1)}, bf16[2,8,16,256]{3,2,1,0:T(8,128)(2,1)}, u32[]{:S(2)}, u32[]{:S(2)}) collective-permute-start(bf16[2,8,16,256]{3,2,1,0:T(8,128)(2,1)} %get-tuple-element.39), channel_id=1, source_target_pairs={{0,16},{4,20},{8,24},{12,28},{16,0},{20,4},{24,8},{28,12},{1,17},{... | collective-permute-start | bytes 393224 | tf_op jit(solution)/shard_map/ppermute | solution.py:45
  60.3 0.1 collective-permute-start.11
  60.4 2.6 %collective-permute-start.12 = (bf16[2,8,16,256]{3,2,1,0:T(8,128)(2,1)}, bf16[2,8,16,256]{3,2,1,0:T(8,128)(2,1)}, u32[]{:S(2)}, u32[]{:S(2)}) collective-permute-start(bf16[2,8,16,256]{3,2,1,0:T(8,128)(2,1)} %get-tuple-element.41), channel_id=1, source_target_pairs={{0,24},{4,28},{8,16},{12,20},{16,8},{20,12},{24,0},{28,4},{1,25},{... | collective-permute-start | bytes 393224 | tf_op jit(solution)/shard_map/ppermute | solution.py:45
  63.0 2.5 %collective-permute-done.8.refs_2_ = bf16[2,8,16,256]{3,2,1,0:T(8,128)(2,1)S(1)} collective-permute-done((bf16[2,8,16,256]{3,2,1,0:T(8,128)(2,1)}, bf16[2,8,16,256]{3,2,1,0:T(8,128)(2,1)S(1)}, u32[]{:S(2)}, u32[]{:S(2)}) %collective-permute-start.8) | collective-permute-done | bytes 131104 | tf_op jit(solution)/shard_map/ppermute | solution.py:45
  65.4 1.4 %collective-permute-start.13 = (bf16[2,8,16,256]{3,2,1,0:T(8,128)(2,1)}, bf16[2,8,16,256]{3,2,1,0:T(8,128)(2,1)}, u32[]{:S(2)}, u32[]{:S(2)}) collective-permute-start(bf16[2,8,16,256]{3,2,1,0:T(8,128)(2,1)} %get-tuple-element.42), channel_id=1, source_target_pairs={{0,28},{4,24},{8,20},{12,16},{16,12},{20,8},{24,4},{28,0},{1,29},{... | collective-permute-start | bytes 393224 | tf_op jit(solution)/shard_map/ppermute | solution.py:45
  66.9 8.8 %all-to-all-done.1 = bf16[32,2,2,16,256]{4,3,2,1,0:T(8,128)(2,1)S(1)} async-done(((bf16[32,2,2,16,256]{4,3,2,1,0:T(8,128)(2,1)}), bf16[32,2,2,16,256]{4,3,2,1,0:T(8,128)(2,1)S(1)}, u32[]{:S(2)}, u32[]{:S(2)}) %all-to-all-start.1) | async-done | bytes 1048608 | tf_op jit(solution)/shard_map/all_to_all | solution.py:58
  75.7 2.3 %shard_map.185.refs_8_ = bf16[2,4,512,256]{3,2,1,0:T(8,128)(2,1)} custom-call(s32[4]{0:T(128)S(1)} %bitcast.11, s32[2]{0:T(128)S(1)} %copy-done.12, bf16[4,512,512]{2,1,0:T(8,128)(2,1)S(1)} %copy-done.2, bf16[8,4,2,2,16,256]{5,4,3,2,1,0:T(8,128)(2,1)S(1)} %bitcast.10), custom_call_target="tpu_custom_call" | custom-call | flops 536870912 | bytes 3145728 | tf_op jit(solution)/shard_map/pallas_call | solution.py:388
  78.0 3.5 %shard_map.186 = bf16[2,4,512,256]{3,2,1,0:T(8,128)(2,1)} custom-call(s32[4]{0:T(128)S(1)} %bitcast.12, s32[2]{0:T(128)S(1)} %copy-done.12, bf16[4,512,512]{2,1,0:T(8,128)(2,1)S(1)} %copy-done.2, bf16[2,8,16,256]{3,2,1,0:T(8,128)(2,1)S(1)} %copy-done.7, bf16[2,8,16,256]{3,2,1,0:T(8,128)(2,1)S(1)} %collective-permute-done.7.refs_1_, ...), custom_call_target="tpu_custom_call", output_to_operand_aliasing={{}: (11, {})} | custom-call | flops 536870912 | bytes 3145728 | tf_op jit(solution)/shard_map/pallas_call | solution.py:388
  (38 shorter events, 0.1 us)
Async XLA Ops:
  0.0 7.8 %copy-start.8 = (bf16[2,256,128]{2,1,0:T(8,128)(2,1)S(1)}, bf16[2,256,128]{2,1,0:T(8,128)(2,1)}, u32[]{:S(2)}) copy-start(bf16[2,256,128]{2,1,0:T(8,128)(2,1)} %constant.34.clone.pick) | copy-start | bytes 393220
  0.0 7.8 %copy-start.9 = (bf16[256,256]{1,0:T(8,128)(2,1)S(1)}, bf16[256,256]{1,0:T(8,128)(2,1)}, u32[]{:S(2)}) copy-start(bf16[256,256]{1,0:T(8,128)(2,1)} %constant.33.clone.table) | copy-start | bytes 393220
  0.1 41.1 %copy-start.11 = (s32[2]{0:T(128)}, s32[2]{0:T(128)S(1)}, u32[]{:S(2)}) copy-start(s32[2]{0:T(128)S(1)} %pad_add_fusion.here) | copy-start | bytes 28
  1.3 1.6 %copy-start = (bf16[2,16,128,256]{3,2,1,0:T(8,128)(2,1)S(1)}, bf16[2,16,128,256]{3,2,1,0:T(8,128)(2,1)}, u32[]{:S(2)}) copy-start(bf16[2,16,128,256]{3,2,1,0:T(8,128)(2,1)} %param.19) | copy-start | bytes 6291460
  2.9 4.9 %copy-start.1 = (bf16[2,16,128,256]{3,2,1,0:T(8,128)(2,1)S(1)}, bf16[2,16,128,256]{3,2,1,0:T(8,128)(2,1)}, u32[]{:S(2)}) copy-start(bf16[2,16,128,256]{3,2,1,0:T(8,128)(2,1)} %param.19) | copy-start | bytes 6291460
  3.5 4.3 %copy-start.14 = (bf16[18,16,256]{2,1,0:T(8,128)(2,1)}, bf16[18,16,256]{2,1,0:T(8,128)(2,1)S(1)}, u32[]{:S(2)}) copy-start(bf16[18,16,256]{2,1,0:T(8,128)(2,1)S(1)} %get-tuple-element.28) | copy-start | bytes 442372
  3.5 6.7 %collective-permute-start = (bf16[18,16,256]{2,1,0:T(8,128)(2,1)S(1)}, bf16[18,16,256]{2,1,0:T(8,128)(2,1)S(1)}, u32[]{:S(2)}, u32[]{:S(2)}) collective-permute-start(bf16[18,16,256]{2,1,0:T(8,128)(2,1)S(1)} %get-tuple-element.25), channel_id=1, source_target_pairs={{0,12},{4,8},{8,4},{12,0},{16,28},{20,24},{24,20},{28,16},{1,13},{... | collective-permute-start | bytes 442376 | tf_op jit(solution)/shard_map/ppermute | solution.py:45
  6.0 5.4 %collective-permute-start.1 = (bf16[18,16,256]{2,1,0:T(8,128)(2,1)S(1)}, bf16[18,16,256]{2,1,0:T(8,128)(2,1)S(1)}, u32[]{:S(2)}, u32[]{:S(2)}) collective-permute-start(bf16[18,16,256]{2,1,0:T(8,128)(2,1)S(1)} %get-tuple-element.26), channel_id=1, source_target_pairs={{0,20},{4,16},{8,28},{12,24},{16,4},{20,0},{24,12},{28,8},{1,21},{... | collective-permute-start | bytes 442376 | tf_op jit(solution)/shard_map/ppermute | solution.py:45
  7.8 33.4 %copy-start.10 = (f32[2,8,256]{2,1,0:T(8,128)S(1)}, f32[2,8,256]{2,1,0:T(8,128)}, u32[]{:S(2)}) copy-start(f32[2,8,256]{2,1,0:T(8,128)} %constant.38.clone.twiddle) | copy-start | bytes 49156
  9.8 31.4 %copy-start.3 = (bf16[8,256,256]{2,1,0:T(8,128)(2,1)S(1)}, bf16[8,256,256]{2,1,0:T(8,128)(2,1)}, u32[]{:S(2)}) copy-start(bf16[8,256,256]{2,1,0:T(8,128)(2,1)} %constant.35.clone.order) | copy-start | bytes 3145732
  9.8 31.4 %copy-start.4 = (bf16[512,512]{1,0:T(8,128)(2,1)S(1)}, bf16[512,512]{1,0:T(8,128)(2,1)}, u32[]{:S(2)}) copy-start(bf16[512,512]{1,0:T(8,128)(2,1)} %constant.37.clone.low) | copy-start | bytes 1572868
  9.8 31.4 %copy-start.5 = (bf16[512,512]{1,0:T(8,128)(2,1)S(1)}, bf16[512,512]{1,0:T(8,128)(2,1)}, u32[]{:S(2)}) copy-start(bf16[512,512]{1,0:T(8,128)(2,1)} %constant.36.clone.high) | copy-start | bytes 1572868
  9.8 31.4 %copy-start.6 = (bf16[512,256]{1,0:T(8,128)(2,1)S(1)}, bf16[512,256]{1,0:T(8,128)(2,1)}, u32[]{:S(2)}) copy-start(bf16[512,256]{1,0:T(8,128)(2,1)} %constant.39.clone.near) | copy-start | bytes 786436
  11.4 34.3 %all-to-all-start = ((bf16[32,9,16,128]{3,2,1,0:T(8,128)(2,1)}), bf16[32,9,16,128]{3,2,1,0:T(8,128)(2,1)}, u32[]{:S(2)}, u32[]{:S(2)}) async-start(bf16[32,9,16,128]{3,2,1,0:T(8,128)(2,1)} %bitcast.4), calls=%async_computation | async-start | bytes 2359296 | tf_op jit(solution)/shard_map/all_to_all | solution.py:58
  17.2 5.4 %collective-permute-start.2 = (bf16[18,16,256]{2,1,0:T(8,128)(2,1)}, bf16[18,16,256]{2,1,0:T(8,128)(2,1)S(1)}, u32[]{:S(2)}, u32[]{:S(2)}) collective-permute-start(bf16[18,16,256]{2,1,0:T(8,128)(2,1)} %copy-done.14), channel_id=1, source_target_pairs={{0,4},{4,0},{8,12},{12,8},{16,20},{20,16},{24,28},{28,24},{1,5},{5... | collective-permute-start | bytes 442376 | tf_op jit(solution)/shard_map/ppermute | solution.py:45
  17.4 14.4 %collective-permute-start.3 = (bf16[18,16,256]{2,1,0:T(8,128)(2,1)S(1)}, bf16[18,16,256]{2,1,0:T(8,128)(2,1)S(1)}, u32[]{:S(2)}, u32[]{:S(2)}) collective-permute-start(bf16[18,16,256]{2,1,0:T(8,128)(2,1)S(1)} %get-tuple-element.29), channel_id=1, source_target_pairs={{0,8},{4,12},{8,0},{12,4},{16,24},{20,28},{24,16},{28,20},{1,9},{5... | collective-permute-start | bytes 442376 | tf_op jit(solution)/shard_map/ppermute | solution.py:45
  19.1 14.1 %collective-permute-start.4 = (bf16[18,16,256]{2,1,0:T(8,128)(2,1)S(1)}, bf16[18,16,256]{2,1,0:T(8,128)(2,1)S(1)}, u32[]{:S(2)}, u32[]{:S(2)}) collective-permute-start(bf16[18,16,256]{2,1,0:T(8,128)(2,1)S(1)} %get-tuple-element.31), channel_id=1, source_target_pairs={{0,16},{4,20},{8,24},{12,28},{16,0},{20,4},{24,8},{28,12},{1,17},{... | collective-permute-start | bytes 442376 | tf_op jit(solution)/shard_map/ppermute | solution.py:45
  20.6 16.9 %collective-permute-start.5 = (bf16[18,16,256]{2,1,0:T(8,128)(2,1)S(1)}, bf16[18,16,256]{2,1,0:T(8,128)(2,1)S(1)}, u32[]{:S(2)}, u32[]{:S(2)}) collective-permute-start(bf16[18,16,256]{2,1,0:T(8,128)(2,1)S(1)} %get-tuple-element.33), channel_id=1, source_target_pairs={{0,24},{4,28},{8,16},{12,20},{16,8},{20,12},{24,0},{28,4},{1,25},{... | collective-permute-start | bytes 442376 | tf_op jit(solution)/shard_map/ppermute | solution.py:45
  20.9 20.3 %collective-permute-start.6 = (bf16[18,16,256]{2,1,0:T(8,128)(2,1)S(1)}, bf16[18,16,256]{2,1,0:T(8,128)(2,1)S(1)}, u32[]{:S(2)}, u32[]{:S(2)}) collective-permute-start(bf16[18,16,256]{2,1,0:T(8,128)(2,1)S(1)} %get-tuple-element.34), channel_id=1, source_target_pairs={{0,28},{4,24},{8,20},{12,16},{16,12},{20,8},{24,4},{28,0},{1,29},{... | collective-permute-start | bytes 442376 | tf_op jit(solution)/shard_map/ppermute | solution.py:45
  45.7 30.0 %all-to-all-start.1 = ((bf16[32,2,2,16,256]{4,3,2,1,0:T(8,128)(2,1)}), bf16[32,2,2,16,256]{4,3,2,1,0:T(8,128)(2,1)S(1)}, u32[]{:S(2)}, u32[]{:S(2)}) async-start(bf16[32,2,2,16,256]{4,3,2,1,0:T(8,128)(2,1)} %bitcast.6), calls=%async_computation.1 | async-start | bytes 2097152 | tf_op jit(solution)/shard_map/all_to_all | solution.py:58
  50.6 25.1 %copy-start.2 = (bf16[4,512,512]{2,1,0:T(8,128)(2,1)S(1)}, bf16[4,512,512]{2,1,0:T(8,128)(2,1)}, u32[]{:S(2)}) copy-start(bf16[4,512,512]{2,1,0:T(8,128)(2,1)} %bank.3) | copy-start | bytes 6291460
  50.7 25.1 %copy-start.12 = (s32[2]{0:T(128)S(1)}, s32[2]{0:T(128)}, u32[]{:S(2)}) copy-start(s32[2]{0:T(128)} %copy-done.11) | copy-start | bytes 28
  50.7 25.0 %copy-start.13 = (s32[4,1]{0,1:T(1,128)S(1)}, s32[4,1]{0,1:T(1,128)}, u32[]{:S(2)}) copy-start(s32[4,1]{0,1:T(1,128)} %param.24) | copy-start | bytes 52
  56.6 3.8 %collective-permute-start.7 = (bf16[2,8,16,256]{3,2,1,0:T(8,128)(2,1)}, bf16[2,8,16,256]{3,2,1,0:T(8,128)(2,1)S(1)}, u32[]{:S(2)}, u32[]{:S(2)}) collective-permute-start(bf16[2,8,16,256]{3,2,1,0:T(8,128)(2,1)} %get-tuple-element.36), channel_id=1, source_target_pairs={{0,4},{4,0},{8,12},{12,8},{16,20},{20,16},{24,28},{28,24},{1,5},{5... | collective-permute-start | bytes 393224 | tf_op jit(solution)/shard_map/ppermute | solution.py:45
  56.9 8.6 %collective-permute-start.8 = (bf16[2,8,16,256]{3,2,1,0:T(8,128)(2,1)}, bf16[2,8,16,256]{3,2,1,0:T(8,128)(2,1)S(1)}, u32[]{:S(2)}, u32[]{:S(2)}) collective-permute-start(bf16[2,8,16,256]{3,2,1,0:T(8,128)(2,1)} %get-tuple-element.37), channel_id=1, source_target_pairs={{0,8},{4,12},{8,0},{12,4},{16,24},{20,28},{24,16},{28,20},{1,9},{5... | collective-permute-start | bytes 393224 | tf_op jit(solution)/shard_map/ppermute | solution.py:45
  58.6 19.4 %collective-permute-start.9 = (bf16[2,8,16,256]{3,2,1,0:T(8,128)(2,1)}, bf16[2,8,16,256]{3,2,1,0:T(8,128)(2,1)S(1)}, u32[]{:S(2)}, u32[]{:S(2)}) collective-permute-start(bf16[2,8,16,256]{3,2,1,0:T(8,128)(2,1)} %get-tuple-element.38), channel_id=1, source_target_pairs={{0,12},{4,8},{8,4},{12,0},{16,28},{20,24},{24,20},{28,16},{1,13},{... | collective-permute-start | bytes 393224 | tf_op jit(solution)/shard_map/ppermute | solution.py:45
  58.6 19.4 %collective-permute-start.10 = (bf16[2,8,16,256]{3,2,1,0:T(8,128)(2,1)}, bf16[2,8,16,256]{3,2,1,0:T(8,128)(2,1)}, u32[]{:S(2)}, u32[]{:S(2)}) collective-permute-start(bf16[2,8,16,256]{3,2,1,0:T(8,128)(2,1)} %get-tuple-element.39), channel_id=1, source_target_pairs={{0,16},{4,20},{8,24},{12,28},{16,0},{20,4},{24,8},{28,12},{1,17},{... | collective-permute-start | bytes 393224 | tf_op jit(solution)/shard_map/ppermute | solution.py:45
  60.3 17.7 %collective-permute-start.11 = (bf16[2,8,16,256]{3,2,1,0:T(8,128)(2,1)}, bf16[2,8,16,256]{3,2,1,0:T(8,128)(2,1)}, u32[]{:S(2)}, u32[]{:S(2)}) collective-permute-start(bf16[2,8,16,256]{3,2,1,0:T(8,128)(2,1)} %get-tuple-element.40), channel_id=1, source_target_pairs={{0,20},{4,16},{8,28},{12,24},{16,4},{20,0},{24,12},{28,8},{1,21},{... | collective-permute-start | bytes 393224 | tf_op jit(solution)/shard_map/ppermute | solution.py:45
  60.4 17.6 %collective-permute-start.12 = (bf16[2,8,16,256]{3,2,1,0:T(8,128)(2,1)}, bf16[2,8,16,256]{3,2,1,0:T(8,128)(2,1)}, u32[]{:S(2)}, u32[]{:S(2)}) collective-permute-start(bf16[2,8,16,256]{3,2,1,0:T(8,128)(2,1)} %get-tuple-element.41), channel_id=1, source_target_pairs={{0,24},{4,28},{8,16},{12,20},{16,8},{20,12},{24,0},{28,4},{1,25},{... | collective-permute-start | bytes 393224 | tf_op jit(solution)/shard_map/ppermute | solution.py:45
  65.4 12.6 %collective-permute-start.13 = (bf16[2,8,16,256]{3,2,1,0:T(8,128)(2,1)}, bf16[2,8,16,256]{3,2,1,0:T(8,128)(2,1)}, u32[]{:S(2)}, u32[]{:S(2)}) collective-permute-start(bf16[2,8,16,256]{3,2,1,0:T(8,128)(2,1)} %get-tuple-element.42), channel_id=1, source_target_pairs={{0,28},{4,24},{8,20},{12,16},{16,12},{20,8},{24,4},{28,0},{1,29},{... | collective-permute-start | bytes 393224 | tf_op jit(solution)/shard_map/ppermute | solution.py:45
  75.7 2.3 %copy-start.7 = (bf16[2,8,16,256]{3,2,1,0:T(8,128)(2,1)S(1)}, bf16[2,8,16,256]{3,2,1,0:T(8,128)(2,1)}, u32[]{:S(2)}) copy-start(bf16[2,8,16,256]{3,2,1,0:T(8,128)(2,1)} %get-tuple-element.35.refs_0_) | copy-start | bytes 393220

commit v4 on v3

--- a/solution.py
+++ b/solution.py
@@ -58,22 +58,12 @@
     return lax.all_to_all(flat, ("tm", "freq"), 0, 0, tiled=True).reshape(packed.shape)
 
 
-def flag_weights(spectrum_power_sum, square_sum, accum_count, rfi_mask):
-    counts = accum_count.astype(jnp.float32)
-    kurtosis = (
-        (counts + 1.0)
-        / (counts - 1.0)
-        * (counts * square_sum / (spectrum_power_sum * spectrum_power_sum) - 1.0)
-    )
-    return rfi_mask.astype(jnp.float32) * jnp.exp(-2.0 * (kurtosis - 1.0) ** 2)
-
-
 def taps(source, target):
     return np.maximum(RIM + 1 - np.abs(np.asarray(source)[:, None] - np.asarray(target)[None, :]), 0)
 
 
-def smoothing_table(length, margin):
-    return taps(np.arange(-margin, length + margin), np.arange(length)).astype(ml_dtypes.bfloat16)
+def smoothing_table(length):
+    return taps(np.arange(length), np.arange(length)).astype(ml_dtypes.bfloat16)
 
 
 def ends_tables(length):
@@ -100,78 +90,85 @@
     return parts
 
 
-def weigh_by_both(vis, flag_weight, table, pick, _, out, smooth, ends):
+def weigh_by_both(vis, power, square, count, mask, table, pick, out, smooth, ends):
     n, _, planes, fs, _ = out.shape
     _, _, _, hb, fl, length = vis.shape
     cols = length // LANES
 
     @pl.when(pl.program_id(0) == 0)
     def _():
+        counts = count[...].astype(jnp.float32)
+        total = power[...]
+        kurtosis = (counts + 1.0) / (counts - 1.0) * (counts * square[...] / (total * total) - 1.0)
+        flag_weight = mask[...].astype(jnp.float32) * jnp.exp(-2.0 * ((kurtosis - 1.0) * (kurtosis - 1.0)))
         lane = lax.broadcasted_iota(jnp.int32, (fl, length), 1)
         inside = (lane >= RIM) & (lane < length - RIM)
-        smooth[...] = jnp.where(inside, smoothed(in_parts(flag_weight[...], 3), table[...]), 1.0)
-        high, low = in_parts(flag_weight[...], 2)
+        smooth[...] = jnp.where(inside, smoothed(in_parts(flag_weight, 3), table[...]), 1.0)
+        high, low = in_parts(flag_weight, 2)
         picked = jnp.dot(high, pick[0], preferred_element_type=jnp.float32)
         picked = picked + jnp.dot(low, pick[1], preferred_element_type=jnp.float32)
         ends[...] = picked.astype(jnp.bfloat16)
 
-    for t in range(n):
-        out[t, 0, planes - 1] = ends[t * fs : (t + 1) * fs]
-    for c in range(2):
-        for b in range(hb):
-            value = (vis[c, 0, 0, b].astype(jnp.float32) * smooth[...]).astype(jnp.bfloat16)
-            for t in range(n):
-                for q in range(cols):
-                    out[t, 0, (c * hb + b) * cols + q] = value[t * fs : (t + 1) * fs, q * LANES : (q + 1) * LANES]
-
-
-def weigh(after, vis, flag_weight, half, n):
+    for z in range(out.shape[1]):
+        for t in range(n):
+            out[t, z, planes - 1] = ends[t * fs : (t + 1) * fs]
+        for c in range(2):
+            for b in range(hb):
+                value = (vis[c, z, 0, b].astype(jnp.float32) * smooth[...]).astype(jnp.bfloat16)
+                for t in range(n):
+                    for q in range(cols):
+                        out[t, z, (c * hb + b) * cols + q] = value[t * fs : (t + 1) * fs, q * LANES : (q + 1) * LANES]
+
+
+def weigh(vis, fields, half, n):
     parts, z_count, _, hb, fl, length = vis.shape
     fs, planes = fl // n, parts * hb * (length // LANES) + 1
-    small = (flag_weight, jnp.asarray(smoothing_table(length, 0)), jnp.asarray(ends_tables(length)[0]))
+    zs = max(1, z_count // 2)
+    small = fields + (jnp.asarray(smoothing_table(length)), jnp.asarray(ends_tables(length)[0]))
     out = jax.ShapeDtypeStruct((n, z_count, planes, fs, LANES), jnp.bfloat16)
+    smooth = jax.ShapeDtypeStruct((fl, length), jnp.float32)
+    ends = jax.ShapeDtypeStruct((fl, LANES), jnp.bfloat16)
     return pl.pallas_call(
         weigh_by_both,
-        grid=(z_count,),
-        out_shape=out,
-        in_specs=[pl.BlockSpec((parts, 1, 1, hb, fl, length), lambda i: (0, i, half, 0, 0, 0))]
-        + [fixed(a) for a in small]
-        + [ANYWHERE],
-        out_specs=pl.BlockSpec((n, 1, planes, fs, LANES), lambda i: (0, i, 0, 0, 0)),
-        scratch_shapes=[pltpu.VMEM((fl, length), jnp.float32), pltpu.VMEM((fl, LANES), jnp.bfloat16)],
-        compiler_params=params(),
+        grid=(z_count // zs,),
+        out_shape=[out, smooth, ends],
+        in_specs=[pl.BlockSpec((parts, zs, 1, hb, fl, length), lambda i: (0, i, half, 0, 0, 0))] + [fixed(a) for a in small],
+        out_specs=[pl.BlockSpec((n, zs, planes, fs, LANES), lambda i: (0, i, 0, 0, 0)), fixed(smooth), fixed(ends)],
+        compiler_params=params(MOST_VMEM_BYTES),
         cost_estimate=cost(0, [out, out]),
-    )(vis, *small, after)
-
-
-def pack_by_channel(here, vis, flag_weight, _, *outs):
-    fs, hb = outs[0].shape[1], vis.shape[3]
+    )(vis, *small)
+
+
+def weigh_by_channel(here, vis, smooth, ends, *outs):
+    planes, fs, _ = outs[0].shape
+    _, z_count, _, hb, _, length = vis.shape
+    cols = length // LANES
     for k, out in enumerate(outs):
         rows = pl.ds(pl.multiple_of((here[0] ^ k) * fs, fs), fs)
-        value = flag_weight[rows, :]
-        high = value.astype(jnp.bfloat16)
-        out[out.shape[0] - 2] = high
-        out[out.shape[0] - 1] = (value - high.astype(jnp.float32)).astype(jnp.bfloat16)
+        out[planes - 1] = ends[rows, :]
+        weight = smooth[rows, :]
         for c in range(2):
-            for z in range(vis.shape[1]):
+            for z in range(z_count):
                 for b in range(hb):
-                    out[(c * vis.shape[1] + z) * hb + b] = vis[c, z, 0, b, rows, :]
-
-
-def pack(kernel, here, after, vis, smooth, half, shapes):
-    parts, z, _, hb, fl, length = vis.shape
-    block = pl.BlockSpec((parts, z, 1, hb, fl, length), lambda i: (0, 0, half, 0, 0, 0))
-    fixed = pl.BlockSpec((fl, length), lambda i: (0, 0))
-    outs = [jax.ShapeDtypeStruct(s, jnp.bfloat16) for s in shapes]
+                    value = (vis[c, z, 0, b, rows, :].astype(jnp.float32) * weight).astype(jnp.bfloat16)
+                    for q in range(cols):
+                        out[((c * z_count + z) * hb + b) * cols + q] = value[:, q * LANES : (q + 1) * LANES]
+
+
+def weigh_early(here, vis, smooth, ends, half, n):
+    parts, z_count, _, hb, fl, length = vis.shape
+    shape = (parts * z_count * hb * (length // LANES) + 1, fl // n, LANES)
+    outs = [jax.ShapeDtypeStruct(shape, jnp.bfloat16)] * n
     return pl.pallas_call(
-        kernel,
+        weigh_by_channel,
         grid=(1,),
         out_shape=outs,
-        in_specs=[SCALARS, block, fixed, ANYWHERE],
-        out_specs=[pl.BlockSpec(s, lambda i, dims=len(s): (0,) * dims) for s in shapes],
+        in_specs=[SCALARS, pl.BlockSpec((parts, z_count, 1, hb, fl, length), lambda i: (0, 0, half, 0, 0, 0))]
+        + [fixed(smooth), fixed(ends)],
+        out_specs=[fixed(o) for o in outs],
         compiler_params=params(),
         cost_estimate=cost(0, outs + outs),
-    )(here, vis, smooth, after)
+    )(here, vis, smooth, ends)
 
 
 def transform_tables(n, length):
@@ -240,35 +237,36 @@
     planes = per * pl.num_programs(0)
     group, cols = length // n, length // LANES
 
+    def weigh_ends():
+        count = smooth.shape[0] * smooth.shape[1] * fs
+        lane = lax.broadcasted_iota(jnp.int32, (count, length), 1)
+        inside = (lane >= RIM) & (lane < length - RIM)
+        ends = smoothed([wide[...].reshape(count, 3 * LANES)], near[...])
+        smooth[...] = jnp.where(inside, 1.0, ends).reshape(smooth.shape)
+
     if first:
 
         @pl.when(i == 0)
         def _():
             for k, block in enumerate(blocks):
-                last, p = block.shape[0], me ^ k
-                for part in range(2):
-                    value = block[last - 2 + part]
-                    wide[part, p, :, LANES : LANES + length] = value
-                    wide[part, (p + 1) % n, :, :LANES] = value[:, length - LANES :]
-                    wide[part, (p + n - 1) % n, :, LANES + length :] = value[:, :LANES]
-            parts = [wide[part].reshape(n * fs, length + 2 * LANES) for part in range(2)]
-            smooth[0] = smoothed(parts, near[...]).reshape(n, fs, length)
+                for shift in range(3):
+                    p = lax.rem((me ^ k) + n + 1 - shift, n)
+                    wide[p, 0, :, shift * LANES : (shift + 1) * LANES] = block[block.shape[0] - 1]
+            weigh_ends()
 
         for k, block in enumerate(blocks):
-            weight = smooth[0, me ^ k]
             for c in range(2):
                 for j in range(per):
-                    value = block[c * planes + i * per + j].astype(jnp.float32) * weight
-                    ready[me ^ k, c, j * fs : (j + 1) * fs] = value.astype(jnp.bfloat16)
+                    for q in range(cols):
+                        lanes = slice(q * LANES, (q + 1) * LANES)
+                        value = block[(c * planes + i * per + j) * cols + q].astype(jnp.float32) * smooth[me ^ k, 0, :, lanes]
+                        ready[me ^ k, c, j * fs : (j + 1) * fs, lanes] = value.astype(jnp.bfloat16)
     else:
         last = packed.shape[2] - 1
         for p in range(n):
             for shift in range(3):
                 wide[p, :, :, shift * LANES : (shift + 1) * LANES] = packed[(p + shift - 1) % n, :, last]
-        lane = lax.broadcasted_iota(jnp.int32, (n * zs * fs, length), 1)
-        inside = (lane >= RIM) & (lane < length - RIM)
-        ends = smoothed([wide[...].reshape(n * zs * fs, 3 * LANES)], near[...])
-        smooth[...] = jnp.where(inside, 1.0, ends).reshape(n, zs, fs, length)
+        weigh_ends()
         for p in range(n):
             for z in range(zs):
                 for c in range(2):
@@ -313,12 +311,11 @@
 def transform_call(here, after, blocks, by_both, first):
     n, z_count, parts, hb, fs, length = by_both
     planes = z_count * hb
-    steps = max(1, planes // 4)
+    steps = max(1, planes // 8)
     per = planes // steps
     rows = per * fs
     zs = per // hb
-    near = smoothing_table(length, LANES) if first else ends_tables(length)[1]
-    tables = [jnp.asarray(t) for t in transform_tables(n, length) + (near,)]
+    tables = [jnp.asarray(t) for t in transform_tables(n, length) + (ends_tables(length)[1],)]
     if first:
         split = pl.BlockSpec((n, zs, parts, hb, fs, length), lambda i: (0, i, 0, 0, 0, 0))
     else:
@@ -341,8 +338,8 @@
             pltpu.VMEM((n, rows, 2 * length), jnp.bfloat16),
             pltpu.VMEM((n, rows, 2 * length), jnp.float32),
             pltpu.VMEM((n, 2, rows, length), jnp.bfloat16),
-            pltpu.VMEM((2, n, fs, length + 2 * LANES) if first else (n, zs, fs, 3 * LANES), jnp.bfloat16),
-            pltpu.VMEM((1, n, fs, length) if first else (n, zs, fs, length), jnp.float32),
+            pltpu.VMEM((n, 1 if first else zs, fs, 3 * LANES), jnp.bfloat16),
+            pltpu.VMEM((n, 1 if first else zs, fs, length), jnp.float32),
         ],
         compiler_params=params(VMEM_BYTES if first else MOST_VMEM_BYTES),
         cost_estimate=cost(4 * n * planes * fs * (2 * length) ** 2, list(blocks) + outs),
@@ -419,15 +416,13 @@
     classes = baseline_delay_class[:, 0]
     vis = visibility.reshape(parts, z_count, 2, hb, fl, length)
     planes = z_count * hb
-    raw_by_channel = [(parts * planes + 2, fs, length)] * n
     out_shape = (parts, 2 * hb, fl * z_count, length)
     by_both = (n, z_count, parts, hb, fs, length)
 
-    flag_weight = flag_weights(spectrum_power_sum, square_sum, accum_count, rfi_mask)
-    early_out = pack(pack_by_channel, here, flag_weight, vis, flag_weight, 0, raw_by_channel)
+    late_out, smooth, ends = weigh(vis, (spectrum_power_sum, square_sum, accum_count, rfi_mask), 1, n)
+    early_out = weigh_early(here, vis, smooth, ends, 0, n)
     early = exchange(early_out, "tm")
-    late_out = weigh(early_out[0], vis, flag_weight, 1, n)
-    first = (3, 5)
+    first = ()
     late_out, *tied = lax.optimization_barrier((late_out, *[early[k] for k in first]))
     for k, value in zip(first, tied):
         early[k] = value

time: 82.9 us -> 78.8 us (0.951)
  starting transfers between devices: 28.1 us -> 25.9 us
  other arithmetic: 1.3 us -> 0.08 us
    ppermute x14, starting transfers between devices: 17.5 us -> 13.6 us  [swap(): return lax.ppermute(value, axis, [(i, i ^ k) for i in range(size)])]
    all_to_all x2, starting transfers between devices: 10.6 us -> 12.3 us  [exchange_both(): lax.all_to_all(flat, ('tm', 'freq'), 0, 0, tiled=True).reshape(packed.shape)]
    ppermute x14, waiting for transfers between devices: 22.7 us -> 21.4 us  [swap(): return lax.ppermute(value, axis, [(i, i ^ k) for i in range(size)])]
    mul x1 -> x0, other arithmetic: 1.23 us -> none  [flag_weights(): return rfi_mask.astype(jnp.float32) * jnp.exp(-2.0 * (kurtosis - 1.0) ** 2)]
    pallas_call x2, Pallas kernels: 2.6 us -> 3.59 us  [the longest x1 2.87 us: weigh(): pl.pallas_call(weigh_by_both, grid=(z_count // zs,), out_shape=[out, smoo...]
  transfers between devices with their start and end apart: 16 -> 16, of which waited for: 8 -> 7; matrix products, arithmetic and copies ran while one was open for 0% -> 0% of each run, Pallas kernels for 18% -> 17%
where the time goes in v4:
time: 78.8 us; the launch traced here: 77.4 us
  waiting for transfers between devices  31 us (39%)
  starting transfers between devices  25.9 us (33%)
  Pallas kernels  19.2 us (24%)
  local copies, waits for them, and re-layouts  1.1 us (1%)
    ppermute x14, waiting for transfers between devices, swap(): return lax.ppermute(value, axis, [(i, i ^ k) for i in range(size)])  21.4 us
    ppermute x14, starting transfers between devices, swap(): return lax.ppermute(value, axis, [(i, i ^ k) for i in range(size)])  13.6 us
    all_to_all x2, starting transfers between devices, exchange_both(): lax.all_to_all(flat, ('tm', 'freq'), 0, 0, tiled=True).reshape(packed.shape)  12.3 us
    pallas_call x2, Pallas kernels, transform_call(): pl.pallas_call(functools.partial(transform, n=n, first=first, hb=hb), gri...  9.86 us
    all_to_all x2, waiting for transfers between devices, exchange_both(): lax.all_to_all(flat, ('tm', 'freq'), 0, 0, tiled=True).reshape(packed.shape)  9.65 us
    pallas_call x2, Pallas kernels, delay_filter(): pl.pallas_call(functools.partial(filter_kernel, count=len(blocks), packed...  5.71 us
    pallas_call x1, Pallas kernels, weigh(): pl.pallas_call(weigh_by_both, grid=(z_count // zs,), out_shape=[out, smoo...  2.87 us
  transfers between devices with their start and end apart: 16, of which 7 were waited for; matrix products, arithmetic and copies ran while one was open for 0% of the time, Pallas kernels for 17%

profile of v4, /device:TPU:0, one launch (start us, length us, event | category | flops | bytes accessed | tf_op | source)
XLA Modules:
  0.0 77.4 jit_solution(15296016298579355936)
XLA Ops:
  0.0 2.9 %shard_map.181 = (bf16[8,4,9,16,128]{4,3,2,1,0:T(8,128)(2,1)}, f32[128,256]{1,0:T(8,128)}, bf16[128,128]{1,0:T(8,128)(2,1)}) custom-call(bf16[2,4,2,2,128,256]{5,4,3,2,1,0:T(8,128)(2,1)} %bitcast.8, f32[128,256]{1,0:T(8,128)} %power.1, f32[128,256]{1,0:T(8,128)} %square.1, s32[128,256]{1,0:T(8,128)} %count.1, s32[128,256]{1,0:T(8,128)} %mask.1, ...), custom_call_target="tpu_custom_call" | custom-call | bytes 2359296 | tf_op jit(solution)/shard_map/pallas_call | solution.py:131
  2.9 0.0 copy-start.6
  2.9 0.0 copy-start.9
  2.9 7.4 %all-to-all-start = ((bf16[32,9,16,128]{3,2,1,0:T(8,128)(2,1)}), bf16[32,9,16,128]{3,2,1,0:T(8,128)(2,1)}, u32[]{:S(2)}, u32[]{:S(2)}) async-start(bf16[32,9,16,128]{3,2,1,0:T(8,128)(2,1)} %bitcast.10), calls=%async_computation | async-start | bytes 2359296 | tf_op jit(solution)/shard_map/all_to_all | solution.py:58
  10.4 0.1 pad_add_fusion.here
  10.5 1.0 %copy-done.8 = f32[128,256]{1,0:T(8,128)S(1)} copy-done((f32[128,256]{1,0:T(8,128)S(1)}, f32[128,256]{1,0:T(8,128)}, u32[]{:S(2)}) %copy-start.8) | copy-done | bytes 131096
  11.5 0.7 shard_map.182
  12.2 0.3 collective-permute-start
  12.5 1.7 %collective-permute-start.1 = (bf16[33,16,128]{2,1,0:T(8,128)(2,1)S(1)}, bf16[33,16,128]{2,1,0:T(8,128)(2,1)S(1)}, u32[]{:S(2)}, u32[]{:S(2)}) collective-permute-start(bf16[33,16,128]{2,1,0:T(8,128)(2,1)S(1)} %get-tuple-element.29), channel_id=1, source_target_pairs={{0,8},{4,12},{8,0},{12,4},{16,24},{20,28},{24,16},{28,20},{1,9},{5... | collective-permute-start | bytes 405512 | tf_op jit(solution)/shard_map/ppermute | solution.py:45
  14.2 0.0 collective-permute-start.2
  14.2 1.7 %collective-permute-start.3 = (bf16[33,16,128]{2,1,0:T(8,128)(2,1)S(1)}, bf16[33,16,128]{2,1,0:T(8,128)(2,1)S(1)}, u32[]{:S(2)}, u32[]{:S(2)}) collective-permute-start(bf16[33,16,128]{2,1,0:T(8,128)(2,1)S(1)} %get-tuple-element.31), channel_id=1, source_target_pairs={{0,16},{4,20},{8,24},{12,28},{16,0},{20,4},{24,8},{28,12},{1,17},{... | collective-permute-start | bytes 405512 | tf_op jit(solution)/shard_map/ppermute | solution.py:45
  15.9 0.1 collective-permute-start.4
  16.0 2.6 %collective-permute-start.5 = (bf16[33,16,128]{2,1,0:T(8,128)(2,1)S(1)}, bf16[33,16,128]{2,1,0:T(8,128)(2,1)S(1)}, u32[]{:S(2)}, u32[]{:S(2)}) collective-permute-start(bf16[33,16,128]{2,1,0:T(8,128)(2,1)S(1)} %get-tuple-element.33), channel_id=1, source_target_pairs={{0,24},{4,28},{8,16},{12,20},{16,8},{20,12},{24,0},{28,4},{1,25},{... | collective-permute-start | bytes 405512 | tf_op jit(solution)/shard_map/ppermute | solution.py:45
  18.6 6.2 %collective-permute-done.1.refs_2_ = bf16[33,16,128]{2,1,0:T(8,128)(2,1)S(1)} collective-permute-done((bf16[33,16,128]{2,1,0:T(8,128)(2,1)S(1)}, bf16[33,16,128]{2,1,0:T(8,128)(2,1)S(1)}, u32[]{:S(2)}, u32[]{:S(2)}) %collective-permute-start.1) | collective-permute-done | bytes 135200 | tf_op jit(solution)/shard_map/ppermute | solution.py:45
  24.8 0.1 collective-permute-start.6
  24.8 2.8 %collective-permute-done.2.refs_3_ = bf16[33,16,128]{2,1,0:T(8,128)(2,1)S(1)} collective-permute-done((bf16[33,16,128]{2,1,0:T(8,128)(2,1)S(1)}, bf16[33,16,128]{2,1,0:T(8,128)(2,1)S(1)}, u32[]{:S(2)}, u32[]{:S(2)}) %collective-permute-start.2) | collective-permute-done | bytes 135200 | tf_op jit(solution)/shard_map/ppermute | solution.py:45
  27.6 0.8 %collective-permute-done.4.refs_5_ = bf16[33,16,128]{2,1,0:T(8,128)(2,1)S(1)} collective-permute-done((bf16[33,16,128]{2,1,0:T(8,128)(2,1)S(1)}, bf16[33,16,128]{2,1,0:T(8,128)(2,1)S(1)}, u32[]{:S(2)}, u32[]{:S(2)}) %collective-permute-start.4) | collective-permute-done | bytes 135200 | tf_op jit(solution)/shard_map/ppermute | solution.py:45
  28.4 6.2 %collective-permute-done.5.refs_6_ = bf16[33,16,128]{2,1,0:T(8,128)(2,1)S(1)} collective-permute-done((bf16[33,16,128]{2,1,0:T(8,128)(2,1)S(1)}, bf16[33,16,128]{2,1,0:T(8,128)(2,1)S(1)}, u32[]{:S(2)}, u32[]{:S(2)}) %collective-permute-start.5) | collective-permute-done | bytes 135200 | tf_op jit(solution)/shard_map/ppermute | solution.py:45
  34.6 2.9 %collective-permute-done.6.refs_7_ = bf16[33,16,128]{2,1,0:T(8,128)(2,1)S(1)} collective-permute-done((bf16[33,16,128]{2,1,0:T(8,128)(2,1)S(1)}, bf16[33,16,128]{2,1,0:T(8,128)(2,1)S(1)}, u32[]{:S(2)}, u32[]{:S(2)}) %collective-permute-start.6) | collective-permute-done | bytes 135200 | tf_op jit(solution)/shard_map/ppermute | solution.py:45
  37.5 4.2 %shard_map.183._ = bf16[8,4,2,2,16,256]{5,4,3,2,1,0:T(8,128)(2,1)} custom-call(s32[2]{0:T(128)S(1)} %pad_add_fusion.here, bf16[8,4,9,16,128]{4,3,2,1,0:T(8,128)(2,1)S(1)} %copy-done.2, bf16[8,256,256]{2,1,0:T(8,128)(2,1)S(1)} %copy-done.3, bf16[512,512]{1,0:T(8,128)(2,1)S(1)} %copy-done.5, bf16[512,512]{1,0:T(8,128)(2,1)S(1)} %copy-done.4, ...), custom_call_target="tpu_custom_call" | custom-call | flops 1073741824 | bytes 2129920 | tf_op jit(solution)/shard_map/pallas_call | solution.py:329
  41.7 4.9 %all-to-all-start.1 = ((bf16[32,2,2,16,256]{4,3,2,1,0:T(8,128)(2,1)}), bf16[32,2,2,16,256]{4,3,2,1,0:T(8,128)(2,1)S(1)}, u32[]{:S(2)}, u32[]{:S(2)}) async-start(bf16[32,2,2,16,256]{4,3,2,1,0:T(8,128)(2,1)} %bitcast.6), calls=%async_computation.1 | async-start | bytes 2097152 | tf_op jit(solution)/shard_map/all_to_all | solution.py:58
  46.6 5.6 %shard_map.184 = (bf16[2,8,16,256]{3,2,1,0:T(8,128)(2,1)}, bf16[2,8,16,256]{3,2,1,0:T(8,128)(2,1)}, bf16[2,8,16,256]{3,2,1,0:T(8,128)(2,1)}, bf16[2,8,16,256]{3,...) custom-call(s32[2]{0:T(128)} %copy-done.11, ...), custom_call_target="tpu_custom_call" | custom-call | flops 1073741824 | bytes 2228224 | tf_op jit(solution)/shard_map/pallas_call | solution.py:329
  52.3 0.3 collective-permute-start.7
  52.5 1.7 %collective-permute-start.8 = (bf16[2,8,16,256]{3,2,1,0:T(8,128)(2,1)}, bf16[2,8,16,256]{3,2,1,0:T(8,128)(2,1)S(1)}, u32[]{:S(2)}, u32[]{:S(2)}) collective-permute-start(bf16[2,8,16,256]{3,2,1,0:T(8,128)(2,1)} %get-tuple-element.37), channel_id=1, source_target_pairs={{0,8},{4,12},{8,0},{12,4},{16,24},{20,28},{24,16},{28,20},{1,9},{5... | collective-permute-start | bytes 393224 | tf_op jit(solution)/shard_map/ppermute | solution.py:45
  54.2 1.7 %collective-permute-start.10 = (bf16[2,8,16,256]{3,2,1,0:T(8,128)(2,1)}, bf16[2,8,16,256]{3,2,1,0:T(8,128)(2,1)}, u32[]{:S(2)}, u32[]{:S(2)}) collective-permute-start(bf16[2,8,16,256]{3,2,1,0:T(8,128)(2,1)} %get-tuple-element.39), channel_id=1, source_target_pairs={{0,16},{4,20},{8,24},{12,28},{16,0},{20,4},{24,8},{28,12},{1,17},{... | collective-permute-start | bytes 393224 | tf_op jit(solution)/shard_map/ppermute | solution.py:45
  55.9 0.1 collective-permute-start.11
  56.0 2.6 %collective-permute-start.12 = (bf16[2,8,16,256]{3,2,1,0:T(8,128)(2,1)}, bf16[2,8,16,256]{3,2,1,0:T(8,128)(2,1)}, u32[]{:S(2)}, u32[]{:S(2)}) collective-permute-start(bf16[2,8,16,256]{3,2,1,0:T(8,128)(2,1)} %get-tuple-element.41), channel_id=1, source_target_pairs={{0,24},{4,28},{8,16},{12,20},{16,8},{20,12},{24,0},{28,4},{1,25},{... | collective-permute-start | bytes 393224 | tf_op jit(solution)/shard_map/ppermute | solution.py:45
  58.6 2.5 %collective-permute-done.8.refs_2_ = bf16[2,8,16,256]{3,2,1,0:T(8,128)(2,1)S(1)} collective-permute-done((bf16[2,8,16,256]{3,2,1,0:T(8,128)(2,1)}, bf16[2,8,16,256]{3,2,1,0:T(8,128)(2,1)S(1)}, u32[]{:S(2)}, u32[]{:S(2)}) %collective-permute-start.8) | collective-permute-done | bytes 131104 | tf_op jit(solution)/shard_map/ppermute | solution.py:45
  61.1 0.9 %collective-permute-start.13 = (bf16[2,8,16,256]{3,2,1,0:T(8,128)(2,1)}, bf16[2,8,16,256]{3,2,1,0:T(8,128)(2,1)}, u32[]{:S(2)}, u32[]{:S(2)}) collective-permute-start(bf16[2,8,16,256]{3,2,1,0:T(8,128)(2,1)} %get-tuple-element.42), channel_id=1, source_target_pairs={{0,28},{4,24},{8,20},{12,16},{16,12},{20,8},{24,4},{28,0},{1,29},{... | collective-permute-start | bytes 393224 | tf_op jit(solution)/shard_map/ppermute | solution.py:45
  62.0 9.6 %all-to-all-done.1 = bf16[32,2,2,16,256]{4,3,2,1,0:T(8,128)(2,1)S(1)} async-done(((bf16[32,2,2,16,256]{4,3,2,1,0:T(8,128)(2,1)}), bf16[32,2,2,16,256]{4,3,2,1,0:T(8,128)(2,1)S(1)}, u32[]{:S(2)}, u32[]{:S(2)}) %all-to-all-start.1) | async-done | bytes 1048608 | tf_op jit(solution)/shard_map/all_to_all | solution.py:58
  71.7 2.3 %shard_map.185.refs_8_ = bf16[2,4,512,256]{3,2,1,0:T(8,128)(2,1)} custom-call(s32[4]{0:T(128)S(1)} %bitcast.12, s32[2]{0:T(128)S(1)} %copy-done.12, bf16[4,512,512]{2,1,0:T(8,128)(2,1)S(1)} %copy-done.1, bf16[8,4,2,2,16,256]{5,4,3,2,1,0:T(8,128)(2,1)S(1)} %bitcast.11), custom_call_target="tpu_custom_call" | custom-call | flops 536870912 | bytes 3145728 | tf_op jit(solution)/shard_map/pallas_call | solution.py:385
  74.0 3.5 %shard_map.186 = bf16[2,4,512,256]{3,2,1,0:T(8,128)(2,1)} custom-call(s32[4]{0:T(128)S(1)} %bitcast.13, s32[2]{0:T(128)S(1)} %copy-done.12, bf16[4,512,512]{2,1,0:T(8,128)(2,1)S(1)} %copy-done.1, bf16[2,8,16,256]{3,2,1,0:T(8,128)(2,1)S(1)} %copy-done.7, bf16[2,8,16,256]{3,2,1,0:T(8,128)(2,1)S(1)} %collective-permute-done.7.refs_1_, ...), custom_call_target="tpu_custom_call", output_to_operand_aliasing={{}: (11, {})} | custom-call | flops 536870912 | bytes 3145728 | tf_op jit(solution)/shard_map/pallas_call | solution.py:385
  (35 shorter events, 0.1 us)
Async XLA Ops:
  0.0 10.5 %copy-start = (bf16[2,16,128,256]{3,2,1,0:T(8,128)(2,1)S(1)}, bf16[2,16,128,256]{3,2,1,0:T(8,128)(2,1)}, u32[]{:S(2)}) copy-start(bf16[2,16,128,256]{3,2,1,0:T(8,128)(2,1)} %param.19) | copy-start | bytes 6291460
  2.9 7.6 %copy-start.10 = (bf16[128,128]{1,0:T(8,128)(2,1)S(1)}, bf16[128,128]{1,0:T(8,128)(2,1)}, u32[]{:S(2)}) copy-start(bf16[128,128]{1,0:T(8,128)(2,1)} %get-tuple-element.26.ends) | copy-start | bytes 98308
  2.9 34.6 %copy-start.2 = (bf16[8,4,9,16,128]{4,3,2,1,0:T(8,128)(2,1)S(1)}, bf16[8,4,9,16,128]{4,3,2,1,0:T(8,128)(2,1)}, u32[]{:S(2)}) copy-start(bf16[8,4,9,16,128]{4,3,2,1,0:T(8,128)(2,1)} %get-tuple-element.24._) | copy-start | bytes 3538948
  2.9 34.6 %copy-start.6 = (bf16[384,256]{1,0:T(8,128)(2,1)S(1)}, bf16[384,256]{1,0:T(8,128)(2,1)}, u32[]{:S(2)}) copy-start(bf16[384,256]{1,0:T(8,128)(2,1)} %constant.29.clone.near) | copy-start | bytes 589828
  2.9 34.6 %copy-start.9 = (f32[2,8,256]{2,1,0:T(8,128)S(1)}, f32[2,8,256]{2,1,0:T(8,128)}, u32[]{:S(2)}) copy-start(f32[2,8,256]{2,1,0:T(8,128)} %constant.28.clone.twiddle) | copy-start | bytes 49156
  2.9 38.8 %all-to-all-start = ((bf16[32,9,16,128]{3,2,1,0:T(8,128)(2,1)}), bf16[32,9,16,128]{3,2,1,0:T(8,128)(2,1)}, u32[]{:S(2)}, u32[]{:S(2)}) async-start(bf16[32,9,16,128]{3,2,1,0:T(8,128)(2,1)} %bitcast.10), calls=%async_computation | async-start | bytes 2359296 | tf_op jit(solution)/shard_map/all_to_all | solution.py:58
  10.4 27.1 %copy-start.3 = (bf16[8,256,256]{2,1,0:T(8,128)(2,1)S(1)}, bf16[8,256,256]{2,1,0:T(8,128)(2,1)}, u32[]{:S(2)}) copy-start(bf16[8,256,256]{2,1,0:T(8,128)(2,1)} %constant.25.clone.order) | copy-start | bytes 3145732
  10.4 27.1 %copy-start.4 = (bf16[512,512]{1,0:T(8,128)(2,1)S(1)}, bf16[512,512]{1,0:T(8,128)(2,1)}, u32[]{:S(2)}) copy-start(bf16[512,512]{1,0:T(8,128)(2,1)} %constant.27.clone.low) | copy-start | bytes 1572868
  10.4 27.1 %copy-start.5 = (bf16[512,512]{1,0:T(8,128)(2,1)S(1)}, bf16[512,512]{1,0:T(8,128)(2,1)}, u32[]{:S(2)}) copy-start(bf16[512,512]{1,0:T(8,128)(2,1)} %constant.26.clone.high) | copy-start | bytes 1572868
  10.5 31.3 %copy-start.11 = (s32[2]{0:T(128)}, s32[2]{0:T(128)S(1)}, u32[]{:S(2)}) copy-start(s32[2]{0:T(128)S(1)} %pad_add_fusion.here) | copy-start | bytes 28
  10.5 1.0 %copy-start.8 = (f32[128,256]{1,0:T(8,128)S(1)}, f32[128,256]{1,0:T(8,128)}, u32[]{:S(2)}) copy-start(f32[128,256]{1,0:T(8,128)} %get-tuple-element.25.smooth) | copy-start | bytes 393220
  12.2 3.7 %collective-permute-start = (bf16[33,16,128]{2,1,0:T(8,128)(2,1)S(1)}, bf16[33,16,128]{2,1,0:T(8,128)(2,1)S(1)}, u32[]{:S(2)}, u32[]{:S(2)}) collective-permute-start(bf16[33,16,128]{2,1,0:T(8,128)(2,1)S(1)} %get-tuple-element.28), channel_id=1, source_target_pairs={{0,4},{4,0},{8,12},{12,8},{16,20},{20,16},{24,28},{28,24},{1,5},{5... | collective-permute-start | bytes 405512 | tf_op jit(solution)/shard_map/ppermute | solution.py:45
  12.5 12.3 %collective-permute-start.1 = (bf16[33,16,128]{2,1,0:T(8,128)(2,1)S(1)}, bf16[33,16,128]{2,1,0:T(8,128)(2,1)S(1)}, u32[]{:S(2)}, u32[]{:S(2)}) collective-permute-start(bf16[33,16,128]{2,1,0:T(8,128)(2,1)S(1)} %get-tuple-element.29), channel_id=1, source_target_pairs={{0,8},{4,12},{8,0},{12,4},{16,24},{20,28},{24,16},{28,20},{1,9},{5... | collective-permute-start | bytes 405512 | tf_op jit(solution)/shard_map/ppermute | solution.py:45
  14.2 13.4 %collective-permute-start.2 = (bf16[33,16,128]{2,1,0:T(8,128)(2,1)S(1)}, bf16[33,16,128]{2,1,0:T(8,128)(2,1)S(1)}, u32[]{:S(2)}, u32[]{:S(2)}) collective-permute-start(bf16[33,16,128]{2,1,0:T(8,128)(2,1)S(1)} %get-tuple-element.30), channel_id=1, source_target_pairs={{0,12},{4,8},{8,4},{12,0},{16,28},{20,24},{24,20},{28,16},{1,13},{... | collective-permute-start | bytes 405512 | tf_op jit(solution)/shard_map/ppermute | solution.py:45
  14.2 13.4 %collective-permute-start.3 = (bf16[33,16,128]{2,1,0:T(8,128)(2,1)S(1)}, bf16[33,16,128]{2,1,0:T(8,128)(2,1)S(1)}, u32[]{:S(2)}, u32[]{:S(2)}) collective-permute-start(bf16[33,16,128]{2,1,0:T(8,128)(2,1)S(1)} %get-tuple-element.31), channel_id=1, source_target_pairs={{0,16},{4,20},{8,24},{12,28},{16,0},{20,4},{24,8},{28,12},{1,17},{... | collective-permute-start | bytes 405512 | tf_op jit(solution)/shard_map/ppermute | solution.py:45
  15.9 12.6 %collective-permute-start.4 = (bf16[33,16,128]{2,1,0:T(8,128)(2,1)S(1)}, bf16[33,16,128]{2,1,0:T(8,128)(2,1)S(1)}, u32[]{:S(2)}, u32[]{:S(2)}) collective-permute-start(bf16[33,16,128]{2,1,0:T(8,128)(2,1)S(1)} %get-tuple-element.32), channel_id=1, source_target_pairs={{0,20},{4,16},{8,28},{12,24},{16,4},{20,0},{24,12},{28,8},{1,21},{... | collective-permute-start | bytes 405512 | tf_op jit(solution)/shard_map/ppermute | solution.py:45
  16.0 18.6 %collective-permute-start.5 = (bf16[33,16,128]{2,1,0:T(8,128)(2,1)S(1)}, bf16[33,16,128]{2,1,0:T(8,128)(2,1)S(1)}, u32[]{:S(2)}, u32[]{:S(2)}) collective-permute-start(bf16[33,16,128]{2,1,0:T(8,128)(2,1)S(1)} %get-tuple-element.33), channel_id=1, source_target_pairs={{0,24},{4,28},{8,16},{12,20},{16,8},{20,12},{24,0},{28,4},{1,25},{... | collective-permute-start | bytes 405512 | tf_op jit(solution)/shard_map/ppermute | solution.py:45
  24.8 12.7 %collective-permute-start.6 = (bf16[33,16,128]{2,1,0:T(8,128)(2,1)S(1)}, bf16[33,16,128]{2,1,0:T(8,128)(2,1)S(1)}, u32[]{:S(2)}, u32[]{:S(2)}) collective-permute-start(bf16[33,16,128]{2,1,0:T(8,128)(2,1)S(1)} %get-tuple-element.34), channel_id=1, source_target_pairs={{0,28},{4,24},{8,20},{12,16},{16,12},{20,8},{24,4},{28,0},{1,29},{... | collective-permute-start | bytes 405512 | tf_op jit(solution)/shard_map/ppermute | solution.py:45
  41.7 29.9 %all-to-all-start.1 = ((bf16[32,2,2,16,256]{4,3,2,1,0:T(8,128)(2,1)}), bf16[32,2,2,16,256]{4,3,2,1,0:T(8,128)(2,1)S(1)}, u32[]{:S(2)}, u32[]{:S(2)}) async-start(bf16[32,2,2,16,256]{4,3,2,1,0:T(8,128)(2,1)} %bitcast.6), calls=%async_computation.1 | async-start | bytes 2097152 | tf_op jit(solution)/shard_map/all_to_all | solution.py:58
  46.6 25.1 %copy-start.1 = (bf16[4,512,512]{2,1,0:T(8,128)(2,1)S(1)}, bf16[4,512,512]{2,1,0:T(8,128)(2,1)}, u32[]{:S(2)}) copy-start(bf16[4,512,512]{2,1,0:T(8,128)(2,1)} %bank.3) | copy-start | bytes 6291460
  46.6 25.1 %copy-start.12 = (s32[2]{0:T(128)S(1)}, s32[2]{0:T(128)}, u32[]{:S(2)}) copy-start(s32[2]{0:T(128)} %copy-done.11) | copy-start | bytes 28
  46.6 25.0 %copy-start.13 = (s32[4,1]{0,1:T(1,128)S(1)}, s32[4,1]{0,1:T(1,128)}, u32[]{:S(2)}) copy-start(s32[4,1]{0,1:T(1,128)} %param.24) | copy-start | bytes 52
  52.3 3.7 %collective-permute-start.7 = (bf16[2,8,16,256]{3,2,1,0:T(8,128)(2,1)}, bf16[2,8,16,256]{3,2,1,0:T(8,128)(2,1)S(1)}, u32[]{:S(2)}, u32[]{:S(2)}) collective-permute-start(bf16[2,8,16,256]{3,2,1,0:T(8,128)(2,1)} %get-tuple-element.36), channel_id=1, source_target_pairs={{0,4},{4,0},{8,12},{12,8},{16,20},{20,16},{24,28},{28,24},{1,5},{5... | collective-permute-start | bytes 393224 | tf_op jit(solution)/shard_map/ppermute | solution.py:45
  52.5 8.6 %collective-permute-start.8 = (bf16[2,8,16,256]{3,2,1,0:T(8,128)(2,1)}, bf16[2,8,16,256]{3,2,1,0:T(8,128)(2,1)S(1)}, u32[]{:S(2)}, u32[]{:S(2)}) collective-permute-start(bf16[2,8,16,256]{3,2,1,0:T(8,128)(2,1)} %get-tuple-element.37), channel_id=1, source_target_pairs={{0,8},{4,12},{8,0},{12,4},{16,24},{20,28},{24,16},{28,20},{1,9},{5... | collective-permute-start | bytes 393224 | tf_op jit(solution)/shard_map/ppermute | solution.py:45
  54.2 19.7 %collective-permute-start.9 = (bf16[2,8,16,256]{3,2,1,0:T(8,128)(2,1)}, bf16[2,8,16,256]{3,2,1,0:T(8,128)(2,1)S(1)}, u32[]{:S(2)}, u32[]{:S(2)}) collective-permute-start(bf16[2,8,16,256]{3,2,1,0:T(8,128)(2,1)} %get-tuple-element.38), channel_id=1, source_target_pairs={{0,12},{4,8},{8,4},{12,0},{16,28},{20,24},{24,20},{28,16},{1,13},{... | collective-permute-start | bytes 393224 | tf_op jit(solution)/shard_map/ppermute | solution.py:45
  54.2 19.7 %collective-permute-start.10 = (bf16[2,8,16,256]{3,2,1,0:T(8,128)(2,1)}, bf16[2,8,16,256]{3,2,1,0:T(8,128)(2,1)}, u32[]{:S(2)}, u32[]{:S(2)}) collective-permute-start(bf16[2,8,16,256]{3,2,1,0:T(8,128)(2,1)} %get-tuple-element.39), channel_id=1, source_target_pairs={{0,16},{4,20},{8,24},{12,28},{16,0},{20,4},{24,8},{28,12},{1,17},{... | collective-permute-start | bytes 393224 | tf_op jit(solution)/shard_map/ppermute | solution.py:45
  55.9 18.0 %collective-permute-start.11 = (bf16[2,8,16,256]{3,2,1,0:T(8,128)(2,1)}, bf16[2,8,16,256]{3,2,1,0:T(8,128)(2,1)}, u32[]{:S(2)}, u32[]{:S(2)}) collective-permute-start(bf16[2,8,16,256]{3,2,1,0:T(8,128)(2,1)} %get-tuple-element.40), channel_id=1, source_target_pairs={{0,20},{4,16},{8,28},{12,24},{16,4},{20,0},{24,12},{28,8},{1,21},{... | collective-permute-start | bytes 393224 | tf_op jit(solution)/shard_map/ppermute | solution.py:45
  56.0 17.9 %collective-permute-start.12 = (bf16[2,8,16,256]{3,2,1,0:T(8,128)(2,1)}, bf16[2,8,16,256]{3,2,1,0:T(8,128)(2,1)}, u32[]{:S(2)}, u32[]{:S(2)}) collective-permute-start(bf16[2,8,16,256]{3,2,1,0:T(8,128)(2,1)} %get-tuple-element.41), channel_id=1, source_target_pairs={{0,24},{4,28},{8,16},{12,20},{16,8},{20,12},{24,0},{28,4},{1,25},{... | collective-permute-start | bytes 393224 | tf_op jit(solution)/shard_map/ppermute | solution.py:45
  61.1 12.8 %collective-permute-start.13 = (bf16[2,8,16,256]{3,2,1,0:T(8,128)(2,1)}, bf16[2,8,16,256]{3,2,1,0:T(8,128)(2,1)}, u32[]{:S(2)}, u32[]{:S(2)}) collective-permute-start(bf16[2,8,16,256]{3,2,1,0:T(8,128)(2,1)} %get-tuple-element.42), channel_id=1, source_target_pairs={{0,28},{4,24},{8,20},{12,16},{16,12},{20,8},{24,4},{28,0},{1,29},{... | collective-permute-start | bytes 393224 | tf_op jit(solution)/shard_map/ppermute | solution.py:45
  71.7 2.3 %copy-start.7 = (bf16[2,8,16,256]{3,2,1,0:T(8,128)(2,1)S(1)}, bf16[2,8,16,256]{3,2,1,0:T(8,128)(2,1)}, u32[]{:S(2)}) copy-start(bf16[2,8,16,256]{3,2,1,0:T(8,128)(2,1)} %get-tuple-element.35.refs_0_) | copy-start | bytes 393220

commit v5 on v4

--- a/solution.py
+++ b/solution.py
@@ -45,11 +45,14 @@
     return lax.ppermute(value, axis, [(i, i ^ k) for i in range(size)])
 
 
-def exchange(blocks, axis):
-    order = sorted(range(1, len(blocks)), key=lambda k: (-bin(k >> 1).count("1"), k))
+def exchange(blocks, axis, core_last=False):
+    order = sorted(range(1, len(blocks)), key=lambda k: (k == 1, -bin(k >> 1).count("1"), k))
     moved = {0: blocks[0]}
     for k in order:
-        moved[k] = swap(blocks[k], axis, k)
+        block = blocks[k]
+        if core_last and k == 1:
+            block, moved[order[0]] = lax.optimization_barrier((block, moved[order[0]]))
+        moved[k] = swap(block, axis, k)
     return [moved[k] for k in range(len(blocks))]
 
 
@@ -346,6 +349,22 @@
     )(here, after, *tables, *blocks)
 
 
+def copy_kernel(source, target):
+    target[...] = source[...]
+
+
+def hold(array):
+    return pl.pallas_call(
+        copy_kernel,
+        grid=(1,),
+        out_shape=jax.ShapeDtypeStruct(array.shape, array.dtype),
+        in_specs=[fixed(array)],
+        out_specs=WHOLE,
+        compiler_params=params(),
+        cost_estimate=cost(0, [array, array]),
+    )(array)
+
+
 def filter_kernel(classes, here, bank, *refs, count, packed, aliased):
     ins, out, lined = refs[:count], refs[count + aliased], refs[-1]
     b = pl.program_id(0)
@@ -429,10 +448,12 @@
     late = exchange_both(late_out)
     early_out = transform_call(here, late_out, early, by_both, True)
     early = exchange_both(early_out[0])
-    late_out = transform_call(here, early_out[0], [late], by_both, False)
-    late = exchange(late_out, "tm")
-    filtered = delay_filter(classes, here, filter_bank, [early], 0, hb, out_shape, None, True)
-    return delay_filter(classes, here, filter_bank, late, 1, hb, out_shape, filtered, False)
+    late_out = list(transform_call(here, early_out[0], [late], by_both, False))
+    own = hold(late_out[0])
+    late_out[1], own = lax.optimization_barrier((late_out[1], own))
+    late = [own] + exchange(late_out, "tm", core_last=True)[1:]
+    filtered = delay_filter(classes, here, filter_bank, late, 1, hb, out_shape, None, False)
+    return delay_filter(classes, here, filter_bank, [early], 0, hb, out_shape, filtered, True)
 
 
 def solution(mesh):

time: 78.8 us -> 77.9 us (0.989); the launches traced: 77.4 us -> 77.5 us
  Pallas kernels: 19.2 us -> 18.1 us
  local copies, waits for them, and re-layouts: 1.1 us -> 2 us
    all_to_all x2, waiting for transfers between devices: 9.65 us -> 0.01 us  [exchange_both(): lax.all_to_all(flat, ('tm', 'freq'), 0, 0, tiled=True).reshape(packed.shape)]
    ppermute x14, waiting for transfers between devices: 21.4 us -> 30.9 us  [swap(): return lax.ppermute(value, axis, [(i, i ^ k) for i in range(size)])]
    pallas_call x2, Pallas kernels: 5.71 us -> 4.62 us  [delay_filter(): pl.pallas_call(functools.partial(filter_kernel, count=len(blocks), packed...]
    unnamed x28, local copies, waits for them, and re-layouts: 1.1 us -> 2 us
  transfers between devices with their start and end apart: 16 -> 16, of which waited for: 7 -> 9; matrix products, arithmetic and copies ran while one was open for 0% -> 0% of each run, Pallas kernels for 17% -> 17%
where the time goes in v5:
time: 77.9 us; the launch traced here: 77.5 us
  waiting for transfers between devices  30.9 us (40%)
  starting transfers between devices  26.3 us (34%)
  Pallas kernels  18.1 us (23%)
  local copies, waits for them, and re-layouts  2 us (3%)
    ppermute x14, waiting for transfers between devices, swap(): return lax.ppermute(value, axis, [(i, i ^ k) for i in range(size)])  30.9 us
    ppermute x14, starting transfers between devices, swap(): return lax.ppermute(value, axis, [(i, i ^ k) for i in range(size)])  14 us
    all_to_all x2, starting transfers between devices, exchange_both(): lax.all_to_all(flat, ('tm', 'freq'), 0, 0, tiled=True).reshape(packed.shape)  12.3 us
    pallas_call x2, Pallas kernels, transform_call(): pl.pallas_call(functools.partial(transform, n=n, first=first, hb=hb), gri...  9.84 us
    pallas_call x2, Pallas kernels, delay_filter(): pl.pallas_call(functools.partial(filter_kernel, count=len(blocks), packed...  4.62 us
    pallas_call x1, Pallas kernels, weigh(): pl.pallas_call(weigh_by_both, grid=(z_count // zs,), out_shape=[out, smoo...  2.87 us
    unnamed x28, local copies, waits for them, and re-layouts  2 us
  transfers between devices with their start and end apart: 16, of which 9 were waited for; matrix products, arithmetic and copies ran while one was open for 0% of the time, Pallas kernels for 17%

profile of v5, /device:TPU:0, one launch (start us, length us, event | category | flops | bytes accessed | tf_op | source)
XLA Modules:
  0.0 77.5 jit_solution(11659824297689472892)
XLA Ops:
  0.0 2.9 %shard_map.181 = (bf16[8,4,9,16,128]{4,3,2,1,0:T(8,128)(2,1)}, f32[128,256]{1,0:T(8,128)}, bf16[128,128]{1,0:T(8,128)(2,1)}) custom-call(bf16[2,4,2,2,128,256]{5,4,3,2,1,0:T(8,128)(2,1)} %bitcast.8, f32[128,256]{1,0:T(8,128)} %power.1, f32[128,256]{1,0:T(8,128)} %square.1, s32[128,256]{1,0:T(8,128)} %count.1, s32[128,256]{1,0:T(8,128)} %mask.1, ...), custom_call_target="tpu_custom_call" | custom-call | bytes 2359296 | tf_op jit(solution)/shard_map/pallas_call | solution.py:134
  2.9 7.4 %all-to-all-start.1 = ((bf16[32,9,16,128]{3,2,1,0:T(8,128)(2,1)}), bf16[32,9,16,128]{3,2,1,0:T(8,128)(2,1)}, u32[]{:S(2)}, u32[]{:S(2)}) async-start(bf16[32,9,16,128]{3,2,1,0:T(8,128)(2,1)} %bitcast.10), calls=%async_computation.1 | async-start | bytes 2359296 | tf_op jit(solution)/shard_map/all_to_all | solution.py:61
  10.4 0.1 pad_add_fusion.here
  10.5 1.0 %copy-done.7 = f32[128,256]{1,0:T(8,128)S(1)} copy-done((f32[128,256]{1,0:T(8,128)S(1)}, f32[128,256]{1,0:T(8,128)}, u32[]{:S(2)}) %copy-start.7) | copy-done | bytes 131096
  11.5 0.7 shard_map.182
  12.2 0.3 collective-permute-start
  12.5 1.7 %collective-permute-start.1 = (bf16[33,16,128]{2,1,0:T(8,128)(2,1)S(1)}, bf16[33,16,128]{2,1,0:T(8,128)(2,1)S(1)}, u32[]{:S(2)}, u32[]{:S(2)}) collective-permute-start(bf16[33,16,128]{2,1,0:T(8,128)(2,1)S(1)} %get-tuple-element.33), channel_id=1, source_target_pairs={{0,8},{4,12},{8,0},{12,4},{16,24},{20,28},{24,16},{28,20},{1,9},{5... | collective-permute-start | bytes 405512 | tf_op jit(solution)/shard_map/ppermute | solution.py:45
  14.2 1.7 %collective-permute-start.3 = (bf16[33,16,128]{2,1,0:T(8,128)(2,1)S(1)}, bf16[33,16,128]{2,1,0:T(8,128)(2,1)S(1)}, u32[]{:S(2)}, u32[]{:S(2)}) collective-permute-start(bf16[33,16,128]{2,1,0:T(8,128)(2,1)S(1)} %get-tuple-element.35), channel_id=1, source_target_pairs={{0,16},{4,20},{8,24},{12,28},{16,0},{20,4},{24,8},{28,12},{1,17},{... | collective-permute-start | bytes 405512 | tf_op jit(solution)/shard_map/ppermute | solution.py:45
  15.9 0.1 collective-permute-start.4
  16.0 2.6 %collective-permute-start.5 = (bf16[33,16,128]{2,1,0:T(8,128)(2,1)S(1)}, bf16[33,16,128]{2,1,0:T(8,128)(2,1)S(1)}, u32[]{:S(2)}, u32[]{:S(2)}) collective-permute-start(bf16[33,16,128]{2,1,0:T(8,128)(2,1)S(1)} %get-tuple-element.37), channel_id=1, source_target_pairs={{0,24},{4,28},{8,16},{12,20},{16,8},{20,12},{24,0},{28,4},{1,25},{... | collective-permute-start | bytes 405512 | tf_op jit(solution)/shard_map/ppermute | solution.py:45
  18.6 6.2 %collective-permute-done.1.refs_2_ = bf16[33,16,128]{2,1,0:T(8,128)(2,1)S(1)} collective-permute-done((bf16[33,16,128]{2,1,0:T(8,128)(2,1)S(1)}, bf16[33,16,128]{2,1,0:T(8,128)(2,1)S(1)}, u32[]{:S(2)}, u32[]{:S(2)}) %collective-permute-start.1) | collective-permute-done | bytes 135200 | tf_op jit(solution)/shard_map/ppermute | solution.py:45
  24.8 0.1 collective-permute-start.6
  24.8 2.8 %collective-permute-done.2.refs_3_ = bf16[33,16,128]{2,1,0:T(8,128)(2,1)S(1)} collective-permute-done((bf16[33,16,128]{2,1,0:T(8,128)(2,1)S(1)}, bf16[33,16,128]{2,1,0:T(8,128)(2,1)S(1)}, u32[]{:S(2)}, u32[]{:S(2)}) %collective-permute-start.2) | collective-permute-done | bytes 135200 | tf_op jit(solution)/shard_map/ppermute | solution.py:45
  27.6 0.8 %collective-permute-done.4.refs_5_ = bf16[33,16,128]{2,1,0:T(8,128)(2,1)S(1)} collective-permute-done((bf16[33,16,128]{2,1,0:T(8,128)(2,1)S(1)}, bf16[33,16,128]{2,1,0:T(8,128)(2,1)S(1)}, u32[]{:S(2)}, u32[]{:S(2)}) %collective-permute-start.4) | collective-permute-done | bytes 135200 | tf_op jit(solution)/shard_map/ppermute | solution.py:45
  28.4 6.2 %collective-permute-done.5.refs_6_ = bf16[33,16,128]{2,1,0:T(8,128)(2,1)S(1)} collective-permute-done((bf16[33,16,128]{2,1,0:T(8,128)(2,1)S(1)}, bf16[33,16,128]{2,1,0:T(8,128)(2,1)S(1)}, u32[]{:S(2)}, u32[]{:S(2)}) %collective-permute-start.5) | collective-permute-done | bytes 135200 | tf_op jit(solution)/shard_map/ppermute | solution.py:45
  34.6 2.9 %collective-permute-done.6.refs_7_ = bf16[33,16,128]{2,1,0:T(8,128)(2,1)S(1)} collective-permute-done((bf16[33,16,128]{2,1,0:T(8,128)(2,1)S(1)}, bf16[33,16,128]{2,1,0:T(8,128)(2,1)S(1)}, u32[]{:S(2)}, u32[]{:S(2)}) %collective-permute-start.6) | collective-permute-done | bytes 135200 | tf_op jit(solution)/shard_map/ppermute | solution.py:45
  37.5 4.2 %shard_map.183._ = bf16[8,4,2,2,16,256]{5,4,3,2,1,0:T(8,128)(2,1)} custom-call(s32[2]{0:T(128)S(1)} %pad_add_fusion.here, bf16[8,4,9,16,128]{4,3,2,1,0:T(8,128)(2,1)S(1)} %copy-done.2, bf16[8,256,256]{2,1,0:T(8,128)(2,1)S(1)} %copy-done.3, bf16[512,512]{1,0:T(8,128)(2,1)S(1)} %copy-done.5, bf16[512,512]{1,0:T(8,128)(2,1)S(1)} %copy-done.4, ...), custom_call_target="tpu_custom_call" | custom-call | flops 1073741824 | bytes 2129920 | tf_op jit(solution)/shard_map/pallas_call | solution.py:332
  41.7 4.9 %all-to-all-start = ((bf16[32,2,2,16,256]{4,3,2,1,0:T(8,128)(2,1)}), bf16[32,2,2,16,256]{4,3,2,1,0:T(8,128)(2,1)S(1)}, u32[]{:S(2)}, u32[]{:S(2)}) async-start(bf16[32,2,2,16,256]{4,3,2,1,0:T(8,128)(2,1)} %bitcast.4), calls=%async_computation | async-start | bytes 2097152 | tf_op jit(solution)/shard_map/all_to_all | solution.py:61
  46.6 5.6 %shard_map.184 = (bf16[2,8,16,256]{3,2,1,0:T(8,128)(2,1)}, bf16[2,8,16,256]{3,2,1,0:T(8,128)(2,1)}, bf16[2,8,16,256]{3,2,1,0:T(8,128)(2,1)}, bf16[2,8,16,256]{3,...) custom-call(s32[2]{0:T(128)} %copy-done.11, ...), custom_call_target="tpu_custom_call" | custom-call | flops 1073741824 | bytes 2228224 | tf_op jit(solution)/shard_map/pallas_call | solution.py:332
  52.3 2.7 %collective-permute-start.7 = (bf16[2,8,16,256]{3,2,1,0:T(8,128)(2,1)}, bf16[2,8,16,256]{3,2,1,0:T(8,128)(2,1)S(1)}, u32[]{:S(2)}, u32[]{:S(2)}) collective-permute-start(bf16[2,8,16,256]{3,2,1,0:T(8,128)(2,1)} %get-tuple-element.43), channel_id=1, source_target_pairs={{0,24},{4,28},{8,16},{12,20},{16,8},{20,12},{24,0},{28,4},{1,25},{... | collective-permute-start | bytes 393224 | tf_op jit(solution)/shard_map/ppermute | solution.py:45
  54.9 0.6 collective-permute-start.9
  55.5 0.9 %copy-done.8 = bf16[2,8,16,256]{3,2,1,0:T(8,128)(2,1)S(1)} copy-done((bf16[2,8,16,256]{3,2,1,0:T(8,128)(2,1)S(1)}, bf16[2,8,16,256]{3,2,1,0:T(8,128)(2,1)}, u32[]{:S(2)}) %copy-start.8) | copy-done | bytes 131096
  56.4 0.7 collective-permute-start.10
  57.1 0.6 collective-permute-start.11
  57.7 1.7 %collective-permute-start.12 = (bf16[2,8,16,256]{3,2,1,0:T(8,128)(2,1)}, bf16[2,8,16,256]{3,2,1,0:T(8,128)(2,1)S(1)}, u32[]{:S(2)}, u32[]{:S(2)}) collective-permute-start(bf16[2,8,16,256]{3,2,1,0:T(8,128)(2,1)} %get-tuple-element.48), channel_id=1, source_target_pairs={{0,20},{4,16},{8,28},{12,24},{16,4},{20,0},{24,12},{28,8},{1,21},{... | collective-permute-start | bytes 393224 | tf_op jit(solution)/shard_map/ppermute | solution.py:45
  59.4 2.7 %collective-permute-done.7.refs_6_ = bf16[2,8,16,256]{3,2,1,0:T(8,128)(2,1)S(1)} collective-permute-done((bf16[2,8,16,256]{3,2,1,0:T(8,128)(2,1)}, bf16[2,8,16,256]{3,2,1,0:T(8,128)(2,1)S(1)}, u32[]{:S(2)}, u32[]{:S(2)}) %collective-permute-start.7) | collective-permute-done | bytes 131104 | tf_op jit(solution)/shard_map/ppermute | solution.py:45
  62.1 1.3 %collective-permute-start.13 = (bf16[2,8,16,256]{3,2,1,0:T(8,128)(2,1)}, bf16[2,8,16,256]{3,2,1,0:T(8,128)(2,1)S(1)}, u32[]{:S(2)}, u32[]{:S(2)}) collective-permute-start(bf16[2,8,16,256]{3,2,1,0:T(8,128)(2,1)} %get-tuple-element.50), channel_id=1, source_target_pairs={{0,28},{4,24},{8,20},{12,16},{16,12},{20,8},{24,4},{28,0},{1,29},{... | collective-permute-start | bytes 393224 | tf_op jit(solution)/shard_map/ppermute | solution.py:45
  63.5 2.8 %collective-permute-done.9.refs_2_ = bf16[2,8,16,256]{3,2,1,0:T(8,128)(2,1)S(1)} collective-permute-done((bf16[2,8,16,256]{3,2,1,0:T(8,128)(2,1)}, bf16[2,8,16,256]{3,2,1,0:T(8,128)(2,1)S(1)}, u32[]{:S(2)}, u32[]{:S(2)}) %collective-permute-start.9) | collective-permute-done | bytes 131104 | tf_op jit(solution)/shard_map/ppermute | solution.py:45
  66.2 2.5 %collective-permute-done.10.refs_3_ = bf16[2,8,16,256]{3,2,1,0:T(8,128)(2,1)S(1)} collective-permute-done((bf16[2,8,16,256]{3,2,1,0:T(8,128)(2,1)}, bf16[2,8,16,256]{3,2,1,0:T(8,128)(2,1)S(1)}, u32[]{:S(2)}, u32[]{:S(2)}) %collective-permute-start.10) | collective-permute-done | bytes 131104 | tf_op jit(solution)/shard_map/ppermute | solution.py:45
  68.8 4.1 %collective-permute-done.13.refs_7_ = bf16[2,8,16,256]{3,2,1,0:T(8,128)(2,1)S(1)} collective-permute-done((bf16[2,8,16,256]{3,2,1,0:T(8,128)(2,1)}, bf16[2,8,16,256]{3,2,1,0:T(8,128)(2,1)S(1)}, u32[]{:S(2)}, u32[]{:S(2)}) %collective-permute-start.13) | collective-permute-done | bytes 131104 | tf_op jit(solution)/shard_map/ppermute | solution.py:45
  72.9 2.4 %shard_map.186.refs_1_ = bf16[2,4,512,256]{3,2,1,0:T(8,128)(2,1)} custom-call(s32[4]{0:T(128)S(1)} %bitcast.12, s32[2]{0:T(128)S(1)} %copy-done.12, bf16[4,512,512]{2,1,0:T(8,128)(2,1)S(1)} %copy-done.1, bf16[2,8,16,256]{3,2,1,0:T(8,128)(2,1)S(1)} %shard_map.185.refs_0_, bf16[2,8,16,256]{3,2,1,0:T(8,128)(2,1)S(1)} %collective-permute-done.8.refs_1_, ...), custom_call_target="tpu_custom_call" | custom-call | flops 536870912 | bytes 3145728 | tf_op jit(solution)/shard_map/pallas_call | solution.py:404
  75.2 2.3 %shard_map.187 = bf16[2,4,512,256]{3,2,1,0:T(8,128)(2,1)} custom-call(s32[4]{0:T(128)S(1)} %bitcast.13, s32[2]{0:T(128)S(1)} %copy-done.12, bf16[4,512,512]{2,1,0:T(8,128)(2,1)S(1)} %copy-done.1, bf16[8,4,2,2,16,256]{5,4,3,2,1,0:T(8,128)(2,1)S(1)} %bitcast.11, bf16[2,4,512,256]{3,2,1,0:T(8,128)(2,1)} %shard_map.186.refs_1_), custom_call_target="tpu_custom_call", output_to_operand_aliasing={{}: (4, {})} | custom-call | flops 536870912 | bytes 3145728 | tf_op jit(solution)/shard_map/pallas_call | solution.py:404
  (36 shorter events, 0.1 us)
Async XLA Ops:
  0.0 10.5 %copy-start = (bf16[2,16,128,256]{3,2,1,0:T(8,128)(2,1)S(1)}, bf16[2,16,128,256]{3,2,1,0:T(8,128)(2,1)}, u32[]{:S(2)}) copy-start(bf16[2,16,128,256]{3,2,1,0:T(8,128)(2,1)} %param.19) | copy-start | bytes 6291460
  2.9 7.6 %copy-start.10 = (bf16[128,128]{1,0:T(8,128)(2,1)S(1)}, bf16[128,128]{1,0:T(8,128)(2,1)}, u32[]{:S(2)}) copy-start(bf16[128,128]{1,0:T(8,128)(2,1)} %get-tuple-element.30.ends) | copy-start | bytes 98308
  2.9 34.6 %copy-start.2 = (bf16[8,4,9,16,128]{4,3,2,1,0:T(8,128)(2,1)S(1)}, bf16[8,4,9,16,128]{4,3,2,1,0:T(8,128)(2,1)}, u32[]{:S(2)}) copy-start(bf16[8,4,9,16,128]{4,3,2,1,0:T(8,128)(2,1)} %get-tuple-element.28._) | copy-start | bytes 3538948
  2.9 34.6 %copy-start.6 = (bf16[384,256]{1,0:T(8,128)(2,1)S(1)}, bf16[384,256]{1,0:T(8,128)(2,1)}, u32[]{:S(2)}) copy-start(bf16[384,256]{1,0:T(8,128)(2,1)} %constant.29.clone.near) | copy-start | bytes 589828
  2.9 34.6 %copy-start.9 = (f32[2,8,256]{2,1,0:T(8,128)S(1)}, f32[2,8,256]{2,1,0:T(8,128)}, u32[]{:S(2)}) copy-start(f32[2,8,256]{2,1,0:T(8,128)} %constant.28.clone.twiddle) | copy-start | bytes 49156
  2.9 38.8 %all-to-all-start.1 = ((bf16[32,9,16,128]{3,2,1,0:T(8,128)(2,1)}), bf16[32,9,16,128]{3,2,1,0:T(8,128)(2,1)}, u32[]{:S(2)}, u32[]{:S(2)}) async-start(bf16[32,9,16,128]{3,2,1,0:T(8,128)(2,1)} %bitcast.10), calls=%async_computation.1 | async-start | bytes 2359296 | tf_op jit(solution)/shard_map/all_to_all | solution.py:61
  10.4 27.1 %copy-start.3 = (bf16[8,256,256]{2,1,0:T(8,128)(2,1)S(1)}, bf16[8,256,256]{2,1,0:T(8,128)(2,1)}, u32[]{:S(2)}) copy-start(bf16[8,256,256]{2,1,0:T(8,128)(2,1)} %constant.25.clone.order) | copy-start | bytes 3145732
  10.4 27.1 %copy-start.4 = (bf16[512,512]{1,0:T(8,128)(2,1)S(1)}, bf16[512,512]{1,0:T(8,128)(2,1)}, u32[]{:S(2)}) copy-start(bf16[512,512]{1,0:T(8,128)(2,1)} %constant.27.clone.low) | copy-start | bytes 1572868
  10.4 27.1 %copy-start.5 = (bf16[512,512]{1,0:T(8,128)(2,1)S(1)}, bf16[512,512]{1,0:T(8,128)(2,1)}, u32[]{:S(2)}) copy-start(bf16[512,512]{1,0:T(8,128)(2,1)} %constant.26.clone.high) | copy-start | bytes 1572868
  10.5 31.3 %copy-start.11 = (s32[2]{0:T(128)}, s32[2]{0:T(128)S(1)}, u32[]{:S(2)}) copy-start(s32[2]{0:T(128)S(1)} %pad_add_fusion.here) | copy-start | bytes 28
  10.5 1.0 %copy-start.7 = (f32[128,256]{1,0:T(8,128)S(1)}, f32[128,256]{1,0:T(8,128)}, u32[]{:S(2)}) copy-start(f32[128,256]{1,0:T(8,128)} %get-tuple-element.29.smooth) | copy-start | bytes 393220
  12.2 3.7 %collective-permute-start = (bf16[33,16,128]{2,1,0:T(8,128)(2,1)S(1)}, bf16[33,16,128]{2,1,0:T(8,128)(2,1)S(1)}, u32[]{:S(2)}, u32[]{:S(2)}) collective-permute-start(bf16[33,16,128]{2,1,0:T(8,128)(2,1)S(1)} %get-tuple-element.32), channel_id=1, source_target_pairs={{0,4},{4,0},{8,12},{12,8},{16,20},{20,16},{24,28},{28,24},{1,5},{5... | collective-permute-start | bytes 405512 | tf_op jit(solution)/shard_map/ppermute | solution.py:45
  12.5 12.3 %collective-permute-start.1 = (bf16[33,16,128]{2,1,0:T(8,128)(2,1)S(1)}, bf16[33,16,128]{2,1,0:T(8,128)(2,1)S(1)}, u32[]{:S(2)}, u32[]{:S(2)}) collective-permute-start(bf16[33,16,128]{2,1,0:T(8,128)(2,1)S(1)} %get-tuple-element.33), channel_id=1, source_target_pairs={{0,8},{4,12},{8,0},{12,4},{16,24},{20,28},{24,16},{28,20},{1,9},{5... | collective-permute-start | bytes 405512 | tf_op jit(solution)/shard_map/ppermute | solution.py:45
  14.2 13.4 %collective-permute-start.2 = (bf16[33,16,128]{2,1,0:T(8,128)(2,1)S(1)}, bf16[33,16,128]{2,1,0:T(8,128)(2,1)S(1)}, u32[]{:S(2)}, u32[]{:S(2)}) collective-permute-start(bf16[33,16,128]{2,1,0:T(8,128)(2,1)S(1)} %get-tuple-element.34), channel_id=1, source_target_pairs={{0,12},{4,8},{8,4},{12,0},{16,28},{20,24},{24,20},{28,16},{1,13},{... | collective-permute-start | bytes 405512 | tf_op jit(solution)/shard_map/ppermute | solution.py:45
  14.2 13.4 %collective-permute-start.3 = (bf16[33,16,128]{2,1,0:T(8,128)(2,1)S(1)}, bf16[33,16,128]{2,1,0:T(8,128)(2,1)S(1)}, u32[]{:S(2)}, u32[]{:S(2)}) collective-permute-start(bf16[33,16,128]{2,1,0:T(8,128)(2,1)S(1)} %get-tuple-element.35), channel_id=1, source_target_pairs={{0,16},{4,20},{8,24},{12,28},{16,0},{20,4},{24,8},{28,12},{1,17},{... | collective-permute-start | bytes 405512 | tf_op jit(solution)/shard_map/ppermute | solution.py:45
  15.9 12.6 %collective-permute-start.4 = (bf16[33,16,128]{2,1,0:T(8,128)(2,1)S(1)}, bf16[33,16,128]{2,1,0:T(8,128)(2,1)S(1)}, u32[]{:S(2)}, u32[]{:S(2)}) collective-permute-start(bf16[33,16,128]{2,1,0:T(8,128)(2,1)S(1)} %get-tuple-element.36), channel_id=1, source_target_pairs={{0,20},{4,16},{8,28},{12,24},{16,4},{20,0},{24,12},{28,8},{1,21},{... | collective-permute-start | bytes 405512 | tf_op jit(solution)/shard_map/ppermute | solution.py:45
  16.0 18.6 %collective-permute-start.5 = (bf16[33,16,128]{2,1,0:T(8,128)(2,1)S(1)}, bf16[33,16,128]{2,1,0:T(8,128)(2,1)S(1)}, u32[]{:S(2)}, u32[]{:S(2)}) collective-permute-start(bf16[33,16,128]{2,1,0:T(8,128)(2,1)S(1)} %get-tuple-element.37), channel_id=1, source_target_pairs={{0,24},{4,28},{8,16},{12,20},{16,8},{20,12},{24,0},{28,4},{1,25},{... | collective-permute-start | bytes 405512 | tf_op jit(solution)/shard_map/ppermute | solution.py:45
  24.8 12.7 %collective-permute-start.6 = (bf16[33,16,128]{2,1,0:T(8,128)(2,1)S(1)}, bf16[33,16,128]{2,1,0:T(8,128)(2,1)S(1)}, u32[]{:S(2)}, u32[]{:S(2)}) collective-permute-start(bf16[33,16,128]{2,1,0:T(8,128)(2,1)S(1)} %get-tuple-element.38), channel_id=1, source_target_pairs={{0,28},{4,24},{8,20},{12,16},{16,12},{20,8},{24,4},{28,0},{1,29},{... | collective-permute-start | bytes 405512 | tf_op jit(solution)/shard_map/ppermute | solution.py:45
  41.7 33.5 %all-to-all-start = ((bf16[32,2,2,16,256]{4,3,2,1,0:T(8,128)(2,1)}), bf16[32,2,2,16,256]{4,3,2,1,0:T(8,128)(2,1)S(1)}, u32[]{:S(2)}, u32[]{:S(2)}) async-start(bf16[32,2,2,16,256]{4,3,2,1,0:T(8,128)(2,1)} %bitcast.4), calls=%async_computation | async-start | bytes 2097152 | tf_op jit(solution)/shard_map/all_to_all | solution.py:61
  46.6 26.2 %copy-start.1 = (bf16[4,512,512]{2,1,0:T(8,128)(2,1)S(1)}, bf16[4,512,512]{2,1,0:T(8,128)(2,1)}, u32[]{:S(2)}) copy-start(bf16[4,512,512]{2,1,0:T(8,128)(2,1)} %bank.3) | copy-start | bytes 6291460
  46.6 26.2 %copy-start.12 = (s32[2]{0:T(128)S(1)}, s32[2]{0:T(128)}, u32[]{:S(2)}) copy-start(s32[2]{0:T(128)} %copy-done.11) | copy-start | bytes 28
  46.6 26.2 %copy-start.13 = (s32[4,1]{0,1:T(1,128)S(1)}, s32[4,1]{0,1:T(1,128)}, u32[]{:S(2)}) copy-start(s32[4,1]{0,1:T(1,128)} %param.24) | copy-start | bytes 52
  52.3 9.8 %collective-permute-start.7 = (bf16[2,8,16,256]{3,2,1,0:T(8,128)(2,1)}, bf16[2,8,16,256]{3,2,1,0:T(8,128)(2,1)S(1)}, u32[]{:S(2)}, u32[]{:S(2)}) collective-permute-start(bf16[2,8,16,256]{3,2,1,0:T(8,128)(2,1)} %get-tuple-element.43), channel_id=1, source_target_pairs={{0,24},{4,28},{8,16},{12,20},{16,8},{20,12},{24,0},{28,4},{1,25},{... | collective-permute-start | bytes 393224 | tf_op jit(solution)/shard_map/ppermute | solution.py:45
  54.9 11.3 %collective-permute-start.9 = (bf16[2,8,16,256]{3,2,1,0:T(8,128)(2,1)}, bf16[2,8,16,256]{3,2,1,0:T(8,128)(2,1)S(1)}, u32[]{:S(2)}, u32[]{:S(2)}) collective-permute-start(bf16[2,8,16,256]{3,2,1,0:T(8,128)(2,1)} %get-tuple-element.45), channel_id=1, source_target_pairs={{0,8},{4,12},{8,0},{12,4},{16,24},{20,28},{24,16},{28,20},{1,9},{5... | collective-permute-start | bytes 393224 | tf_op jit(solution)/shard_map/ppermute | solution.py:45
  55.5 0.9 %copy-start.8 = (bf16[2,8,16,256]{3,2,1,0:T(8,128)(2,1)S(1)}, bf16[2,8,16,256]{3,2,1,0:T(8,128)(2,1)}, u32[]{:S(2)}) copy-start(bf16[2,8,16,256]{3,2,1,0:T(8,128)(2,1)} %get-tuple-element.40.source) | copy-start | bytes 393220
  56.4 12.3 %collective-permute-start.10 = (bf16[2,8,16,256]{3,2,1,0:T(8,128)(2,1)}, bf16[2,8,16,256]{3,2,1,0:T(8,128)(2,1)S(1)}, u32[]{:S(2)}, u32[]{:S(2)}) collective-permute-start(bf16[2,8,16,256]{3,2,1,0:T(8,128)(2,1)} %get-tuple-element.46), channel_id=1, source_target_pairs={{0,12},{4,8},{8,4},{12,0},{16,28},{20,24},{24,20},{28,16},{1,13},{... | collective-permute-start | bytes 393224 | tf_op jit(solution)/shard_map/ppermute | solution.py:45
  57.1 11.6 %collective-permute-start.11 = (bf16[2,8,16,256]{3,2,1,0:T(8,128)(2,1)}, bf16[2,8,16,256]{3,2,1,0:T(8,128)(2,1)S(1)}, u32[]{:S(2)}, u32[]{:S(2)}) collective-permute-start(bf16[2,8,16,256]{3,2,1,0:T(8,128)(2,1)} %get-tuple-element.47), channel_id=1, source_target_pairs={{0,16},{4,20},{8,24},{12,28},{16,0},{20,4},{24,8},{28,12},{1,17},{... | collective-permute-start | bytes 393224 | tf_op jit(solution)/shard_map/ppermute | solution.py:45
  57.7 11.1 %collective-permute-start.12 = (bf16[2,8,16,256]{3,2,1,0:T(8,128)(2,1)}, bf16[2,8,16,256]{3,2,1,0:T(8,128)(2,1)S(1)}, u32[]{:S(2)}, u32[]{:S(2)}) collective-permute-start(bf16[2,8,16,256]{3,2,1,0:T(8,128)(2,1)} %get-tuple-element.48), channel_id=1, source_target_pairs={{0,20},{4,16},{8,28},{12,24},{16,4},{20,0},{24,12},{28,8},{1,21},{... | collective-permute-start | bytes 393224 | tf_op jit(solution)/shard_map/ppermute | solution.py:45
  62.1 10.7 %collective-permute-start.13 = (bf16[2,8,16,256]{3,2,1,0:T(8,128)(2,1)}, bf16[2,8,16,256]{3,2,1,0:T(8,128)(2,1)S(1)}, u32[]{:S(2)}, u32[]{:S(2)}) collective-permute-start(bf16[2,8,16,256]{3,2,1,0:T(8,128)(2,1)} %get-tuple-element.50), channel_id=1, source_target_pairs={{0,28},{4,24},{8,20},{12,16},{16,12},{20,8},{24,4},{28,0},{1,29},{... | collective-permute-start | bytes 393224 | tf_op jit(solution)/shard_map/ppermute | solution.py:45
  66.2 6.6 %collective-permute-start.8 = (bf16[2,8,16,256]{3,2,1,0:T(8,128)(2,1)}, bf16[2,8,16,256]{3,2,1,0:T(8,128)(2,1)S(1)}, u32[]{:S(2)}, u32[]{:S(2)}) collective-permute-start(bf16[2,8,16,256]{3,2,1,0:T(8,128)(2,1)} %get-tuple-element.44), channel_id=1, source_target_pairs={{0,4},{4,0},{8,12},{12,8},{16,20},{20,16},{24,28},{28,24},{1,5},{5... | collective-permute-start | bytes 393224 | tf_op jit(solution)/shard_map/ppermute | solution.py:45
